TPU v7x, 256 devices: a whole 4x4x8 slice. The times are simulated.
256 devices in a mesh: cx: 32 (over y, x, core), tp: 8 (over z).
Axes of the slice: x: 4, y: 4, z: 8, core: 2. Of those that a mesh axis runs over, the one named last changes fastest.
Arguments:
- layer_input: bfloat16 [4096, 3072], P('cx', 'tp'), may hold values from -40 to 40
- queries: bfloat16 [4096, 4096], P('cx', 'tp'), may hold values from -6 to 6
- keys: bfloat16 [4096, 4096], P('cx', 'tp'), may hold values from -6 to 6
- values: bfloat16 [4096, 4096], P('cx', 'tp'), may hold values from -6 to 6
- gate_input: bfloat16 [4096, 4096], P('cx', 'tp'), may hold values from -6 to 6
- log_decay: float32 [32, 4096], P('tp', 'cx'), may hold values from -1 to 0
- prior_state: float32 [32, 128, 128], P('tp'), may hold values from -192 to 192
- attn_gain: float32 [4096], P('tp'), may hold values from 0.5 to 1.5
- out_weight: bfloat16 [4096, 3072], P('tp'), may hold values from -0.09375 to 0.09375
- moe_gain: float32 [3072], replicated, may hold values from 0.5 to 1.5
- router: bfloat16 [3072, 16], replicated, may hold values from -0.109375 to 0.109375
- expert_ids: int32 [4096, 2], P('cx'), may hold values from 0 to 15, all different within a row; in each aligned block of 128 rows (0 to 127, 128 to 255, ...) at most 32 rows name the same one
- w_gate: bfloat16 [32, 3072, 3072], P('cx', None, 'tp'), may hold values from -0.109375 to 0.109375
- w_up: bfloat16 [32, 3072, 3072], P('cx', None, 'tp'), may hold values from -0.109375 to 0.109375
- w_down: bfloat16 [32, 3072, 3072], P('cx', 'tp'), may hold values from -0.078125 to 0.078125
Outputs:
- mixed: bfloat16 [4096, 3072], P('cx', 'tp')
Inputs may be any that keep to these rules, and one draw needn't show every extreme that they name: `expert_ids`: each row names 2 different experts. Among the rows of one index of cx no expert is named by more than 32 rows, and in every draw some expert is named by exactly 32 of them.
All inputs are finite; a program needn't handle non-finite values.
Results may differ from a plain program's by a relative error of at most 0.0085.
Values may be sent and summed in bfloat16 or wider, within the bound.
No kernel may reach another device: no remote copies, remote signals or barrier semaphores. Data moves between devices by JAX's collectives and lax.ppermute only.
A program may use at most 128 MiB of HBM per device.

v0:
```python
import jax
import jax.numpy as jnp
from jax import lax
from jax.sharding import PartitionSpec as P

epsilon = 1e-06
highest_precision = lax.Precision.HIGHEST


def prefix(shard, axis, combine, identity):
    peers, index = (lax.axis_size(axis), lax.axis_index(axis))
    everything = jax.tree.map(lambda part: lax.all_gather(part, axis), shard)
    start = jax.tree.map(
        lambda part, zero: jnp.broadcast_to(jnp.asarray(zero, part.dtype), part.shape),
        shard,
        identity,
    )

    def lap(k, before):
        reached = k < index
        new = combine(before, jax.tree.map(lambda part: part[k], everything))
        return jax.tree.map(lambda a, b: jnp.where(reached, a, b), new, before)

    return lax.fori_loop(0, peers, lap, start)


def feed_forward(routed, gate_weight, up_weight, down_weight):
    gated = jnp.dot(routed, gate_weight, preferred_element_type=jnp.float32)
    lifted = jnp.dot(routed, up_weight, preferred_element_type=jnp.float32)
    activated = (jax.nn.silu(gated) * lifted).astype(jnp.bfloat16)
    return jnp.dot(activated, down_weight, preferred_element_type=jnp.float32)


def combine_states(earlier, later):
    return (earlier[0] + later[0], jnp.exp(later[0])[:, None, None] * earlier[1] + later[1])


def shards(
    layer_input,
    queries,
    keys,
    values,
    gate_input,
    log_decay,
    prior_state,
    attn_gain,
    out_weight,
    moe_gain,
    router,
    expert_ids,
    w_gate,
    w_up,
    w_down,
):
    positions = queries.shape[0]
    heads_here = log_decay.shape[0]
    head_size = prior_state.shape[1]
    query_vectors = queries.reshape(positions, heads_here, head_size)
    key_rows = keys.reshape(positions, heads_here, head_size)
    value_single_float = values.reshape(positions, heads_here, head_size).astype(jnp.float32)
    running_state = jnp.cumsum(log_decay, axis=1)
    causal = (jnp.arange(positions)[:, None] >= jnp.arange(positions)[None, :])[None]
    spread = running_state[:, :, None] - running_state[:, None, :]
    weights = jnp.where(causal, jnp.exp(jnp.where(causal, spread, 0.0)), 0.0)
    scores = (
        jnp.einsum("thk,shk->hts", query_vectors, key_rows, preferred_element_type=jnp.float32)
        * weights
    )
    inner = jnp.einsum("hts,shv->thv", scores, value_single_float, precision=highest_precision)
    trailing_rows = jnp.exp(running_state[:, -1:] - running_state)
    key_single_float = key_rows.astype(jnp.float32) * trailing_rows.T[:, :, None]
    within_block_state = jnp.einsum(
        "gpc,gpw->pcw", key_single_float, value_single_float, precision=highest_precision
    )
    total_decay = running_state[:, -1]
    identity = (
        jnp.zeros((heads_here,), jnp.float32),
        jnp.zeros((heads_here, head_size, head_size), jnp.float32),
    )
    before_total, before_state = prefix(
        (total_decay, within_block_state), "cx", combine_states, identity
    )
    incoming_state = jnp.exp(before_total)[:, None, None] * prior_state + before_state
    carried_contribution = jnp.exp(running_state).T[:, :, None] * jnp.einsum(
        "rxg,xgd->rxd",
        query_vectors.astype(jnp.float32),
        incoming_state,
        precision=highest_precision,
    )
    attended = inner + carried_contribution
    squares = jnp.mean(attended * attended, axis=-1, keepdims=True)
    gating = jax.nn.sigmoid(
        gate_input.astype(jnp.float32).reshape(positions, heads_here, head_size)
    )
    normed = (
        attended * lax.rsqrt(squares + epsilon) * attn_gain.reshape(heads_here, head_size) * gating
    )
    normed = normed.astype(jnp.bfloat16).reshape(positions, heads_here * head_size)
    partial_rows = jnp.dot(normed, out_weight, preferred_element_type=jnp.float32)
    model_width = out_weight.shape[1]
    width_share = layer_input.shape[1]
    column_start = lax.axis_index("tp") * width_share
    own_columns = lax.dynamic_slice_in_dim(
        partial_rows, column_start, width_share, 1
    ) + layer_input.astype(jnp.float32)
    partial_rows = lax.dynamic_update_slice_in_dim(partial_rows, own_columns, column_start, 1)
    expert_count = router.shape[1]
    hidden_state = lax.psum(partial_rows, "tp")
    row_mean = jnp.mean(hidden_state * hidden_state, axis=-1, keepdims=True)
    full_input = (hidden_state * lax.rsqrt(row_mean + epsilon) * moe_gain).astype(jnp.bfloat16)
    logits = jnp.dot(full_input, router, preferred_element_type=jnp.float32)
    hidden_share = lax.dynamic_slice_in_dim(hidden_state, column_start, width_share, 1)
    matched = expert_ids[:, :, None] == jnp.arange(expert_count, dtype=jnp.int32)[None, None, :]
    chosen = jnp.sum(jnp.where(matched, logits[:, None, :], 0.0), axis=-1)
    margin = chosen[:, 0] - chosen[:, 1]
    mixing = jnp.stack([jax.nn.sigmoid(margin), jax.nn.sigmoid(-margin)], axis=1)
    choices_made = expert_ids.shape[1]
    onehot = matched.reshape(positions * choices_made, expert_count).astype(jnp.int32)
    before = jnp.cumsum(onehot, axis=0) - onehot
    position = jnp.sum(before * onehot, axis=1).reshape(positions, choices_made)
    capacity = 8 * positions // lax.axis_size("cx")
    at_slot = position[:, :, None] == jnp.arange(capacity, dtype=jnp.int32)[None, None, :]
    picked = matched[:, :, :, None] & at_slot[:, :, None, :]
    dispatch = (
        jnp.sum(picked, axis=1).astype(jnp.bfloat16).reshape(positions, expert_count * capacity)
    )
    weighting = jnp.sum(jnp.where(picked, mixing[:, :, None, None], 0.0), axis=1).reshape(
        positions, expert_count * capacity
    )
    gate_weight = w_gate[0]
    up_weight = w_up[0]
    down_weight = w_down[0]
    outgoing = jnp.einsum(
        "tm,td->md", dispatch, full_input, preferred_element_type=jnp.float32
    ).astype(jnp.bfloat16)
    outgoing = jnp.repeat(outgoing.reshape(expert_count, capacity, model_width), 2, axis=0)
    received = lax.all_to_all(outgoing, "cx", split_axis=0, concat_axis=0, tiled=True)
    owners, slots, columns = received.shape
    produced = feed_forward(
        received.reshape(owners * slots, columns), gate_weight, up_weight, down_weight
    )
    returned = lax.all_to_all(
        produced.reshape(owners, slots, columns).astype(jnp.bfloat16),
        "cx",
        split_axis=0,
        concat_axis=0,
        tiled=True,
    ).astype(jnp.float32)
    halves = jnp.sum(returned.reshape(expert_count, 2, capacity, model_width), axis=1)
    moe_rows = jnp.dot(
        weighting,
        halves.reshape(expert_count * capacity, model_width),
        precision=highest_precision,
        preferred_element_type=jnp.float32,
    )
    moe_share = lax.psum_scatter(
        moe_rows.astype(jnp.bfloat16), "tp", scatter_dimension=1, tiled=True
    ).astype(jnp.float32)
    return (hidden_share + moe_share).astype(jnp.bfloat16)


def solution(mesh):
    placed = (
        P("cx", "tp"),
        P("cx", "tp"),
        P("cx", "tp"),
        P("cx", "tp"),
        P("cx", "tp"),
        P("tp", "cx"),
        P("tp", None, None),
        P("tp"),
        P("tp", None),
        P(),
        P(),
        P("cx", None),
        P("cx", None, "tp"),
        P("cx", None, "tp"),
        P("cx", "tp", None),
    )
    return jax.shard_map(
        shards, mesh=mesh, in_specs=placed, out_specs=P("cx", "tp"), check_vma=False
    )
```

profile of v0, /device:TPU:2, one launch (start us, length us, event | category | flops | bytes accessed | tf_op | source)
XLA Modules:
  0.0 476.9 jit_solution(17910165851488862531)
XLA Ops:
  9.9 1.9 fusion.15
  11.9 1.3 dynamic-slice
  14.1 63.5 %all-reduce = f32[128]{0:T(128)} all-reduce(f32[128]{0:T(128)S(1)} %dynamic-update-slice), channel_id=2, replica_groups=mesh['cx'=32,'tp'=8] {'cx'}, use_global_device_ids=true, to_apply=%add | all-reduce | flops 128 | bytes 1024
  78.3 1.7 add_divide_fusion
  80.0 1.8 copy.56
  84.1 70.2 %while.16 = (s32[]{:T(128)}, f32[4]{0:T(128)}, f32[4,128,128]{2,1,0:T(8,128)S(1)}, s32[]{:T(128)}, f32[32,4]{1,0:T(8,128)S(1)}, /*index=5*/f32[32,4,128,128]{3,2,1,0:T(8,128)}, s32[]{:T(128)}, s32[]{:T(128)}) while((s32[]{:T(128)}, f32[4]{0:T(128)}, f32[4,128,128]{2,1,0:T(8,128)S(1)}, s32[]{:T(128)}, f32[32,4]{1,0:T(8,128)S(1)}, ...), condition=%wide.region_2.3_spmd.clone, body=%wide.region_1.2_spmd.clone.sunk | while | flops 262160 | bytes 786627 | solution.py:24
  154.9 1.5 multiply_reduce_fusion.1
  157.6 1.8 fusion.33
  159.4 1.6 add_dynamic-update-slice_fusion
  162.7 79.9 %all-reduce.3.cloned.1.call-done = f32[128,3072]{1,0:T(8,128)} async-done(((f32[128,3072]{1,0:T(8,128)}), f32[128,3072]{1,0:T(8,128)}) %all-reduce.3.cloned.1.call-update) | async-done | bytes 1572880 | tf_op jit(solution)/shard_map/psum | solution.py:108
  242.6 1.7 multiply_reduce_fusion
  244.5 1.8 convolution_convert_fusion.1
  247.0 79.6 %all_to_all.10 = bf16[32,32,3072]{2,1,0:T(8,128)(2,1)S(1)} all-to-all(bf16[32,32,3072]{2,1,0:T(8,128)(2,1)S(1)} %bitcast.111), channel_id=1, replica_groups=mesh['cx'=32,'tp'=8] {'cx'}, dimensions={0} | all-to-all | bytes 12582912 | tf_op jit(solution)/shard_map/all_to_all | solution.py:137
  326.7 3.4 fusion.5
  330.1 3.5 multiply_convert_fusion
  333.7 5.4 %convolution_convert_fusion = bf16[32,32,3072]{2,1,0:T(8,128)(2,1)} fusion(bf16[32,32,384]{2,1,0:T(8,128)(2,1)S(1)} %bitcast.124, bf16[1,384,3072]{2,1,0:T(8,128)(2,1)S(1)} %copy-done.12), kind=kOutput, calls=%fused_computation.7 | convolution fusion | flops 2419064832 | bytes 9437184 | tf_op jit(solution)/shard_map/dot_general | solution.py:31
  339.1 6.3 %all-to-all-start.1 = ((bf16[32,32,3072]{2,1,0:T(8,128)(2,1)}), bf16[32,32,3072]{2,1,0:T(8,128)(2,1)}, u32[]{:S(2)}, u32[]{:S(2)}) async-start(bf16[32,32,3072]{2,1,0:T(8,128)(2,1)} %convolution_convert_fusion), calls=%async_computation.1 | async-start | bytes 12582912 | tf_op jit(solution)/shard_map/all_to_all | solution.py:142
  345.4 1.8 fusion.32
  347.3 73.3 %all-to-all-done.1 = bf16[32,32,3072]{2,1,0:T(8,128)(2,1)} async-done(((bf16[32,32,3072]{2,1,0:T(8,128)(2,1)}), bf16[32,32,3072]{2,1,0:T(8,128)(2,1)}, u32[]{:S(2)}, u32[]{:S(2)}) %all-to-all-start.1) | async-done | bytes 6291488 | tf_op jit(solution)/shard_map/all_to_all | solution.py:142
  420.6 5.2 %convert_reduce_fusion = f32[16,32,3072]{2,1,0:T(8,128)S(1)} fusion(bf16[32,32,3072]{2,1,0:T(8,128)(2,1)} %all-to-all-done.1), kind=kLoop, calls=%fused_computation.6 | loop fusion | flops 4718592 | bytes 12582912 | tf_op jit(solution)/shard_map/reduce_sum | solution.py:149
  425.8 4.3 fusion.1
  430.1 2.3 copy.62
  432.4 35.3 %reduce-scatter.4.cloned.1.call-done = bf16[384,128]{1,0:T(8,128)(2,1)} async-done(((bf16[3072,128]{1,0:T(8,128)(2,1)}), bf16[384,128]{1,0:T(8,128)(2,1)}) %reduce-scatter.4.cloned.1.call-update) | async-done | bytes 98320
  468.7 1.6 add_convert_fusion
  (134 shorter events, 81.5 us)
Async XLA Ops:
  6.5 151.0 %copy-start = (bf16[512,3072]{1,0:T(8,128)(2,1)S(1)}, bf16[512,3072]{1,0:T(8,128)(2,1)}, u32[]{:S(2)}) copy-start(bf16[512,3072]{1,0:T(8,128)(2,1)} %param.25) | copy-start | bytes 9437188
  6.5 76.5 %copy-start.2 = (bf16[128,512]{1,0:T(8,128)(2,1)S(1)}, bf16[128,512]{1,0:T(8,128)(2,1)}, u32[]{:S(2)}) copy-start(bf16[128,512]{1,0:T(8,128)(2,1)} %param.20) | copy-start | bytes 393220
  6.5 77.6 %all-gather.4.cloned.1.call-start = ((), (), s32[]{:S(2)}) async-start(), calls=%async_computation.4 | async-start | bytes 8650752 | tf_op jit(solution)/shard_map/all_gather | solution.py:12
  7.7 0.6 copy-start.8
  9.9 2.0 copy-start.3
  11.8 230.7 %all-reduce.3.cloned.1.call-start = ((), (), s32[]{:S(2)}) async-start(), calls=%async_computation.3 | async-start | bytes 3145728 | tf_op jit(solution)/shard_map/psum | solution.py:108
  84.1 70.8 %copy-start.4 = (bf16[128,512]{1,0:T(8,128)(2,1)S(1)}, bf16[128,512]{1,0:T(8,128)(2,1)}, u32[]{:S(2)}) copy-start(bf16[128,512]{1,0:T(8,128)(2,1)} %param.18) | copy-start | bytes 393220
  157.6 1.8 copy-start.6
  157.6 3.4 copy-start.9
  242.6 1.9 copy-start.1
  247.0 79.7 %copy-start.10 = (bf16[1,3072,384]{2,1,0:T(8,128)(2,1)S(1)}, bf16[1,3072,384]{2,1,0:T(8,128)(2,1)}, u32[]{:S(2)}) copy-start(bf16[1,3072,384]{2,1,0:T(8,128)(2,1)} %param.29) | copy-start | bytes 7077892
  326.7 3.4 copy-start.11
  330.1 3.5 copy-start.12
  339.1 6.3 %copy-start.5 = (bf16[3072,16]{0,1:T(8,128)(2,1)S(1)}, bf16[3072,16]{0,1:T(8,128)(2,1)}, u32[]{:S(2)}) copy-start(bf16[3072,16]{0,1:T(8,128)(2,1)} %param.27) | copy-start | bytes 294916
  339.1 6.3 %copy-start.7 = (f32[3072]{0:T(1024)S(1)}, f32[3072]{0:T(1024)}, u32[]{:S(2)}) copy-start(f32[3072]{0:T(1024)} %param.26) | copy-start | bytes 36868
  339.1 81.6 %all-to-all-start.1 = ((bf16[32,32,3072]{2,1,0:T(8,128)(2,1)}), bf16[32,32,3072]{2,1,0:T(8,128)(2,1)}, u32[]{:S(2)}, u32[]{:S(2)}) async-start(bf16[32,32,3072]{2,1,0:T(8,128)(2,1)} %convolution_convert_fusion), calls=%async_computation.1 | async-start | bytes 12582912 | tf_op jit(solution)/shard_map/all_to_all | solution.py:142
  345.3 122.4 %reduce-scatter.4.cloned.1.call-start = ((), (), s32[]{:S(2)}) async-start(), calls=%async_computation.5 | async-start | bytes 884736
Sparse Core Ops, SparseCore 0:
  12.0 60.9 all-gather.3
  161.1 81.3 all-reduce.2
  432.5 35.1 reduce-scatter.3
where the time goes:
time: 479 us; the launch traced here: 477 us
  waiting for transfers between devices  189 us (39%)
  blocking collectives  143 us (30%)
  other arithmetic  85 us (18%)
  matrix products  27.7 us (6%)
  between operations  14.1 us (3%)
  local copies, waits for them, and re-layouts  11.3 us (2%)
  starting transfers between devices  6.34 us (1%)
    psum x1, waiting for transfers between devices, shards(): hidden_state = lax.psum(partial_rows, 'tp')  79.9 us
    all_to_all x1, blocking collectives, shards(): lax.all_to_all(outgoing, 'cx', split_axis=0, concat_axis=0, tiled=True)  79.6 us
    all_to_all x1, waiting for transfers between devices, shards(): lax.all_to_all(produced.reshape(owners, slots, columns).astype(jnp.bfloat...  73.3 us
    unnamed x1, blocking collectives  63.5 us
    exp x32, other arithmetic, combine_states(): jnp.exp(later[0])[:, None, None] * earlier[1] + later[1]  35.8 us
    unnamed x4, waiting for transfers between devices  35.3 us
    select_n x32, other arithmetic, lap(): return jax.tree.map(lambda a, b: jnp.where(reached, a, b), new, before)  33.6 us
  transfers between devices with their start and end apart: 4, of which 3 were waited for; matrix products, arithmetic and copies ran while one was open for 2% of the time, Pallas kernels for 0%

commit v1 on v0

v1 whole, which is shorter than its diff:
```python
import functools

import jax
import jax.numpy as jnp
from jax import lax
from jax.experimental import pallas as pl
from jax.experimental.pallas import tpu as pltpu
from jax.sharding import Mesh, PartitionSpec as P

epsilon = 1e-06
exact = lax.Precision.HIGHEST
bf16 = jnp.bfloat16
f32 = jnp.float32
MIB = 1 << 20


def mm(a, b, contract_a=1, contract_b=0, precision=None):
    return lax.dot_general(
        a, b, (((contract_a,), (contract_b,)), ((), ())),
        precision=precision, preferred_element_type=f32,
    )


def lower_triangle(n, strict=False):
    rows = lax.broadcasted_iota(jnp.int32, (n, n), 0)
    cols = lax.broadcasted_iota(jnp.int32, (n, n), 1)
    return (rows > cols) if strict else (rows >= cols)


def block_state_kernel(keys, values, log_decay, out):
    heads, positions = log_decay.shape
    size = keys.shape[1] // heads
    per_head = out.shape[1]
    rows = size // per_head
    until = mm(lower_triangle(positions).astype(f32), log_decay[...], 1, 1, exact)
    for h in range(heads):
        lanes = slice(h * size, (h + 1) * size)
        total = until[positions - 1:positions, h:h + 1]
        trailing = jnp.exp(total - until[:, h:h + 1])
        weighted = (keys[:, lanes].astype(f32) * trailing).astype(bf16)
        state = mm(weighted, values[:, lanes], 0, 0)
        out[h, :, :rows, :] = state.astype(bf16).reshape(per_head, rows, size)
        high = total.astype(bf16).astype(f32)
        middle = (total - high).astype(bf16).astype(f32)
        low = total - high - middle
        row = lax.broadcasted_iota(jnp.int32, (rows, size), 0)
        terms = jnp.where(row == 0, high, jnp.where(row == 1, middle, jnp.where(row == 2, low, 0.0)))
        out[h, :, rows:, :] = jnp.broadcast_to(terms.astype(bf16), (per_head, rows, size))


def state_scan_kernel(part, received, prior, out):
    blocks, rows, _ = out.shape
    state = prior[pl.ds(pl.multiple_of(part[0] * rows, rows), rows), :]
    for k in range(blocks):
        out[k] = state.astype(bf16)
        terms = received[k, rows:, :].astype(f32)
        total = terms[0:1] + terms[1:2] + terms[2:3]
        state = jnp.exp(total) * state + received[k, :rows, :].astype(f32)


def inner_kernel(queries, keys, values, log_decay, out, growth):
    heads, positions = log_decay.shape
    size = queries.shape[1] // heads
    causal = lower_triangle(positions)
    until = mm(causal.astype(f32), log_decay[...], 1, 1, exact)
    until_row = mm(log_decay[...], causal.astype(f32), 1, 1, exact)
    for h in range(heads):
        lanes = slice(h * size, (h + 1) * size)
        spread = until[:, h:h + 1] - until_row[h:h + 1, :]
        weights = jnp.where(causal, jnp.exp(jnp.where(causal, spread, 0.0)), 0.0)
        scores = mm(queries[:, lanes], keys[:, lanes], 1, 1) * weights
        out[:, lanes] = mm(scores.astype(bf16), values[:, lanes])
        growth[:, lanes] = jnp.broadcast_to(jnp.exp(until[:, h:h + 1]), (positions, size))


def project_kernel(queries, inner, growth, state, gate_input, gain, weight, out, normed, *, heads):
    size = queries.shape[1] // heads

    @pl.when(pl.program_id(0) == 0)
    def _():
        for h in range(heads):
            lanes = slice(h * size, (h + 1) * size)
            carried = mm(queries[:, lanes], state[lanes, :])
            attended = inner[:, lanes] + growth[:, lanes] * carried
            squares = jnp.mean(attended * attended, axis=1, keepdims=True)
            gating = jax.nn.sigmoid(gate_input[:, lanes].astype(f32))
            rows = attended * lax.rsqrt(squares + epsilon) * gain[:, lanes] * gating
            normed[:, lanes] = rows.astype(bf16)

    product = mm(normed[...], weight[...])
    for c in range(out.shape[0]):
        width = out.shape[2]
        out[c] = product[:, c * width:(c + 1) * width].astype(bf16)


def slots_of(ids, experts, capacity):
    positions = ids.shape[0]
    expert = lax.broadcasted_iota(jnp.int32, (positions, experts), 1)
    first = (ids[:, 0:1] == expert).astype(f32)
    second = (ids[:, 1:2] == expert).astype(f32)
    earlier = mm(lower_triangle(positions, True).astype(bf16), (first + second).astype(bf16))
    places = []
    for choice in (first, second):
        position = jnp.sum(choice * earlier, axis=1, keepdims=True).astype(jnp.int32)
        number = jnp.sum(choice * expert.astype(f32), axis=1, keepdims=True).astype(jnp.int32)
        places.append(number * capacity + position)
    return first, second, places


def dispatch_kernel(index, partial, layer_input, gain, router, ids, outgoing, hidden, sums, *, experts, capacity):
    del index
    positions, width = layer_input.shape
    total = layer_input[...].astype(f32)
    for k in range(partial.shape[0]):
        total += partial[k].astype(f32)
    hidden[...] = total
    scaled = (total * gain[0]).astype(bf16)
    logits = mm(scaled, router[...])
    squares = jnp.sum(total * total, axis=1, keepdims=True)
    sums[...] = jnp.concatenate(
        [logits, jnp.broadcast_to(squares, (positions, sums.shape[1] - experts))], axis=1
    )
    _, _, places = slots_of(ids[...], experts, capacity)
    slot = lax.broadcasted_iota(jnp.int32, (positions, experts * capacity), 1)
    chosen = ((slot == places[0]) | (slot == places[1])).astype(bf16)
    outgoing[...] = mm(chosen, scaled, 0, 0).astype(bf16)


def expert_kernel(rows, inverse, gate_up_hbm_gate, gate_up_hbm_up, down_hbm, out, gate_up, down, sems, *, width):
    chunks, _, share = rows.shape

    @pl.when(pl.program_id(0) == 0)
    def _():
        copies = [
            pltpu.make_async_copy(gate_up_hbm_gate, gate_up.at[:, pl.ds(0, share)], sems.at[0]),
            pltpu.make_async_copy(gate_up_hbm_up, gate_up.at[:, pl.ds(share, share)], sems.at[1]),
            pltpu.make_async_copy(down_hbm, down, sems.at[2]),
        ]
        for copy in copies:
            copy.start()
        for copy in copies:
            copy.wait()

    squares = jnp.zeros((rows.shape[1], 1), f32)
    total = jnp.zeros((rows.shape[1], 2 * share), f32)
    for c in range(0, chunks, 2):
        pair = jnp.concatenate([rows[c], rows[c + 1]], axis=1)
        lanes = slice(c * share, (c + 2) * share)
        wide = pair.astype(f32) * inverse[:, lanes]
        squares += jnp.sum(wide * wide, axis=1, keepdims=True)
        total += mm(pair, gate_up[lanes, :])
    total *= lax.rsqrt(squares / width + epsilon)
    gated = total[:, :share]
    activated = (gated * jax.nn.sigmoid(gated) * total[:, share:]).astype(bf16)
    for c in range(0, chunks, 2):
        product = mm(activated, down[:, c * share:(c + 2) * share])
        out[c] = product[:, :share].astype(bf16)
        out[c + 1] = product[:, share:].astype(bf16)


def combine_kernel(returned, hidden, sums, ids, out, *, experts, capacity, width):
    positions = hidden.shape[0]
    first, second, places = slots_of(ids[...], experts, capacity)
    scale = lax.rsqrt(sums[:, experts:experts + 1] / width + epsilon)
    logits = sums[:, :experts] * scale
    margin = jnp.sum((first - second) * logits, axis=1, keepdims=True)
    slot = lax.broadcasted_iota(jnp.int32, (positions, experts * capacity), 1)
    total = hidden[...]
    for place, mixing in zip(places, (jax.nn.sigmoid(margin), jax.nn.sigmoid(-margin))):
        total += mixing * mm((slot == place).astype(bf16), returned[...])
    out[...] = total.astype(out.dtype)


def call(kernel, shapes, *args, limit=48, **kwargs):
    return pl.pallas_call(
        kernel,
        out_shape=shapes,
        compiler_params=pltpu.CompilerParams(vmem_limit_bytes=limit * MIB),
        **kwargs,
    )(*args)


def whole(shape):
    return pl.BlockSpec(shape, lambda *_: (0,) * len(shape))


def shards(
    layer_input, queries, keys, values, gate_input, log_decay, prior_state, attn_gain,
    out_weight, moe_gain, router, expert_ids, w_gate, w_up, w_down,
):
    struct = jax.ShapeDtypeStruct
    positions, head_lanes = queries.shape
    heads, size, _ = prior_state.shape
    chips, cores, peers = lax.axis_size("chip"), lax.axis_size("core"), lax.axis_size("tp")
    blocks = chips * cores
    width = out_weight.shape[1]
    share = layer_input.shape[1]
    experts = router.shape[1]
    capacity = 8 * positions // blocks
    slots = experts * capacity
    core = lax.axis_index("core")
    cx = lax.axis_index("chip") * cores + core
    tp = lax.axis_index("tp")

    rows = heads * size // blocks
    parts = call(block_state_kernel, struct((heads, size // rows, 2 * rows, size), bf16), keys, values, log_decay)
    received = lax.all_to_all(parts.reshape(blocks, 2 * rows, size), ("chip", "core"), 0, 0, tiled=True)
    inner, growth = call(
        inner_kernel,
        (struct((positions, head_lanes), f32), struct((positions, head_lanes), f32)),
        queries, keys, values, log_decay,
    )
    befores = call(
        state_scan_kernel, struct((blocks, rows, size), bf16),
        cx.reshape(1), received, prior_state.reshape(heads * size, size),
        in_specs=[pl.BlockSpec(memory_space=pltpu.SMEM)] + [pl.BlockSpec(memory_space=pltpu.VMEM)] * 2,
    )
    state = lax.all_to_all(befores, ("chip", "core"), 0, 0, tiled=True).reshape(heads * size, size)

    steps = 4
    each = peers // steps
    partial = call(
        functools.partial(project_kernel, heads=heads),
        struct((peers, positions, share), bf16),
        queries, inner, growth, state, gate_input, attn_gain.reshape(1, head_lanes), out_weight,
        grid=(steps,),
        in_specs=[whole((positions, head_lanes))] * 3
        + [whole((heads * size, size)), whole((positions, head_lanes)), whole((1, head_lanes))]
        + [pl.BlockSpec((head_lanes, each * share), lambda i: (0, i))],
        out_specs=pl.BlockSpec((each, positions, share), lambda i: (i, 0, 0)),
        scratch_shapes=[pltpu.VMEM((positions, head_lanes), bf16)],
    )
    partial = lax.all_to_all(partial, "tp", 0, 0, tiled=True)
    outgoing, hidden, sums = pl.pallas_call(
        functools.partial(dispatch_kernel, experts=experts, capacity=capacity),
        out_shape=(struct((slots, share), bf16), struct((positions, share), f32), struct((positions, 128), f32)),
        grid_spec=pltpu.PrefetchScalarGridSpec(
            num_scalar_prefetch=1,
            grid=(1,),
            in_specs=[
                whole((peers, positions, share)),
                whole((positions, share)),
                pl.BlockSpec((1, 1, share), lambda i, index: (index[0], 0, 0)),
                pl.BlockSpec((share, experts), lambda i, index: (index[0], 0)),
                whole((positions, 2)),
            ],
            out_specs=[whole((slots, share)), whole((positions, share)), whole((positions, 128))],
        ),
        compiler_params=pltpu.CompilerParams(vmem_limit_bytes=48 * MIB),
    )(tp.reshape(1), partial, layer_input, moe_gain.reshape(peers, 1, share), router, expert_ids)

    arrived = lax.all_to_all(outgoing.reshape(chips, capacity, share), "chip", 0, 0, tiled=True)
    gathered = lax.all_gather(arrived.reshape(chips * capacity, share), ("core", "tp"))
    sums = lax.psum(sums, "tp")
    held = chips * capacity
    rows_step = 256
    per_half = held // rows_step
    produced = call(
        functools.partial(expert_kernel, width=width),
        struct((cores * peers, held, share), bf16),
        gathered.reshape(cores * peers, held, share), (1.0 / moe_gain).reshape(1, width),
        w_gate[0], w_up[0], w_down[0],
        grid=(cores * per_half,),
        in_specs=[
            pl.BlockSpec((peers, rows_step, share), lambda i: (i // per_half, i % per_half, 0)),
            whole((1, width)),
        ] + [pl.BlockSpec(memory_space=pl.ANY)] * 3,
        out_specs=pl.BlockSpec((peers, rows_step, share), lambda i: (i // per_half, i % per_half, 0)),
        scratch_shapes=[
            pltpu.VMEM((width, 2 * share), bf16),
            pltpu.VMEM((share, width), bf16),
            pltpu.SemaphoreType.DMA((3,)),
        ],
    ).reshape(cores, peers, held, share)

    other = lax.dynamic_index_in_dim(produced, 1 - core, 0, False)
    own = lax.dynamic_index_in_dim(produced, core, 0, False)
    other = lax.ppermute(other, "core", [(0, 1), (1, 0)])
    both = (own.astype(f32) + other.astype(f32)).astype(bf16)
    summed = lax.psum_scatter(both.reshape(peers * held, share), "tp", scatter_dimension=0, tiled=True)
    returned = lax.all_to_all(summed.reshape(chips, capacity, share), "chip", 0, 0, tiled=True)
    return call(
        functools.partial(combine_kernel, experts=experts, capacity=capacity, width=width),
        struct((positions, share), bf16),
        returned.reshape(slots, share), hidden, sums, expert_ids,
    )


def solution(mesh):
    cx, tp = mesh.devices.shape
    fine = Mesh(mesh.devices.reshape(cx // 2, 2, tp), ("chip", "core", "tp"))
    both = ("chip", "core")
    placed = (
        P(both, "tp"), P(both, "tp"), P(both, "tp"), P(both, "tp"), P(both, "tp"),
        P("tp", both), P("tp", None, None), P("tp"), P("tp", None), P(), P(),
        P(both, None), P(both, None, "tp"), P(both, None, "tp"), P(both, "tp", None),
    )
    return jax.shard_map(shards, mesh=fine, in_specs=placed, out_specs=P(both, "tp"), check_vma=False)
```

time: 479 us -> 303 us (0.63)
  blocking collectives: 143 us -> 13.7 us
  other arithmetic: 85 us -> 5.34 us
  matrix products: 27.7 us -> 0 us
  Pallas kernels: 0 us -> 25.7 us
  starting transfers between devices: 6.34 us -> 28.9 us
  waiting for transfers between devices: 189 us -> 197 us
  local copies, waits for them, and re-layouts: 11.3 us -> 18.1 us
    all_to_all x1, blocking collectives: 79.6 us -> 13.7 us  [shards(): lax.all_to_all(outgoing.reshape(chips, capacity, share), 'chip', 0, 0, ti...]
    unnamed x1 -> x0, blocking collectives: 63.5 us -> none
    reduce_scatter x0 -> x1, waiting for transfers between devices: none -> 45.6 us  [shards(): lax.psum_scatter(both.reshape(peers * held, share), 'tp', scatter_dimensi...]
    all_to_all x1 -> x4, waiting for transfers between devices: 73.3 us -> 32.9 us  [the longest x1 22.9 us: shards(): partial = lax.all_to_all(partial, 'tp', 0, 0, tiled=True)]
    all_gather x1, waiting for transfers between devices: 0.01 us -> 39.4 us  [shards(): lax.all_gather(arrived.reshape(chips * capacity, share), ('core', 'tp'))]
    exp x33 -> x0, other arithmetic: 36.4 us -> none  [the longest x32 35.8 us: combine_states(): jnp.exp(later[0])[:, None, None] * earlier[1] + later[1]]
    unnamed x4 -> x3, waiting for transfers between devices: 35.3 us -> 0.71 us
    select_n x32 -> x0, other arithmetic: 33.6 us -> none  [lap(): return jax.tree.map(lambda a, b: jnp.where(reached, a, b), new, before)]
  transfers between devices with their start and end apart: 4 -> 8, of which waited for: 3 -> 7; matrix products, arithmetic and copies ran while one was open for 2% -> 0% of each run, Pallas kernels for 0% -> 0%
where the time goes in v1:
time: 303 us; the launch traced here: 302 us
  waiting for transfers between devices  197 us (65%)
  starting transfers between devices  28.9 us (10%)
  Pallas kernels  25.7 us (8%)
  local copies, waits for them, and re-layouts  18.1 us (6%)
  blocking collectives  13.7 us (5%)
  between operations  13.2 us (4%)
  other arithmetic  5.34 us (2%)
    psum x1, waiting for transfers between devices, shards(): sums = lax.psum(sums, 'tp')  72.9 us
    reduce_scatter x1, waiting for transfers between devices, shards(): lax.psum_scatter(both.reshape(peers * held, share), 'tp', scatter_dimensi...  45.6 us
    all_gather x1, waiting for transfers between devices, shards(): lax.all_gather(arrived.reshape(chips * capacity, share), ('core', 'tp'))  39.4 us
    pallas_call x6, Pallas kernels, call(): pl.pallas_call(kernel, out_shape=shapes, compiler_params=pltpu.CompilerPa...  24.6 us
    all_to_all x1, waiting for transfers between devices, shards(): partial = lax.all_to_all(partial, 'tp', 0, 0, tiled=True)  22.9 us
    unnamed x40, local copies, waits for them, and re-layouts  15.9 us
    all_to_all x1, blocking collectives, shards(): lax.all_to_all(outgoing.reshape(chips, capacity, share), 'chip', 0, 0, ti...  13.7 us
    all_to_all x1, starting transfers between devices, shards(): partial = lax.all_to_all(partial, 'tp', 0, 0, tiled=True)  8.46 us
  transfers between devices with their start and end apart: 8, of which 7 were waited for; matrix products, arithmetic and copies ran while one was open for 0% of the time, Pallas kernels for 0%

profile of v1, /device:TPU:2, one launch (start us, length us, event | category | flops | bytes accessed | tf_op | source)
XLA Modules:
  0.0 302.2 jit_solution(5700919953792467948)
XLA Ops:
  9.0 1.2 shard_map.146
  10.3 7.6 %all-to-all-start = ((bf16[32,32,128]{2,1,0:T(8,128)(2,1)}), bf16[32,32,128]{2,1,0:T(8,128)(2,1)S(1)}, u32[]{:S(2)}, u32[]{:S(2)}) async-start(bf16[32,32,128]{2,1,0:T(8,128)(2,1)} %bitcast.2), calls=%async_computation | async-start | bytes 524288 | tf_op jit(solution)/shard_map/all_to_all | solution.py:207
  17.9 7.7 %all-to-all-done.received = bf16[32,32,128]{2,1,0:T(8,128)(2,1)S(1)} async-done(((bf16[32,32,128]{2,1,0:T(8,128)(2,1)}), bf16[32,32,128]{2,1,0:T(8,128)(2,1)S(1)}, u32[]{:S(2)}, u32[]{:S(2)}) %all-to-all-start) | async-done | bytes 262176 | tf_op jit(solution)/shard_map/all_to_all | solution.py:207
  25.6 0.9 copy-done.9
  27.3 5.0 %all-to-all-start.1 = ((bf16[32,16,128]{2,1,0:T(8,128)(2,1)}), bf16[32,16,128]{2,1,0:T(8,128)(2,1)S(1)}, u32[]{:S(2)}, u32[]{:S(2)}) async-start(bf16[32,16,128]{2,1,0:T(8,128)(2,1)} %shard_map.147), calls=%async_computation.1 | async-start | bytes 262144 | tf_op jit(solution)/shard_map/all_to_all | solution.py:218
  35.6 0.9 shard_map.145
  36.6 2.4 all-to-all-done.1
  39.0 1.9 copy-done
  43.4 2.7 shard_map.148
  46.1 8.5 %all-to-all-start.2 = ((bf16[8,128,384]{2,1,0:T(8,128)(2,1)}), bf16[8,128,384]{2,1,0:T(8,128)(2,1)S(1)}, u32[]{:S(2)}, u32[]{:S(2)}) async-start(bf16[8,128,384]{2,1,0:T(8,128)(2,1)} %shard_map.148), calls=%async_computation.2 | async-start | bytes 1572864 | tf_op jit(solution)/shard_map/all_to_all | solution.py:233
  55.1 22.9 %all-to-all-done.2.partial = bf16[8,128,384]{2,1,0:T(8,128)(2,1)S(1)} async-done(((bf16[8,128,384]{2,1,0:T(8,128)(2,1)}), bf16[8,128,384]{2,1,0:T(8,128)(2,1)S(1)}, u32[]{:S(2)}, u32[]{:S(2)}) %all-to-all-start.2) | async-done | bytes 786464 | tf_op jit(solution)/shard_map/all_to_all | solution.py:233
  78.0 1.2 shard_map.149
  79.1 13.7 %all_to_all.25 = bf16[16,32,384]{2,1,0:T(8,128)(2,1)} all-to-all(bf16[16,32,384]{2,1,0:T(8,128)(2,1)S(1)} %bitcast.26), channel_id=1, replica_groups=mesh['chip'=16,'core'=2,'tp'=8] {'chip'}, dimensions={0} | all-to-all | bytes 786432 | tf_op jit(solution)/shard_map/all_to_all | solution.py:252
  93.0 39.4 %all-gather.2.cloned.1.call-done.rows = bf16[16,512,384]{2,1,0:T(8,128)(2,1)} async-done(((bf16[1,512,384]{2,1,0:T(8,128)(2,1)}), bf16[16,512,384]{2,1,0:T(8,128)(2,1)}) %all-gather.2.cloned.1.call-update) | async-done | bytes 6291472 | tf_op jit(solution)/shard_map/all_gather | solution.py:253
  132.4 1.7 copy-done.1
  134.1 1.7 copy-done.2
  135.7 17.7 %shard_map.150 = bf16[16,512,384]{2,1,0:T(8,128)(2,1)} custom-call(bf16[16,512,384]{2,1,0:T(8,128)(2,1)} %all-gather.2.cloned.1.call-done.rows, f32[1,3072]{1,0:T(1,128)S(1)} %bitcast.29, bf16[3072,384]{1,0:T(8,128)(2,1)S(1)} %bitcast.22, bf16[3072,384]{1,0:T(8,128)(2,1)S(1)} %bitcast.23, bf16[384,3072]{1,0:T(8,128)(2,1)} %bitcast.34), custom_call_target="tpu_custom_call" | custom-call | tf_op jit(solution)/shard_map/pallas_call | solution.py:175
  153.5 2.3 dynamic-slice_bitcast_fusion
  156.1 5.5 %collective-permute-done = bf16[8,512,384]{2,1,0:T(8,128)(2,1)} collective-permute-done((bf16[8,512,384]{2,1,0:T(8,128)(2,1)S(1)}, bf16[8,512,384]{2,1,0:T(8,128)(2,1)}, u32[]{:S(2)}, u32[]{:S(2)}) %collective-permute-start) | collective-permute-done | bytes 3145760 | tf_op jit(solution)/shard_map/ppermute | solution.py:278
  161.6 5.3 %fusion = bf16[8,512,384]{2,1,0:T(8,128)(2,1)} fusion(bf16[8,512,384]{2,1,0:T(8,128)(2,1)} %collective-permute-done, bf16[2,8,512,384]{3,2,1,0:T(8,128)(2,1)} %bitcast.32, s32[]{:T(128)S(6)} %select_n.7), kind=kLoop, calls=%fused_computation.1 | loop fusion | flops 6291456 | bytes 9437188 | tf_op jit(solution)/shard_map/convert_element_type | solution.py:279
  167.0 45.6 %reduce-scatter.2.cloned.1.call-done = bf16[512,384]{1,0:T(8,128)(2,1)} async-done(((bf16[4096,384]{1,0:T(8,128)(2,1)}), bf16[512,384]{1,0:T(8,128)(2,1)}) %reduce-scatter.2.cloned.1.call-update) | async-done | bytes 393232 | tf_op jit(solution)/shard_map/reduce_scatter | solution.py:280
  212.6 7.4 %all-to-all-start.4 = ((bf16[16,32,384]{2,1,0:T(8,128)(2,1)}), bf16[16,32,384]{2,1,0:T(8,128)(2,1)S(1)}, u32[]{:S(2)}, u32[]{:S(2)}) async-start(bf16[16,32,384]{2,1,0:T(8,128)(2,1)} %bitcast.36), calls=%async_computation.5 | async-start | bytes 786432 | tf_op jit(solution)/shard_map/all_to_all | solution.py:281
  220.7 72.9 %all-reduce.2.cloned.1.call-done.sums = f32[128,128]{1,0:T(8,128)} async-done(((f32[128,128]{1,0:T(8,128)}), f32[128,128]{1,0:T(8,128)}) %all-reduce.2.cloned.1.call-update) | async-done | bytes 65552 | tf_op jit(solution)/shard_map/psum | solution.py:254
  294.4 1.2 shard_map.151
  (46 shorter events, 11.6 us)
Async XLA Ops:
  6.5 0.9 copy-start.5
  7.4 0.9 copy-start.7
  10.3 15.3 %all-to-all-start = ((bf16[32,32,128]{2,1,0:T(8,128)(2,1)}), bf16[32,32,128]{2,1,0:T(8,128)(2,1)S(1)}, u32[]{:S(2)}, u32[]{:S(2)}) async-start(bf16[32,32,128]{2,1,0:T(8,128)(2,1)} %bitcast.2), calls=%async_computation | async-start | bytes 524288 | tf_op jit(solution)/shard_map/all_to_all | solution.py:207
  25.6 1.0 copy-start.9
  27.3 11.7 %all-to-all-start.1 = ((bf16[32,16,128]{2,1,0:T(8,128)(2,1)}), bf16[32,16,128]{2,1,0:T(8,128)(2,1)S(1)}, u32[]{:S(2)}, u32[]{:S(2)}) async-start(bf16[32,16,128]{2,1,0:T(8,128)(2,1)} %shard_map.147), calls=%async_computation.1 | async-start | bytes 262144 | tf_op jit(solution)/shard_map/all_to_all | solution.py:218
  32.2 0.9 copy-start.3
  33.2 0.9 copy-start.6
  34.1 0.9 copy-start.8
  39.0 1.9 copy-start
  40.9 0.9 copy-start.4
  41.8 0.9 copy-start.10
  43.3 11.2 %copy-start.17 = (bf16[3072,16]{0,1:T(8,128)(2,1)S(1)}, bf16[3072,16]{0,1:T(8,128)(2,1)}, u32[]{:S(2)}) copy-start(bf16[3072,16]{0,1:T(8,128)(2,1)} %param.25) | copy-start | bytes 294916
  43.3 11.6 %copy-start.18 = (s32[128,2]{0,1:T(2,128)S(1)}, s32[128,2]{0,1:T(2,128)}, u32[]{:S(2)}) copy-start(s32[128,2]{0,1:T(2,128)} %param.26) | copy-start | bytes 3076
  43.4 34.6 %copy-start.11 = (bf16[128,384]{1,0:T(8,128)(2,1)S(1)}, bf16[128,384]{1,0:T(8,128)(2,1)}, u32[]{:S(2)}) copy-start(bf16[128,384]{1,0:T(8,128)(2,1)} %layer_input.1) | copy-start | bytes 294916
  43.4 34.6 %copy-start.13 = (f32[3072]{0:T(1024)S(1)}, f32[3072]{0:T(1024)}, u32[]{:S(2)}) copy-start(f32[3072]{0:T(1024)} %param.24) | copy-start | bytes 36868
  46.1 31.9 %all-to-all-start.2 = ((bf16[8,128,384]{2,1,0:T(8,128)(2,1)}), bf16[8,128,384]{2,1,0:T(8,128)(2,1)S(1)}, u32[]{:S(2)}, u32[]{:S(2)}) async-start(bf16[8,128,384]{2,1,0:T(8,128)(2,1)} %shard_map.148), calls=%async_computation.2 | async-start | bytes 1572864 | tf_op jit(solution)/shard_map/all_to_all | solution.py:233
  54.5 77.9 %all-gather.2.cloned.1.call-start = ((), (), s32[]{:S(2)}) async-start(), calls=%async_computation.6 | async-start | bytes 6684672 | tf_op jit(solution)/shard_map/all_gather | solution.py:253
  92.9 119.7 %reduce-scatter.2.cloned.1.call-start = ((), (), s32[]{:S(2)}) async-start(), calls=%async_computation.7 | async-start | bytes 3538944 | tf_op jit(solution)/shard_map/reduce_scatter | solution.py:280
  132.4 1.7 copy-start.1
  134.1 1.7 copy-start.2
  155.7 5.9 %collective-permute-start = (bf16[8,512,384]{2,1,0:T(8,128)(2,1)S(1)}, bf16[8,512,384]{2,1,0:T(8,128)(2,1)}, u32[]{:S(2)}, u32[]{:S(2)}) collective-permute-start(bf16[8,512,384]{2,1,0:T(8,128)(2,1)S(1)} %dynamic-slice_bitcast_fusion), channel_id=1, source_target_pairs={{0,8},{8,0},{1,9},{9,1},{2,10},{10,2},{3,11},{11,3},{4,12},{12,4},... | collective-permute-start | bytes 9437192 | tf_op jit(solution)/shard_map/ppermute | solution.py:278
  212.6 81.0 %all-to-all-start.4 = ((bf16[16,32,384]{2,1,0:T(8,128)(2,1)}), bf16[16,32,384]{2,1,0:T(8,128)(2,1)S(1)}, u32[]{:S(2)}, u32[]{:S(2)}) async-start(bf16[16,32,384]{2,1,0:T(8,128)(2,1)} %bitcast.36), calls=%async_computation.5 | async-start | bytes 786432 | tf_op jit(solution)/shard_map/all_to_all | solution.py:281
  219.9 73.6 %all-reduce.2.cloned.1.call-start = ((), (), s32[]{:S(2)}) async-start(), calls=%async_computation.8 | async-start | bytes 131072 | tf_op jit(solution)/shard_map/psum | solution.py:254
  293.5 0.8 copy-start.12
  (3 other events, 2.0 us)
Sparse Core Ops, SparseCore 0:
  93.0 39.3 all-gather.1
  167.1 45.4 reduce-scatter.1
  223.1 70.4 all-reduce.1

commit v2 on v1

--- a/solution.py
+++ b/solution.py
@@ -11,7 +11,7 @@
 exact = lax.Precision.HIGHEST
 bf16 = jnp.bfloat16
 f32 = jnp.float32
-MIB = 1 << 20
+LIMIT = 60 << 20
 
 
 def mm(a, b, contract_a=1, contract_b=0, precision=None):
@@ -126,20 +126,22 @@
     outgoing[...] = mm(chosen, scaled, 0, 0).astype(bf16)
 
 
-def expert_kernel(rows, inverse, gate_up_hbm_gate, gate_up_hbm_up, down_hbm, out, gate_up, down, sems, *, width):
+def expert_kernel(core, rows, inverse, gate_hbm, up_hbm, down_hbm, other, own, gate_up, down, sems, *, width, per_half):
+    del core
     chunks, _, share = rows.shape
-
-    @pl.when(pl.program_id(0) == 0)
+    step = pl.program_id(0)
+    copies = [
+        pltpu.make_async_copy(gate_hbm, gate_up.at[:, pl.ds(0, share)], sems.at[0]),
+        pltpu.make_async_copy(up_hbm, gate_up.at[:, pl.ds(share, share)], sems.at[1]),
+        pltpu.make_async_copy(down_hbm, down, sems.at[2]),
+    ]
+
+    @pl.when(step == 0)
     def _():
-        copies = [
-            pltpu.make_async_copy(gate_up_hbm_gate, gate_up.at[:, pl.ds(0, share)], sems.at[0]),
-            pltpu.make_async_copy(gate_up_hbm_up, gate_up.at[:, pl.ds(share, share)], sems.at[1]),
-            pltpu.make_async_copy(down_hbm, down, sems.at[2]),
-        ]
         for copy in copies:
             copy.start()
-        for copy in copies:
-            copy.wait()
+        copies[0].wait()
+        copies[1].wait()
 
     squares = jnp.zeros((rows.shape[1], 1), f32)
     total = jnp.zeros((rows.shape[1], 2 * share), f32)
@@ -152,10 +154,23 @@
     total *= lax.rsqrt(squares / width + epsilon)
     gated = total[:, :share]
     activated = (gated * jax.nn.sigmoid(gated) * total[:, share:]).astype(bf16)
-    for c in range(0, chunks, 2):
-        product = mm(activated, down[:, c * share:(c + 2) * share])
-        out[c] = product[:, :share].astype(bf16)
-        out[c + 1] = product[:, share:].astype(bf16)
+
+    @pl.when(step == 0)
+    def _():
+        copies[2].wait()
+
+    def produce(out):
+        for c in range(0, chunks, 2):
+            product = mm(activated, down[:, c * share:(c + 2) * share])
+            out[c] = product[:, :share].astype(bf16)
+            out[c + 1] = product[:, share:].astype(bf16)
+
+    pl.when(step < per_half)(lambda: produce(other))
+    pl.when(step >= per_half)(lambda: produce(own))
+
+
+def add_kernel(a, b, out):
+    out[...] = (a[...].astype(f32) + b[...].astype(f32)).astype(bf16)
 
 
 def combine_kernel(returned, hidden, sums, ids, out, *, experts, capacity, width):
@@ -171,11 +186,11 @@
     out[...] = total.astype(out.dtype)
 
 
-def call(kernel, shapes, *args, limit=48, **kwargs):
+def call(kernel, shapes, *args, **kwargs):
     return pl.pallas_call(
         kernel,
         out_shape=shapes,
-        compiler_params=pltpu.CompilerParams(vmem_limit_bytes=limit * MIB),
+        compiler_params=pltpu.CompilerParams(vmem_limit_bytes=LIMIT),
         **kwargs,
     )(*args)
 
@@ -246,37 +261,49 @@
             ],
             out_specs=[whole((slots, share)), whole((positions, share)), whole((positions, 128))],
         ),
-        compiler_params=pltpu.CompilerParams(vmem_limit_bytes=48 * MIB),
+        compiler_params=pltpu.CompilerParams(vmem_limit_bytes=LIMIT),
     )(tp.reshape(1), partial, layer_input, moe_gain.reshape(peers, 1, share), router, expert_ids)
 
     arrived = lax.all_to_all(outgoing.reshape(chips, capacity, share), "chip", 0, 0, tiled=True)
     gathered = lax.all_gather(arrived.reshape(chips * capacity, share), ("core", "tp"))
-    sums = lax.psum(sums, "tp")
+    for distance in (1, 2, 4):
+        sums += lax.ppermute(sums, "tp", [(i, i ^ distance) for i in range(peers)])
     held = chips * capacity
     rows_step = 256
     per_half = held // rows_step
-    produced = call(
-        functools.partial(expert_kernel, width=width),
-        struct((cores * peers, held, share), bf16),
-        gathered.reshape(cores * peers, held, share), (1.0 / moe_gain).reshape(1, width),
+    block = (peers, rows_step, share)
+    other, own = pl.pallas_call(
+        functools.partial(expert_kernel, width=width, per_half=per_half),
+        out_shape=(struct((peers, held, share), bf16),) * 2,
+        grid_spec=pltpu.PrefetchScalarGridSpec(
+            num_scalar_prefetch=1,
+            grid=(cores * per_half,),
+            in_specs=[
+                pl.BlockSpec(block, lambda i, core: (jnp.where(i < per_half, 1 - core[0], core[0]), i % per_half, 0)),
+                whole((1, width)),
+            ] + [pl.BlockSpec(memory_space=pl.ANY)] * 3,
+            out_specs=[
+                pl.BlockSpec(block, lambda i, core: (0, jnp.minimum(i, per_half - 1), 0)),
+                pl.BlockSpec(block, lambda i, core: (0, jnp.maximum(i - per_half, 0), 0)),
+            ],
+            scratch_shapes=[
+                pltpu.VMEM((width, 2 * share), bf16),
+                pltpu.VMEM((share, width), bf16),
+                pltpu.SemaphoreType.DMA((3,)),
+            ],
+        ),
+        compiler_params=pltpu.CompilerParams(vmem_limit_bytes=LIMIT),
+    )(
+        core.reshape(1), gathered.reshape(cores * peers, held, share), (1.0 / moe_gain).reshape(1, width),
         w_gate[0], w_up[0], w_down[0],
-        grid=(cores * per_half,),
-        in_specs=[
-            pl.BlockSpec((peers, rows_step, share), lambda i: (i // per_half, i % per_half, 0)),
-            whole((1, width)),
-        ] + [pl.BlockSpec(memory_space=pl.ANY)] * 3,
-        out_specs=pl.BlockSpec((peers, rows_step, share), lambda i: (i // per_half, i % per_half, 0)),
-        scratch_shapes=[
-            pltpu.VMEM((width, 2 * share), bf16),
-            pltpu.VMEM((share, width), bf16),
-            pltpu.SemaphoreType.DMA((3,)),
-        ],
-    ).reshape(cores, peers, held, share)
-
-    other = lax.dynamic_index_in_dim(produced, 1 - core, 0, False)
-    own = lax.dynamic_index_in_dim(produced, core, 0, False)
+    )
+
     other = lax.ppermute(other, "core", [(0, 1), (1, 0)])
-    both = (own.astype(f32) + other.astype(f32)).astype(bf16)
+    part = pl.BlockSpec((1, held, share), lambda i: (i, 0, 0))
+    both = call(
+        add_kernel, struct((peers, held, share), bf16), own, other,
+        grid=(peers,), in_specs=[part, part], out_specs=part,
+    )
     summed = lax.psum_scatter(both.reshape(peers * held, share), "tp", scatter_dimension=0, tiled=True)
     returned = lax.all_to_all(summed.reshape(chips, capacity, share), "chip", 0, 0, tiled=True)
     return call(

time: 303 us -> 249 us (0.82)
  waiting for transfers between devices: 197 us -> 140 us
  Pallas kernels: 25.7 us -> 39.2 us
  local copies, waits for them, and re-layouts: 18.1 us -> 6.6 us
  starting transfers between devices: 28.9 us -> 33 us
  other arithmetic: 5.34 us -> 1.25 us
    psum x1 -> x0, waiting for transfers between devices: 72.9 us -> none  [shards(): sums = lax.psum(sums, 'tp')]
    ppermute x0 -> x3, waiting for transfers between devices: none -> 16.4 us  [shards(): sums += lax.ppermute(sums, 'tp', [(i, i ^ distance) for i in range(peers)])]
    pallas_call x0 -> x1, Pallas kernels: none -> 15.7 us  [shards(): pl.pallas_call(functools.partial(expert_kernel, width=width, per_half=per...]
    unnamed x40 -> x20, local copies, waits for them, and re-layouts: 15.9 us -> 6.6 us
    convert_element_type x1 -> x0, other arithmetic: 5.33 us -> none  [shards(): both = (own.astype(f32) + other.astype(f32)).astype(bf16)]
    ppermute x0 -> x3, starting transfers between devices: none -> 3.93 us  [shards(): sums += lax.ppermute(sums, 'tp', [(i, i ^ distance) for i in range(peers)])]
    pallas_call x6, Pallas kernels: 24.6 us -> 20.8 us  [call(): pl.pallas_call(kernel, out_shape=shapes, compiler_params=pltpu.CompilerPa...]
  transfers between devices with their start and end apart: 8 -> 10, of which waited for: 7 -> 9; matrix products, arithmetic and copies ran while one was open for 0% -> 1% of each run, Pallas kernels for 0% -> 1%
where the time goes in v2:
time: 249 us; the launch traced here: 248 us
  waiting for transfers between devices  140 us (56%)
  Pallas kernels  39.2 us (16%)
  starting transfers between devices  33 us (13%)
  blocking collectives  14.7 us (6%)
  between operations  13.5 us (5%)
  local copies, waits for them, and re-layouts  6.6 us (3%)
    reduce_scatter x1, waiting for transfers between devices, shards(): lax.psum_scatter(both.reshape(peers * held, share), 'tp', scatter_dimensi...  45.5 us
    all_gather x1, waiting for transfers between devices, shards(): lax.all_gather(arrived.reshape(chips * capacity, share), ('core', 'tp'))  38.8 us
    all_to_all x1, waiting for transfers between devices, shards(): partial = lax.all_to_all(partial, 'tp', 0, 0, tiled=True)  21.4 us
    pallas_call x6, Pallas kernels, call(): pl.pallas_call(kernel, out_shape=shapes, compiler_params=pltpu.CompilerPa...  20.8 us
    ppermute x3, waiting for transfers between devices, shards(): sums += lax.ppermute(sums, 'tp', [(i, i ^ distance) for i in range(peers)])  16.4 us
    pallas_call x1, Pallas kernels, shards(): pl.pallas_call(functools.partial(expert_kernel, width=width, per_half=per...  15.7 us
    all_to_all x1, blocking collectives, shards(): lax.all_to_all(outgoing.reshape(chips, capacity, share), 'chip', 0, 0, ti...  14.7 us
    all_to_all x1, starting transfers between devices, shards(): partial = lax.all_to_all(partial, 'tp', 0, 0, tiled=True)  8.6 us
  transfers between devices with their start and end apart: 10, of which 9 were waited for; matrix products, arithmetic and copies ran while one was open for 1% of the time, Pallas kernels for 1%

profile of v2, /device:TPU:2, one launch (start us, length us, event | category | flops | bytes accessed | tf_op | source)
XLA Modules:
  0.0 247.7 jit_solution(16803621417155965031)
XLA Ops:
  6.5 2.2 shard_map.146
  8.8 7.6 %all-to-all-start = ((bf16[32,32,128]{2,1,0:T(8,128)(2,1)}), bf16[32,32,128]{2,1,0:T(8,128)(2,1)S(1)}, u32[]{:S(2)}, u32[]{:S(2)}) async-start(bf16[32,32,128]{2,1,0:T(8,128)(2,1)} %bitcast.23), calls=%async_computation | async-start | bytes 524288 | tf_op jit(solution)/shard_map/all_to_all | solution.py:222
  16.4 7.7 %all-to-all-done.received = bf16[32,32,128]{2,1,0:T(8,128)(2,1)S(1)} async-done(((bf16[32,32,128]{2,1,0:T(8,128)(2,1)}), bf16[32,32,128]{2,1,0:T(8,128)(2,1)S(1)}, u32[]{:S(2)}, u32[]{:S(2)}) %all-to-all-start) | async-done | bytes 262176 | tf_op jit(solution)/shard_map/all_to_all | solution.py:222
  24.8 1.8 shard_map.147
  26.5 5.0 %all-to-all-start.1 = ((bf16[32,16,128]{2,1,0:T(8,128)(2,1)}), bf16[32,16,128]{2,1,0:T(8,128)(2,1)S(1)}, u32[]{:S(2)}, u32[]{:S(2)}) async-start(bf16[32,16,128]{2,1,0:T(8,128)(2,1)} %shard_map.147), calls=%async_computation.1 | async-start | bytes 262144 | tf_op jit(solution)/shard_map/all_to_all | solution.py:233
  31.5 2.7 %shard_map.145 = (f32[128,512]{1,0:T(8,128)}, f32[128,512]{1,0:T(8,128)}) custom-call(bf16[128,512]{1,0:T(8,128)(2,1)} %queries.3, bf16[128,512]{1,0:T(8,128)(2,1)} %keys.3, bf16[128,512]{1,0:T(8,128)(2,1)} %values.3, f32[4,128]{1,0:T(4,128)} %log_decay.3), custom_call_target="tpu_custom_call" | custom-call | tf_op jit(solution)/shard_map/pallas_call | solution.py:190
  34.2 4.0 %all-to-all-done.1 = bf16[32,16,128]{2,1,0:T(8,128)(2,1)S(1)} async-done(((bf16[32,16,128]{2,1,0:T(8,128)(2,1)}), bf16[32,16,128]{2,1,0:T(8,128)(2,1)S(1)}, u32[]{:S(2)}, u32[]{:S(2)}) %all-to-all-start.1) | async-done | bytes 131104 | tf_op jit(solution)/shard_map/all_to_all | solution.py:233
  38.9 4.8 %shard_map.148 = bf16[8,128,384]{2,1,0:T(8,128)(2,1)} custom-call(bf16[128,512]{1,0:T(8,128)(2,1)} %queries.3, f32[128,512]{1,0:T(8,128)} %get-tuple-element.12.inner, f32[128,512]{1,0:T(8,128)} %get-tuple-element.13.growth, bf16[512,128]{1,0:T(8,128)(2,1)} %bitcast.24, bf16[128,512]{1,0:T(8,128)(2,1)} %gate_input.1, f32[1,512]{1,0:T(1,128)} %bitcast.30, ...), custom_call_target="tpu_custom_call" | custom-call | tf_op jit(solution)/shard_map/pallas_call | solution.py:190
  43.7 8.6 %all-to-all-start.2 = ((bf16[8,128,384]{2,1,0:T(8,128)(2,1)}), bf16[8,128,384]{2,1,0:T(8,128)(2,1)S(1)}, u32[]{:S(2)}, u32[]{:S(2)}) async-start(bf16[8,128,384]{2,1,0:T(8,128)(2,1)} %shard_map.148), calls=%async_computation.2 | async-start | bytes 1572864 | tf_op jit(solution)/shard_map/all_to_all | solution.py:248
  54.3 21.4 %all-to-all-done.2.partial = bf16[8,128,384]{2,1,0:T(8,128)(2,1)S(1)} async-done(((bf16[8,128,384]{2,1,0:T(8,128)(2,1)}), bf16[8,128,384]{2,1,0:T(8,128)(2,1)S(1)}, u32[]{:S(2)}, u32[]{:S(2)}) %all-to-all-start.2) | async-done | bytes 786464 | tf_op jit(solution)/shard_map/all_to_all | solution.py:248
  76.6 2.7 %shard_map.149 = (bf16[512,384]{1,0:T(8,128)(2,1)}, f32[128,384]{1,0:T(8,128)}, f32[128,128]{1,0:T(8,128)}) custom-call(s32[1]{0:T(128)} %bitcast.1.index, bf16[8,128,384]{2,1,0:T(8,128)(2,1)} %copy-done, bf16[128,384]{1,0:T(8,128)(2,1)} %layer_input.1, f32[8,1,384]{2,1,0:T(1,128)} %bitcast.28, bf16[3072,16]{1,0:T(8,128)(2,1)} %copy.19.router, ...), custom_call_target="tpu_custom_call" | custom-call | tf_op jit(solution)/shard_map/pallas_call | solution.py:249
  79.4 14.7 %all_to_all.25 = bf16[16,32,384]{2,1,0:T(8,128)(2,1)} all-to-all(bf16[16,32,384]{2,1,0:T(8,128)(2,1)} %bitcast.26), channel_id=1, replica_groups=mesh['chip'=16,'core'=2,'tp'=8] {'chip'}, dimensions={0} | all-to-all | bytes 786432 | tf_op jit(solution)/shard_map/all_to_all | solution.py:267
  94.7 38.8 %all-gather.2.cloned.1.call-done.rows = bf16[16,512,384]{2,1,0:T(8,128)(2,1)} async-done(((bf16[1,512,384]{2,1,0:T(8,128)(2,1)}), bf16[16,512,384]{2,1,0:T(8,128)(2,1)}) %all-gather.2.cloned.1.call-update) | async-done | bytes 6291472 | tf_op jit(solution)/shard_map/all_gather | solution.py:268
  133.6 15.7 %shard_map.150 = (bf16[8,512,384]{2,1,0:T(8,128)(2,1)}, bf16[8,512,384]{2,1,0:T(8,128)(2,1)}) custom-call(s32[1]{0:T(128)} %bitcast.core, bf16[16,512,384]{2,1,0:T(8,128)(2,1)} %all-gather.2.cloned.1.call-done.rows, f32[1,3072]{1,0:T(1,128)} %bitcast.29, bf16[3072,384]{1,0:T(8,128)(2,1)} %bitcast.18, bf16[3072,384]{1,0:T(8,128)(2,1)} %bitcast.19, ...), custom_call_target="tpu_custom_call" | custom-call | tf_op jit(solution)/shard_map/pallas_call | solution.py:275
  149.6 5.6 %collective-permute-done.b = bf16[8,512,384]{2,1,0:T(8,128)(2,1)S(1)} collective-permute-done((bf16[8,512,384]{2,1,0:T(8,128)(2,1)}, bf16[8,512,384]{2,1,0:T(8,128)(2,1)S(1)}, u32[]{:S(2)}, u32[]{:S(2)}) %collective-permute-start) | collective-permute-done | bytes 3145760 | tf_op jit(solution)/shard_map/ppermute | solution.py:301
  155.2 1.7 copy-done.1
  156.9 7.0 %shard_map.151 = bf16[8,512,384]{2,1,0:T(8,128)(2,1)} custom-call(bf16[8,512,384]{2,1,0:T(8,128)(2,1)} %get-tuple-element.15.a, bf16[8,512,384]{2,1,0:T(8,128)(2,1)} %copy-done.1), custom_call_target="tpu_custom_call" | custom-call | tf_op jit(solution)/shard_map/pallas_call | solution.py:190
  163.9 45.5 %reduce-scatter.2.cloned.1.call-done = bf16[512,384]{1,0:T(8,128)(2,1)} async-done(((bf16[4096,384]{1,0:T(8,128)(2,1)}), bf16[512,384]{1,0:T(8,128)(2,1)}) %reduce-scatter.2.cloned.1.call-update) | async-done | bytes 393232 | tf_op jit(solution)/shard_map/reduce_scatter | solution.py:307
  209.4 7.5 %all-to-all-start.4 = ((bf16[16,32,384]{2,1,0:T(8,128)(2,1)}), bf16[16,32,384]{2,1,0:T(8,128)(2,1)S(1)}, u32[]{:S(2)}, u32[]{:S(2)}) async-start(bf16[16,32,384]{2,1,0:T(8,128)(2,1)} %bitcast.25), calls=%async_computation.5 | async-start | bytes 786432 | tf_op jit(solution)/shard_map/all_to_all | solution.py:308
  217.7 4.2 %collective-permute-done.1 = f32[128,128]{1,0:T(8,128)S(1)} collective-permute-done((f32[128,128]{1,0:T(8,128)S(1)}, f32[128,128]{1,0:T(8,128)S(1)}, u32[]{:S(2)}, u32[]{:S(2)}) %collective-permute-start.1) | collective-permute-done | bytes 65568 | tf_op jit(solution)/shard_map/ppermute | solution.py:270
  222.8 6.1 %collective-permute-done.2 = f32[128,128]{1,0:T(8,128)S(1)} collective-permute-done((f32[128,128]{1,0:T(8,128)S(1)}, f32[128,128]{1,0:T(8,128)S(1)}, u32[]{:S(2)}, u32[]{:S(2)}) %collective-permute-start.2) | collective-permute-done | bytes 65568 | tf_op jit(solution)/shard_map/ppermute | solution.py:270
  228.9 2.1 collective-permute-start.3
  231.0 6.1 %collective-permute-done.3 = f32[128,128]{1,0:T(8,128)S(1)} collective-permute-done((f32[128,128]{1,0:T(8,128)S(1)}, f32[128,128]{1,0:T(8,128)S(1)}, u32[]{:S(2)}, u32[]{:S(2)}) %collective-permute-start.3) | collective-permute-done | bytes 65568 | tf_op jit(solution)/shard_map/ppermute | solution.py:270
  238.6 2.3 shard_map.152
  (31 shorter events, 8.4 us)
Async XLA Ops:
  8.8 15.3 %all-to-all-start = ((bf16[32,32,128]{2,1,0:T(8,128)(2,1)}), bf16[32,32,128]{2,1,0:T(8,128)(2,1)S(1)}, u32[]{:S(2)}, u32[]{:S(2)}) async-start(bf16[32,32,128]{2,1,0:T(8,128)(2,1)} %bitcast.23), calls=%async_computation | async-start | bytes 524288 | tf_op jit(solution)/shard_map/all_to_all | solution.py:222
  24.1 0.7 copy-start.3
  26.5 11.7 %all-to-all-start.1 = ((bf16[32,16,128]{2,1,0:T(8,128)(2,1)}), bf16[32,16,128]{2,1,0:T(8,128)(2,1)S(1)}, u32[]{:S(2)}, u32[]{:S(2)}) async-start(bf16[32,16,128]{2,1,0:T(8,128)(2,1)} %shard_map.147), calls=%async_computation.1 | async-start | bytes 262144 | tf_op jit(solution)/shard_map/all_to_all | solution.py:233
  38.2 0.7 copy-start.4
  38.9 13.5 %copy-start.8 = (s32[128,2]{0,1:T(2,128)S(1)}, s32[128,2]{0,1:T(2,128)}, u32[]{:S(2)}) copy-start(s32[128,2]{0,1:T(2,128)} %param.26) | copy-start | bytes 3076
  38.9 14.2 %copy-start.5 = (bf16[3072,16]{0,1:T(8,128)(2,1)S(1)}, bf16[3072,16]{0,1:T(8,128)(2,1)}, u32[]{:S(2)}) copy-start(bf16[3072,16]{0,1:T(8,128)(2,1)} %param.25) | copy-start | bytes 294916
  43.7 50.4 %copy-start.7 = (f32[3072]{0:T(1024)S(1)}, f32[3072]{0:T(1024)}, u32[]{:S(2)}) copy-start(f32[3072]{0:T(1024)} %param.24) | copy-start | bytes 36868
  43.7 32.0 %all-to-all-start.2 = ((bf16[8,128,384]{2,1,0:T(8,128)(2,1)}), bf16[8,128,384]{2,1,0:T(8,128)(2,1)S(1)}, u32[]{:S(2)}, u32[]{:S(2)}) async-start(bf16[8,128,384]{2,1,0:T(8,128)(2,1)} %shard_map.148), calls=%async_computation.2 | async-start | bytes 1572864 | tf_op jit(solution)/shard_map/all_to_all | solution.py:248
  52.3 81.2 %all-gather.2.cloned.1.call-start = ((), (), s32[]{:S(2)}) async-start(), calls=%async_computation.6 | async-start | bytes 6684672 | tf_op jit(solution)/shard_map/all_gather | solution.py:268
  75.8 0.9 copy-start
  94.1 115.3 %reduce-scatter.2.cloned.1.call-start = ((), (), s32[]{:S(2)}) async-start(), calls=%async_computation.7 | async-start | bytes 3538944 | tf_op jit(solution)/shard_map/reduce_scatter | solution.py:307
  149.3 6.0 %collective-permute-start = (bf16[8,512,384]{2,1,0:T(8,128)(2,1)}, bf16[8,512,384]{2,1,0:T(8,128)(2,1)S(1)}, u32[]{:S(2)}, u32[]{:S(2)}) collective-permute-start(bf16[8,512,384]{2,1,0:T(8,128)(2,1)} %get-tuple-element.16), channel_id=1, source_target_pairs={{0,8},{8,0},{1,9},{9,1},{2,10},{10,2},{3,11},{11,3},{4,12},{12,4},... | collective-permute-start | bytes 9437192 | tf_op jit(solution)/shard_map/ppermute | solution.py:301
  155.2 1.7 copy-start.1
  163.9 53.0 %copy-start.6 = (f32[128,128]{1,0:T(8,128)S(1)}, f32[128,128]{1,0:T(8,128)}, u32[]{:S(2)}) copy-start(f32[128,128]{1,0:T(8,128)} %get-tuple-element.18) | copy-start | bytes 196612
  209.4 28.4 %all-to-all-start.4 = ((bf16[16,32,384]{2,1,0:T(8,128)(2,1)}), bf16[16,32,384]{2,1,0:T(8,128)(2,1)S(1)}, u32[]{:S(2)}, u32[]{:S(2)}) async-start(bf16[16,32,384]{2,1,0:T(8,128)(2,1)} %bitcast.25), calls=%async_computation.5 | async-start | bytes 786432 | tf_op jit(solution)/shard_map/all_to_all | solution.py:308
  216.8 5.0 %collective-permute-start.1 = (f32[128,128]{1,0:T(8,128)S(1)}, f32[128,128]{1,0:T(8,128)S(1)}, u32[]{:S(2)}, u32[]{:S(2)}) collective-permute-start(f32[128,128]{1,0:T(8,128)S(1)} %copy-done.6), channel_id=1, source_target_pairs={{0,1},{1,0},{2,3},{3,2},{4,5},{5,4},{6,7},{7,6},{8,9},{9,8},{10,11... | collective-permute-start | bytes 196616 | tf_op jit(solution)/shard_map/ppermute | solution.py:270
  221.9 7.0 %collective-permute-start.2 = (f32[128,128]{1,0:T(8,128)S(1)}, f32[128,128]{1,0:T(8,128)S(1)}, u32[]{:S(2)}, u32[]{:S(2)}) collective-permute-start(f32[128,128]{1,0:T(8,128)S(1)} %add.15), channel_id=1, source_target_pairs={{0,2},{1,3},{2,0},{3,1},{4,6},{5,7},{6,4},{7,5},{8,10},{9,11},{10,... | collective-permute-start | bytes 196616 | tf_op jit(solution)/shard_map/ppermute | solution.py:270
  228.9 8.3 %collective-permute-start.3 = (f32[128,128]{1,0:T(8,128)S(1)}, f32[128,128]{1,0:T(8,128)S(1)}, u32[]{:S(2)}, u32[]{:S(2)}) collective-permute-start(f32[128,128]{1,0:T(8,128)S(1)} %add.16), channel_id=1, source_target_pairs={{0,4},{1,5},{2,6},{3,7},{4,0},{5,1},{6,2},{7,3},{8,12},{9,13},{10,... | collective-permute-start | bytes 196616 | tf_op jit(solution)/shard_map/ppermute | solution.py:270
  237.8 0.7 copy-start.2
Sparse Core Ops, SparseCore 0:
  94.2 39.3 all-gather.1
  164.0 45.3 reduce-scatter.1

commit v3 on v2

--- a/solution.py
+++ b/solution.py
@@ -126,23 +126,24 @@
     outgoing[...] = mm(chosen, scaled, 0, 0).astype(bf16)
 
 
-def expert_kernel(core, rows, inverse, gate_hbm, up_hbm, down_hbm, other, own, gate_up, down, sems, *, width, per_half):
-    del core
+def fetch(pairs, sems):
+    copies = [pltpu.make_async_copy(source, target, sems.at[k]) for k, (source, target) in enumerate(pairs)]
+    for copy in copies:
+        copy.start()
+    return copies
+
+
+def column_pairs(tp, hbm, scratch, distances, peers):
+    share = hbm.shape[1] // peers
+    pairs = []
+    for k, distance in enumerate(distances):
+        start = pl.multiple_of(lax.rem(tp + distance + peers, peers) * share, share)
+        pairs.append((hbm.at[:, pl.ds(start, share)], scratch.at[:, pl.ds(k * share, share)]))
+    return pairs
+
+
+def activate(rows, inverse, gate_up, width):
     chunks, _, share = rows.shape
-    step = pl.program_id(0)
-    copies = [
-        pltpu.make_async_copy(gate_hbm, gate_up.at[:, pl.ds(0, share)], sems.at[0]),
-        pltpu.make_async_copy(up_hbm, gate_up.at[:, pl.ds(share, share)], sems.at[1]),
-        pltpu.make_async_copy(down_hbm, down, sems.at[2]),
-    ]
-
-    @pl.when(step == 0)
-    def _():
-        for copy in copies:
-            copy.start()
-        copies[0].wait()
-        copies[1].wait()
-
     squares = jnp.zeros((rows.shape[1], 1), f32)
     total = jnp.zeros((rows.shape[1], 2 * share), f32)
     for c in range(0, chunks, 2):
@@ -153,24 +154,69 @@
         total += mm(pair, gate_up[lanes, :])
     total *= lax.rsqrt(squares / width + epsilon)
     gated = total[:, :share]
-    activated = (gated * jax.nn.sigmoid(gated) * total[:, share:]).astype(bf16)
-
-    @pl.when(step == 0)
+    return (gated * jax.nn.sigmoid(gated) * total[:, share:]).astype(bf16)
+
+
+def products(activated, down, chunks):
+    share = down.shape[1] // chunks
+    found = []
+    for c in range(0, chunks, 2):
+        both = min(2, chunks - c)
+        product = mm(activated, down[:, c * share:(c + both) * share])
+        found += [product[:, k * share:(k + 1) * share] for k in range(both)]
+    return found
+
+
+def other_half_kernel(
+    place, rows, inverse, gate_hbm, up_hbm, down_hbm, first, rest, gate_up, down, sems, *, width, distances
+):
+    chunks, _, share = rows.shape
+    near = len(distances) - rest.shape[0]
+    pairs = [(gate_hbm, gate_up.at[:, pl.ds(0, share)]), (up_hbm, gate_up.at[:, pl.ds(share, share)])]
+    pairs += column_pairs(place[1], down_hbm, down, distances, chunks)
+
+    @pl.when(pl.program_id(0) == 0)
     def _():
-        copies[2].wait()
-
-    def produce(out):
-        for c in range(0, chunks, 2):
-            product = mm(activated, down[:, c * share:(c + 2) * share])
-            out[c] = product[:, :share].astype(bf16)
-            out[c + 1] = product[:, share:].astype(bf16)
-
-    pl.when(step < per_half)(lambda: produce(other))
-    pl.when(step >= per_half)(lambda: produce(own))
-
-
-def add_kernel(a, b, out):
-    out[...] = (a[...].astype(f32) + b[...].astype(f32)).astype(bf16)
+        copies = fetch(pairs, sems)
+        for copy in copies:
+            copy.wait()
+
+    for k, product in enumerate(products(activate(rows, inverse, gate_up, width), down, chunks)):
+        if k < near:
+            first[k] = product.astype(bf16)
+        else:
+            rest[k - near] = product.astype(bf16)
+
+
+def own_half_kernel(place, rows, inverse, gate_hbm, up_hbm, out, gate_up, sems, *, width):
+    del place
+    share = rows.shape[2]
+
+    @pl.when(pl.program_id(0) == 0)
+    def _():
+        copies = fetch([(gate_hbm, gate_up.at[:, pl.ds(0, share)]), (up_hbm, gate_up.at[:, pl.ds(share, share)])], sems)
+        for copy in copies:
+            copy.wait()
+
+    out[...] = activate(rows, inverse, gate_up, width)
+
+
+def own_products_kernel(place, activated, sibling, down_hbm, *rest, distances, peers, split):
+    outs, (down, sems) = rest[:-2], rest[-2:]
+    copies = fetch(column_pairs(place[1], down_hbm, down, distances, peers), sems)
+    for copy in copies:
+        copy.wait()
+    half = activated.shape[0] // 2
+    for h in range(2):
+        rows = slice(h * half, (h + 1) * half)
+        for k, product in enumerate(products(activated[rows, :], down, len(distances))):
+            total = (product + sibling[k, rows, :].astype(f32)).astype(bf16)
+            if split:
+                outs[2 * k + h][...] = total
+            elif k < len(distances) - 1:
+                outs[2 * k + h][...] = total
+            else:
+                outs[-1][rows, :] = total
 
 
 def combine_kernel(returned, hidden, sums, ids, out, *, experts, capacity, width):
@@ -268,43 +314,92 @@
     gathered = lax.all_gather(arrived.reshape(chips * capacity, share), ("core", "tp"))
     for distance in (1, 2, 4):
         sums += lax.ppermute(sums, "tp", [(i, i ^ distance) for i in range(peers)])
+    gathered, sums = lax.optimization_barrier((gathered, sums))
+    gathered = gathered.reshape(cores * peers, chips * capacity, share)
     held = chips * capacity
     rows_step = 256
     per_half = held // rows_step
+    half = held // 2
+    far, near = (4, 3, -3), (2, -2, 1, -1, 0)
+    place = jnp.stack([core, tp])
+    inverse = (1.0 / moe_gain).reshape(1, width)
+    params = pltpu.CompilerParams(vmem_limit_bytes=LIMIT)
+    hbm = pl.BlockSpec(memory_space=pl.ANY)
+    gate, up, down = w_gate[0], w_up[0], w_down[0]
+    work = 2 * held * width * share
     block = (peers, rows_step, share)
-    other, own = pl.pallas_call(
-        functools.partial(expert_kernel, width=width, per_half=per_half),
-        out_shape=(struct((peers, held, share), bf16),) * 2,
+
+    first, rest = pl.pallas_call(
+        functools.partial(other_half_kernel, width=width, distances=far + near),
+        out_shape=(struct((len(far), held, share), bf16), struct((len(near), held, share), bf16)),
         grid_spec=pltpu.PrefetchScalarGridSpec(
             num_scalar_prefetch=1,
-            grid=(cores * per_half,),
-            in_specs=[
-                pl.BlockSpec(block, lambda i, core: (jnp.where(i < per_half, 1 - core[0], core[0]), i % per_half, 0)),
-                whole((1, width)),
-            ] + [pl.BlockSpec(memory_space=pl.ANY)] * 3,
+            grid=(per_half,),
+            in_specs=[pl.BlockSpec(block, lambda i, place: (1 - place[0], i, 0)), whole((1, width)), hbm, hbm, hbm],
             out_specs=[
-                pl.BlockSpec(block, lambda i, core: (0, jnp.minimum(i, per_half - 1), 0)),
-                pl.BlockSpec(block, lambda i, core: (0, jnp.maximum(i - per_half, 0), 0)),
+                pl.BlockSpec((len(far), rows_step, share), lambda i, place: (0, i, 0)),
+                pl.BlockSpec((len(near), rows_step, share), lambda i, place: (0, i, 0)),
             ],
             scratch_shapes=[
                 pltpu.VMEM((width, 2 * share), bf16),
                 pltpu.VMEM((share, width), bf16),
-                pltpu.SemaphoreType.DMA((3,)),
+                pltpu.SemaphoreType.DMA((2 + peers,)),
             ],
         ),
-        compiler_params=pltpu.CompilerParams(vmem_limit_bytes=LIMIT),
-    )(
-        core.reshape(1), gathered.reshape(cores * peers, held, share), (1.0 / moe_gain).reshape(1, width),
-        w_gate[0], w_up[0], w_down[0],
-    )
-
-    other = lax.ppermute(other, "core", [(0, 1), (1, 0)])
-    part = pl.BlockSpec((1, held, share), lambda i: (i, 0, 0))
-    both = call(
-        add_kernel, struct((peers, held, share), bf16), own, other,
-        grid=(peers,), in_specs=[part, part], out_specs=part,
-    )
-    summed = lax.psum_scatter(both.reshape(peers * held, share), "tp", scatter_dimension=0, tiled=True)
+        compiler_params=params,
+        cost_estimate=pl.CostEstimate(flops=3 * work, bytes_accessed=14 << 20, transcendentals=held * share),
+    )(place, gathered, inverse, gate, up, down)
+    swap = [(0, 1), (1, 0)]
+    first = lax.ppermute(first, "core", swap)
+    rest = lax.ppermute(rest, "core", swap)
+    activated = pl.pallas_call(
+        functools.partial(own_half_kernel, width=width),
+        out_shape=struct((held, share), bf16),
+        grid_spec=pltpu.PrefetchScalarGridSpec(
+            num_scalar_prefetch=1,
+            grid=(per_half,),
+            in_specs=[pl.BlockSpec(block, lambda i, place: (place[0], i, 0)), whole((1, width)), hbm, hbm],
+            out_specs=pl.BlockSpec((rows_step, share), lambda i, place: (i, 0)),
+            scratch_shapes=[pltpu.VMEM((width, 2 * share), bf16), pltpu.SemaphoreType.DMA((2,))],
+        ),
+        compiler_params=params,
+        cost_estimate=pl.CostEstimate(flops=2 * work, bytes_accessed=8 << 20, transcendentals=held * share),
+    )(place, gathered, inverse, gate, up)
+
+    def own_products(sibling, distances, split):
+        n = len(distances)
+        piece = struct((half, share), bf16)
+        shapes = (piece,) * (2 * n) if split else (piece,) * (2 * n - 2) + (struct((held, share), bf16),)
+        return pl.pallas_call(
+            functools.partial(own_products_kernel, distances=distances, peers=peers, split=split),
+            out_shape=shapes,
+            grid_spec=pltpu.PrefetchScalarGridSpec(
+                num_scalar_prefetch=1,
+                grid=(1,),
+                in_specs=[whole((held, share)), whole((n, held, share)), hbm],
+                out_specs=[whole(s.shape) for s in shapes],
+                scratch_shapes=[pltpu.VMEM((share, n * share), bf16), pltpu.SemaphoreType.DMA((n,))],
+            ),
+            compiler_params=pltpu.CompilerParams(vmem_limit_bytes=24 << 20),
+            cost_estimate=pl.CostEstimate(flops=n * work // peers, bytes_accessed=3 * n * held * share * 2, transcendentals=0),
+        )(place, activated, sibling, down)
+
+    def moved(piece, step):
+        return lax.ppermute(piece, "tp", [(i, (i + step) % peers) for i in range(peers)])
+
+    def plus(*pieces):
+        return sum(piece.astype(f32) for piece in pieces).astype(bf16)
+
+    a4, b4, a3, b3, a3m, b3m = own_products(first, far, True)
+    a_up, b_down = moved(a4, 1), moved(b4, -1)
+    a_down, b_up = moved(a3m, -1), moved(b3, 1)
+    a2, b2, a2m, b2m, a1, b1, a1m, b1m, mine = own_products(rest, near, False)
+    a_up, b_down = moved(plus(a_up, a3), 1), moved(plus(b_down, b3m), -1)
+    a_down, b_up = moved(plus(a_down, a2m), -1), moved(plus(b_up, b2), 1)
+    a_up, b_down = moved(plus(a_up, a2), 1), moved(plus(b_down, b2m), -1)
+    a_down, b_up = moved(plus(a_down, a1m), -1), moved(plus(b_up, b1), 1)
+    a_up, b_down = moved(plus(a_up, a1), 1), moved(plus(b_down, b1m), -1)
+    summed = jnp.concatenate([plus(mine[:half], a_up, a_down), plus(mine[half:], b_up, b_down)])
     returned = lax.all_to_all(summed.reshape(chips, capacity, share), "chip", 0, 0, tiled=True)
     return call(
         functools.partial(combine_kernel, experts=experts, capacity=capacity, width=width),

time: 249 us -> 225 us (0.904)
  waiting for transfers between devices: 140 us -> 83.3 us
  blocking collectives: 14.7 us -> 29.8 us
  starting transfers between devices: 33 us -> 45.9 us
  Pallas kernels: 39.2 us -> 43 us
    reduce_scatter x1 -> x0, waiting for transfers between devices: 45.5 us -> none  [shards(): lax.psum_scatter(both.reshape(peers * held, share), 'tp', scatter_dimensi...]
    ppermute x1 -> x16, starting transfers between devices: 0.34 us -> 24.5 us  [the longest x14 23.9 us: moved(): lax.ppermute(piece, 'tp', [(i, (i + step) % peers) for i in range(peers)])]
    all_gather x1, waiting for transfers between devices: 38.8 us -> 19 us  [shards(): lax.all_gather(arrived.reshape(chips * capacity, share), ('core', 'tp'))]
    all_to_all x0 -> x1, blocking collectives: none -> 15.1 us  [shards(): lax.all_to_all(summed.reshape(chips, capacity, share), 'chip', 0, 0, tile...]
    pallas_call x1 -> x4, Pallas kernels: 15.7 us -> 26.4 us  [the longest x1 12.9 us: shards(): pl.pallas_call(functools.partial(other_half_kernel, width=width, distance...]
    all_to_all x1 -> x0, starting transfers between devices: 7.46 us -> none  [shards(): lax.all_to_all(summed.reshape(chips, capacity, share), 'chip', 0, 0, tile...]
    pallas_call x6 -> x5, Pallas kernels: 20.8 us -> 13.9 us  [call(): pl.pallas_call(kernel, out_shape=shapes, compiler_params=pltpu.CompilerPa...]
    ppermute x1 -> x16, waiting for transfers between devices: 5.62 us -> 10.8 us  [the longest x14 10.8 us: moved(): lax.ppermute(piece, 'tp', [(i, (i + step) % peers) for i in range(peers)])]
  transfers between devices with their start and end apart: 10 -> 23, of which waited for: 9 -> 14; matrix products, arithmetic and copies ran while one was open for 1% -> 2% of each run, Pallas kernels for 1% -> 7%
where the time goes in v3:
time: 225 us; the launch traced here: 224 us
  waiting for transfers between devices  83.3 us (37%)
  starting transfers between devices  45.9 us (20%)
  Pallas kernels  43 us (19%)
  blocking collectives  29.8 us (13%)
  between operations  13.7 us (6%)
  local copies, waits for them, and re-layouts  5.16 us (2%)
  other arithmetic  3.42 us (2%)
    ppermute x14, starting transfers between devices, moved(): lax.ppermute(piece, 'tp', [(i, (i + step) % peers) for i in range(peers)])  23.9 us
    all_to_all x1, waiting for transfers between devices, shards(): partial = lax.all_to_all(partial, 'tp', 0, 0, tiled=True)  21.4 us
    ppermute x3, waiting for transfers between devices, shards(): sums += lax.ppermute(sums, 'tp', [(i, i ^ distance) for i in range(peers)])  20.4 us
    all_gather x1, waiting for transfers between devices, shards(): lax.all_gather(arrived.reshape(chips * capacity, share), ('core', 'tp'))  19 us
    all_to_all x1, blocking collectives, shards(): lax.all_to_all(summed.reshape(chips, capacity, share), 'chip', 0, 0, tile...  15.1 us
    all_to_all x1, blocking collectives, shards(): lax.all_to_all(outgoing.reshape(chips, capacity, share), 'chip', 0, 0, ti...  14.7 us
    pallas_call x5, Pallas kernels, call(): pl.pallas_call(kernel, out_shape=shapes, compiler_params=pltpu.CompilerPa...  13.9 us
    pallas_call x1, Pallas kernels, shards(): pl.pallas_call(functools.partial(other_half_kernel, width=width, distance...  12.9 us
  transfers between devices with their start and end apart: 23, of which 14 were waited for; matrix products, arithmetic and copies ran while one was open for 2% of the time, Pallas kernels for 7%

profile of v3, /device:TPU:2, one launch (start us, length us, event | category | flops | bytes accessed | tf_op | source)
XLA Modules:
  0.0 224.3 jit_solution(16098793052621162861)
XLA Ops:
  8.8 7.6 %all-to-all-start = ((bf16[32,32,128]{2,1,0:T(8,128)(2,1)}), bf16[32,32,128]{2,1,0:T(8,128)(2,1)S(1)}, u32[]{:S(2)}, u32[]{:S(2)}) async-start(bf16[32,32,128]{2,1,0:T(8,128)(2,1)} %bitcast.26), calls=%async_computation | async-start | bytes 524288 | tf_op jit(solution)/shard_map/all_to_all | solution.py:268
  16.4 7.7 %all-to-all-done.received = bf16[32,32,128]{2,1,0:T(8,128)(2,1)S(1)} async-done(((bf16[32,32,128]{2,1,0:T(8,128)(2,1)}), bf16[32,32,128]{2,1,0:T(8,128)(2,1)S(1)}, u32[]{:S(2)}, u32[]{:S(2)}) %all-to-all-start) | async-done | bytes 262176 | tf_op jit(solution)/shard_map/all_to_all | solution.py:268
  26.5 5.0 %all-to-all-start.1 = ((bf16[32,16,128]{2,1,0:T(8,128)(2,1)}), bf16[32,16,128]{2,1,0:T(8,128)(2,1)S(1)}, u32[]{:S(2)}, u32[]{:S(2)}) async-start(bf16[32,16,128]{2,1,0:T(8,128)(2,1)} %shard_map.147), calls=%async_computation.1 | async-start | bytes 262144 | tf_op jit(solution)/shard_map/all_to_all | solution.py:279
  34.2 4.0 %all-to-all-done.1 = bf16[32,16,128]{2,1,0:T(8,128)(2,1)S(1)} async-done(((bf16[32,16,128]{2,1,0:T(8,128)(2,1)}), bf16[32,16,128]{2,1,0:T(8,128)(2,1)S(1)}, u32[]{:S(2)}, u32[]{:S(2)}) %all-to-all-start.1) | async-done | bytes 131104 | tf_op jit(solution)/shard_map/all_to_all | solution.py:279
  38.9 4.8 %shard_map.148 = bf16[8,128,384]{2,1,0:T(8,128)(2,1)} custom-call(bf16[128,512]{1,0:T(8,128)(2,1)} %queries.3, f32[128,512]{1,0:T(8,128)} %get-tuple-element.29.inner, f32[128,512]{1,0:T(8,128)} %get-tuple-element.30.growth, bf16[512,128]{1,0:T(8,128)(2,1)} %bitcast.27, bf16[128,512]{1,0:T(8,128)(2,1)} %gate_input.1, f32[1,512]{1,0:T(1,128)} %bitcast.33, ...), custom_call_target="tpu_custom_call" | custom-call | tf_op jit(solution)/shard_map/pallas_call | solution.py:236
  43.7 8.5 %all-to-all-start.2 = ((bf16[8,128,384]{2,1,0:T(8,128)(2,1)}), bf16[8,128,384]{2,1,0:T(8,128)(2,1)S(1)}, u32[]{:S(2)}, u32[]{:S(2)}) async-start(bf16[8,128,384]{2,1,0:T(8,128)(2,1)} %shard_map.148), calls=%async_computation.2 | async-start | bytes 1572864 | tf_op jit(solution)/shard_map/all_to_all | solution.py:294
  54.2 21.4 %all-to-all-done.2.partial = bf16[8,128,384]{2,1,0:T(8,128)(2,1)S(1)} async-done(((bf16[8,128,384]{2,1,0:T(8,128)(2,1)}), bf16[8,128,384]{2,1,0:T(8,128)(2,1)S(1)}, u32[]{:S(2)}, u32[]{:S(2)}) %all-to-all-start.2) | async-done | bytes 786464 | tf_op jit(solution)/shard_map/all_to_all | solution.py:294
  76.5 2.7 %shard_map.149 = (bf16[512,384]{1,0:T(8,128)(2,1)}, f32[128,384]{1,0:T(8,128)}, f32[128,128]{1,0:T(8,128)}) custom-call(s32[1]{0:T(128)} %bitcast.1.index, bf16[8,128,384]{2,1,0:T(8,128)(2,1)} %copy-done.3, bf16[128,384]{1,0:T(8,128)(2,1)} %layer_input.1, f32[8,1,384]{2,1,0:T(1,128)} %bitcast.30, bf16[3072,16]{1,0:T(8,128)(2,1)} %copy.19.router, ...), custom_call_target="tpu_custom_call" | custom-call | tf_op jit(solution)/shard_map/pallas_call | solution.py:295
  79.2 14.7 %all_to_all.25 = bf16[16,32,384]{2,1,0:T(8,128)(2,1)} all-to-all(bf16[16,32,384]{2,1,0:T(8,128)(2,1)} %bitcast.28), channel_id=1, replica_groups=mesh['chip'=16,'core'=2,'tp'=8] {'chip'}, dimensions={0} | all-to-all | bytes 786432 | tf_op jit(solution)/shard_map/all_to_all | solution.py:313
  94.0 4.5 %collective-permute-done = f32[128,128]{1,0:T(8,128)S(1)} collective-permute-done((f32[128,128]{1,0:T(8,128)}, f32[128,128]{1,0:T(8,128)S(1)}, u32[]{:S(2)}, u32[]{:S(2)}) %collective-permute-start) | collective-permute-done | bytes 65568 | tf_op jit(solution)/shard_map/ppermute | solution.py:316
  100.0 7.0 %collective-permute-done.1 = f32[128,128]{1,0:T(8,128)S(1)} collective-permute-done((f32[128,128]{1,0:T(8,128)S(1)}, f32[128,128]{1,0:T(8,128)S(1)}, u32[]{:S(2)}, u32[]{:S(2)}) %collective-permute-start.1) | collective-permute-done | bytes 65568 | tf_op jit(solution)/shard_map/ppermute | solution.py:316
  107.8 8.9 %collective-permute-done.2 = f32[128,128]{1,0:T(8,128)S(1)} collective-permute-done((f32[128,128]{1,0:T(8,128)S(1)}, f32[128,128]{1,0:T(8,128)S(1)}, u32[]{:S(2)}, u32[]{:S(2)}) %collective-permute-start.2) | collective-permute-done | bytes 65568 | tf_op jit(solution)/shard_map/ppermute | solution.py:316
  117.3 19.0 %all-gather.2.cloned.1.call-done.rows = bf16[16,512,384]{2,1,0:T(8,128)(2,1)} async-done(((bf16[1,512,384]{2,1,0:T(8,128)(2,1)}), bf16[16,512,384]{2,1,0:T(8,128)(2,1)}) %all-gather.2.cloned.1.call-update) | async-done | bytes 6291472 | tf_op jit(solution)/shard_map/all_gather | solution.py:314
  136.3 12.9 %shard_map.151 = (bf16[3,512,384]{2,1,0:T(8,128)(2,1)}, bf16[5,512,384]{2,1,0:T(8,128)(2,1)}) custom-call(s32[2]{0:T(128)} %pad_add_fusion.place, bf16[16,512,384]{2,1,0:T(8,128)(2,1)} %all-gather.2.cloned.1.call-done.rows, f32[1,3072]{1,0:T(1,128)} %bitcast.31, bf16[3072,384]{1,0:T(8,128)(2,1)} %bitcast.19, bf16[3072,384]{1,0:T(8,128)(2,1)} %bitcast.21, ...), custom_call_target="tpu_custom_call" | custom-call | flops 3623878656 | bytes 14680064 | tf_op jit(solution)/shard_map/pallas_call | solution.py:332
  149.9 8.4 %shard_map.150.activated = bf16[512,384]{1,0:T(8,128)(2,1)} custom-call(s32[2]{0:T(128)} %pad_add_fusion.place, bf16[16,512,384]{2,1,0:T(8,128)(2,1)} %all-gather.2.cloned.1.call-done.rows, f32[1,3072]{1,0:T(1,128)} %bitcast.32, bf16[3072,384]{1,0:T(8,128)(2,1)} %bitcast.20, bf16[3072,384]{1,0:T(8,128)(2,1)} %bitcast.22), custom_call_target="tpu_custom_call" | custom-call | flops 2415919104 | bytes 8388608 | tf_op jit(solution)/shard_map/pallas_call | solution.py:355
  164.2 3.2 %collective-permute-start.15 = (bf16[256,384]{1,0:T(8,128)(2,1)S(1)}, bf16[256,384]{1,0:T(8,128)(2,1)S(1)}, u32[]{:S(2)}, u32[]{:S(2)}) collective-permute-start(bf16[256,384]{1,0:T(8,128)(2,1)S(1)} %get-tuple-element.47), channel_id=1, source_target_pairs={{0,7},{1,0},{2,1},{3,2},{4,3},{5,4},{6,5},{7,6},{8,15},{9,8},{10,9... | collective-permute-start | bytes 589832 | tf_op jit(solution)/shard_map/ppermute | solution.py:388
  170.1 3.1 %collective-permute-done.15 = bf16[256,384]{1,0:T(8,128)(2,1)S(1)} collective-permute-done((bf16[256,384]{1,0:T(8,128)(2,1)S(1)}, bf16[256,384]{1,0:T(8,128)(2,1)S(1)}, u32[]{:S(2)}, u32[]{:S(2)}) %collective-permute-start.15) | collective-permute-done | bytes 196640 | tf_op jit(solution)/shard_map/ppermute | solution.py:388
  173.2 3.2 %collective-permute-start.16 = (bf16[256,384]{1,0:T(8,128)(2,1)S(1)}, bf16[256,384]{1,0:T(8,128)(2,1)S(1)}, u32[]{:S(2)}, u32[]{:S(2)}) collective-permute-start(bf16[256,384]{1,0:T(8,128)(2,1)S(1)} %add_convert_fusion.3), channel_id=1, source_target_pairs={{0,7},{1,0},{2,1},{3,2},{4,3},{5,4},{6,5},{7,6},{8,15},{9,8},{10,9... | collective-permute-start | bytes 589832 | tf_op jit(solution)/shard_map/ppermute | solution.py:388
  176.5 3.6 %shard_map.152 = (bf16[256,384]{1,0:T(8,128)(2,1)S(1)}, bf16[256,384]{1,0:T(8,128)(2,1)S(1)}, bf16[256,384]{1,0:T(8,128)(2,1)S(1)}, bf16[256,384]{1,0:T(8,128)(2...) custom-call(s32[2]{0:T(128)S(1)} %copy-done.2, ...), custom_call_target="tpu_custom_call" | custom-call | flops 754974720 | bytes 5898240 | tf_op jit(solution)/shard_map/pallas_call | solution.py:373
  180.3 3.3 %collective-permute-start.10 = (bf16[256,384]{1,0:T(8,128)(2,1)S(1)}, bf16[256,384]{1,0:T(8,128)(2,1)S(1)}, u32[]{:S(2)}, u32[]{:S(2)}) collective-permute-start(bf16[256,384]{1,0:T(8,128)(2,1)S(1)} %add_convert_fusion.8), channel_id=1, source_target_pairs={{0,7},{1,0},{2,1},{3,2},{4,3},{5,4},{6,5},{7,6},{8,15},{9,8},{10,9... | collective-permute-start | bytes 589832 | tf_op jit(solution)/shard_map/ppermute | solution.py:388
  183.8 3.3 %collective-permute-start.17 = (bf16[256,384]{1,0:T(8,128)(2,1)S(1)}, bf16[256,384]{1,0:T(8,128)(2,1)S(1)}, u32[]{:S(2)}, u32[]{:S(2)}) collective-permute-start(bf16[256,384]{1,0:T(8,128)(2,1)S(1)} %add_convert_fusion.2), channel_id=1, source_target_pairs={{0,7},{1,0},{2,1},{3,2},{4,3},{5,4},{6,5},{7,6},{8,15},{9,8},{10,9... | collective-permute-start | bytes 589832 | tf_op jit(solution)/shard_map/ppermute | solution.py:388
  188.6 3.6 %collective-permute-start.11 = (bf16[256,384]{1,0:T(8,128)(2,1)S(1)}, bf16[256,384]{1,0:T(8,128)(2,1)S(1)}, u32[]{:S(2)}, u32[]{:S(2)}) collective-permute-start(bf16[256,384]{1,0:T(8,128)(2,1)S(1)} %add_convert_fusion.7), channel_id=1, source_target_pairs={{0,7},{1,0},{2,1},{3,2},{4,3},{5,4},{6,5},{7,6},{8,15},{9,8},{10,9... | collective-permute-start | bytes 589832 | tf_op jit(solution)/shard_map/ppermute | solution.py:388
  193.0 3.5 %collective-permute-start.18 = (bf16[256,384]{1,0:T(8,128)(2,1)S(1)}, bf16[256,384]{1,0:T(8,128)(2,1)S(1)}, u32[]{:S(2)}, u32[]{:S(2)}) collective-permute-start(bf16[256,384]{1,0:T(8,128)(2,1)S(1)} %add_convert_fusion.1), channel_id=1, source_target_pairs={{0,7},{1,0},{2,1},{3,2},{4,3},{5,4},{6,5},{7,6},{8,15},{9,8},{10,9... | collective-permute-start | bytes 589832 | tf_op jit(solution)/shard_map/ppermute | solution.py:388
  200.0 15.1 %all_to_all.26 = bf16[16,32,384]{2,1,0:T(8,128)(2,1)} all-to-all(bf16[16,32,384]{2,1,0:T(8,128)(2,1)S(1)} %bitcast.25), channel_id=1, replica_groups=mesh['chip'=16,'core'=2,'tp'=8] {'chip'}, dimensions={0} | all-to-all | bytes 786432 | tf_op jit(solution)/shard_map/all_to_all | solution.py:403
  (72 shorter events, 31.6 us)
Async XLA Ops:
  8.8 15.3 %all-to-all-start = ((bf16[32,32,128]{2,1,0:T(8,128)(2,1)}), bf16[32,32,128]{2,1,0:T(8,128)(2,1)S(1)}, u32[]{:S(2)}, u32[]{:S(2)}) async-start(bf16[32,32,128]{2,1,0:T(8,128)(2,1)} %bitcast.26), calls=%async_computation | async-start | bytes 524288 | tf_op jit(solution)/shard_map/all_to_all | solution.py:268
  26.5 11.7 %all-to-all-start.1 = ((bf16[32,16,128]{2,1,0:T(8,128)(2,1)}), bf16[32,16,128]{2,1,0:T(8,128)(2,1)S(1)}, u32[]{:S(2)}, u32[]{:S(2)}) async-start(bf16[32,16,128]{2,1,0:T(8,128)(2,1)} %shard_map.147), calls=%async_computation.1 | async-start | bytes 262144 | tf_op jit(solution)/shard_map/all_to_all | solution.py:279
  43.7 31.9 %all-to-all-start.2 = ((bf16[8,128,384]{2,1,0:T(8,128)(2,1)}), bf16[8,128,384]{2,1,0:T(8,128)(2,1)S(1)}, u32[]{:S(2)}, u32[]{:S(2)}) async-start(bf16[8,128,384]{2,1,0:T(8,128)(2,1)} %shard_map.148), calls=%async_computation.2 | async-start | bytes 1572864 | tf_op jit(solution)/shard_map/all_to_all | solution.py:294
  52.2 47.2 %copy-start.7 = (f32[3072]{0:T(1024)S(1)}, f32[3072]{0:T(1024)}, u32[]{:S(2)}) copy-start(f32[3072]{0:T(1024)} %param.24) | copy-start | bytes 36868
  52.2 84.2 %all-gather.2.cloned.1.call-start = ((), (), s32[]{:S(2)}) async-start(), calls=%async_computation.5 | async-start | bytes 6684672 | tf_op jit(solution)/shard_map/all_gather | solution.py:314
  93.9 4.6 %collective-permute-start = (f32[128,128]{1,0:T(8,128)}, f32[128,128]{1,0:T(8,128)S(1)}, u32[]{:S(2)}, u32[]{:S(2)}) collective-permute-start(f32[128,128]{1,0:T(8,128)} %get-tuple-element.32), channel_id=1, source_target_pairs={{0,1},{1,0},{2,3},{3,2},{4,5},{5,4},{6,7},{7,6},{8,9},{9,8},{10,11... | collective-permute-start | bytes 196616 | tf_op jit(solution)/shard_map/ppermute | solution.py:316
  99.3 7.7 %collective-permute-start.1 = (f32[128,128]{1,0:T(8,128)S(1)}, f32[128,128]{1,0:T(8,128)S(1)}, u32[]{:S(2)}, u32[]{:S(2)}) collective-permute-start(f32[128,128]{1,0:T(8,128)S(1)} %add.55), channel_id=1, source_target_pairs={{0,2},{1,3},{2,0},{3,1},{4,6},{5,7},{6,4},{7,5},{8,10},{9,11},{10,... | collective-permute-start | bytes 196616 | tf_op jit(solution)/shard_map/ppermute | solution.py:316
  107.1 9.6 %collective-permute-start.2 = (f32[128,128]{1,0:T(8,128)S(1)}, f32[128,128]{1,0:T(8,128)S(1)}, u32[]{:S(2)}, u32[]{:S(2)}) collective-permute-start(f32[128,128]{1,0:T(8,128)S(1)} %add.56), channel_id=1, source_target_pairs={{0,4},{1,5},{2,6},{3,7},{4,0},{5,1},{6,2},{7,3},{8,12},{9,13},{10,... | collective-permute-start | bytes 196616 | tf_op jit(solution)/shard_map/ppermute | solution.py:316
  149.3 27.2 %collective-permute-start.3 = (bf16[5,512,384]{2,1,0:T(8,128)(2,1)}, bf16[5,512,384]{2,1,0:T(8,128)(2,1)}, u32[]{:S(2)}, u32[]{:S(2)}) collective-permute-start(bf16[5,512,384]{2,1,0:T(8,128)(2,1)} %get-tuple-element.34), channel_id=1, source_target_pairs={{0,8},{8,0},{1,9},{9,1},{2,10},{10,2},{3,11},{11,3},{4,12},{12,4},... | collective-permute-start | bytes 5898248 | tf_op jit(solution)/shard_map/ppermute | solution.py:354
  149.6 8.7 %collective-permute-start.4 = (bf16[3,512,384]{2,1,0:T(8,128)(2,1)}, bf16[3,512,384]{2,1,0:T(8,128)(2,1)S(1)}, u32[]{:S(2)}, u32[]{:S(2)}) collective-permute-start(bf16[3,512,384]{2,1,0:T(8,128)(2,1)} %get-tuple-element.36), channel_id=1, source_target_pairs={{0,8},{8,0},{1,9},{9,1},{2,10},{10,2},{3,11},{11,3},{4,12},{12,4},... | collective-permute-start | bytes 3538952 | tf_op jit(solution)/shard_map/ppermute | solution.py:353
  160.8 9.0 %collective-permute-start.5 = (bf16[256,384]{1,0:T(8,128)(2,1)S(1)}, bf16[256,384]{1,0:T(8,128)(2,1)S(1)}, u32[]{:S(2)}, u32[]{:S(2)}) collective-permute-start(bf16[256,384]{1,0:T(8,128)(2,1)S(1)} %get-tuple-element.37), channel_id=1, source_target_pairs={{0,1},{1,2},{2,3},{3,4},{4,5},{5,6},{6,7},{7,0},{8,9},{9,10},{10,1... | collective-permute-start | bytes 589832 | tf_op jit(solution)/shard_map/ppermute | solution.py:388
  162.2 18.0 %collective-permute-start.9 = (bf16[256,384]{1,0:T(8,128)(2,1)S(1)}, bf16[256,384]{1,0:T(8,128)(2,1)S(1)}, u32[]{:S(2)}, u32[]{:S(2)}) collective-permute-start(bf16[256,384]{1,0:T(8,128)(2,1)S(1)} %get-tuple-element.41), channel_id=1, source_target_pairs={{0,7},{1,0},{2,1},{3,2},{4,3},{5,4},{6,5},{7,6},{8,15},{9,8},{10,9... | collective-permute-start | bytes 589832 | tf_op jit(solution)/shard_map/ppermute | solution.py:388
  164.2 19.4 %collective-permute-start.12 = (bf16[256,384]{1,0:T(8,128)(2,1)S(1)}, bf16[256,384]{1,0:T(8,128)(2,1)S(1)}, u32[]{:S(2)}, u32[]{:S(2)}) collective-permute-start(bf16[256,384]{1,0:T(8,128)(2,1)S(1)} %get-tuple-element.44), channel_id=1, source_target_pairs={{0,1},{1,2},{2,3},{3,4},{4,5},{5,6},{6,7},{7,0},{8,9},{9,10},{10,1... | collective-permute-start | bytes 589832 | tf_op jit(solution)/shard_map/ppermute | solution.py:388
  164.2 9.0 %collective-permute-start.15 = (bf16[256,384]{1,0:T(8,128)(2,1)S(1)}, bf16[256,384]{1,0:T(8,128)(2,1)S(1)}, u32[]{:S(2)}, u32[]{:S(2)}) collective-permute-start(bf16[256,384]{1,0:T(8,128)(2,1)S(1)} %get-tuple-element.47), channel_id=1, source_target_pairs={{0,7},{1,0},{2,1},{3,2},{4,3},{5,4},{6,5},{7,6},{8,15},{9,8},{10,9... | collective-permute-start | bytes 589832 | tf_op jit(solution)/shard_map/ppermute | solution.py:388
  169.9 10.1 %collective-permute-start.6 = (bf16[256,384]{1,0:T(8,128)(2,1)S(1)}, bf16[256,384]{1,0:T(8,128)(2,1)S(1)}, u32[]{:S(2)}, u32[]{:S(2)}) collective-permute-start(bf16[256,384]{1,0:T(8,128)(2,1)S(1)} %add_convert_fusion.11), channel_id=1, source_target_pairs={{0,1},{1,2},{2,3},{3,4},{4,5},{5,6},{6,7},{7,0},{8,9},{9,10},{10,1... | collective-permute-start | bytes 589832 | tf_op jit(solution)/shard_map/ppermute | solution.py:388
  173.2 10.5 %collective-permute-start.16 = (bf16[256,384]{1,0:T(8,128)(2,1)S(1)}, bf16[256,384]{1,0:T(8,128)(2,1)S(1)}, u32[]{:S(2)}, u32[]{:S(2)}) collective-permute-start(bf16[256,384]{1,0:T(8,128)(2,1)S(1)} %add_convert_fusion.3), channel_id=1, source_target_pairs={{0,7},{1,0},{2,1},{3,2},{4,3},{5,4},{6,5},{7,6},{8,15},{9,8},{10,9... | collective-permute-start | bytes 589832 | tf_op jit(solution)/shard_map/ppermute | solution.py:388
  180.1 8.3 %collective-permute-start.7 = (bf16[256,384]{1,0:T(8,128)(2,1)S(1)}, bf16[256,384]{1,0:T(8,128)(2,1)S(1)}, u32[]{:S(2)}, u32[]{:S(2)}) collective-permute-start(bf16[256,384]{1,0:T(8,128)(2,1)S(1)} %add_convert_fusion.10), channel_id=1, source_target_pairs={{0,1},{1,2},{2,3},{3,4},{4,5},{5,6},{6,7},{7,0},{8,9},{9,10},{10,1... | collective-permute-start | bytes 589832 | tf_op jit(solution)/shard_map/ppermute | solution.py:388
  180.3 8.3 %collective-permute-start.10 = (bf16[256,384]{1,0:T(8,128)(2,1)S(1)}, bf16[256,384]{1,0:T(8,128)(2,1)S(1)}, u32[]{:S(2)}, u32[]{:S(2)}) collective-permute-start(bf16[256,384]{1,0:T(8,128)(2,1)S(1)} %add_convert_fusion.8), channel_id=1, source_target_pairs={{0,7},{1,0},{2,1},{3,2},{4,3},{5,4},{6,5},{7,6},{8,15},{9,8},{10,9... | collective-permute-start | bytes 589832 | tf_op jit(solution)/shard_map/ppermute | solution.py:388
  183.6 9.1 %collective-permute-start.13 = (bf16[256,384]{1,0:T(8,128)(2,1)S(1)}, bf16[256,384]{1,0:T(8,128)(2,1)S(1)}, u32[]{:S(2)}, u32[]{:S(2)}) collective-permute-start(bf16[256,384]{1,0:T(8,128)(2,1)S(1)} %add_convert_fusion.5), channel_id=1, source_target_pairs={{0,1},{1,2},{2,3},{3,4},{4,5},{5,6},{6,7},{7,0},{8,9},{9,10},{10,1... | collective-permute-start | bytes 589832 | tf_op jit(solution)/shard_map/ppermute | solution.py:388
  183.8 9.1 %collective-permute-start.17 = (bf16[256,384]{1,0:T(8,128)(2,1)S(1)}, bf16[256,384]{1,0:T(8,128)(2,1)S(1)}, u32[]{:S(2)}, u32[]{:S(2)}) collective-permute-start(bf16[256,384]{1,0:T(8,128)(2,1)S(1)} %add_convert_fusion.2), channel_id=1, source_target_pairs={{0,7},{1,0},{2,1},{3,2},{4,3},{5,4},{6,5},{7,6},{8,15},{9,8},{10,9... | collective-permute-start | bytes 589832 | tf_op jit(solution)/shard_map/ppermute | solution.py:388
  188.5 8.7 %collective-permute-start.8 = (bf16[256,384]{1,0:T(8,128)(2,1)S(1)}, bf16[256,384]{1,0:T(8,128)(2,1)S(1)}, u32[]{:S(2)}, u32[]{:S(2)}) collective-permute-start(bf16[256,384]{1,0:T(8,128)(2,1)S(1)} %add_convert_fusion.9), channel_id=1, source_target_pairs={{0,1},{1,2},{2,3},{3,4},{4,5},{5,6},{6,7},{7,0},{8,9},{9,10},{10,1... | collective-permute-start | bytes 589832 | tf_op jit(solution)/shard_map/ppermute | solution.py:388
  188.6 8.9 %collective-permute-start.11 = (bf16[256,384]{1,0:T(8,128)(2,1)S(1)}, bf16[256,384]{1,0:T(8,128)(2,1)S(1)}, u32[]{:S(2)}, u32[]{:S(2)}) collective-permute-start(bf16[256,384]{1,0:T(8,128)(2,1)S(1)} %add_convert_fusion.7), channel_id=1, source_target_pairs={{0,7},{1,0},{2,1},{3,2},{4,3},{5,4},{6,5},{7,6},{8,15},{9,8},{10,9... | collective-permute-start | bytes 589832 | tf_op jit(solution)/shard_map/ppermute | solution.py:388
  192.8 7.0 %collective-permute-start.14 = (bf16[256,384]{1,0:T(8,128)(2,1)S(1)}, bf16[256,384]{1,0:T(8,128)(2,1)S(1)}, u32[]{:S(2)}, u32[]{:S(2)}) collective-permute-start(bf16[256,384]{1,0:T(8,128)(2,1)S(1)} %add_convert_fusion.4), channel_id=1, source_target_pairs={{0,1},{1,2},{2,3},{3,4},{4,5},{5,6},{6,7},{7,0},{8,9},{9,10},{10,1... | collective-permute-start | bytes 589832 | tf_op jit(solution)/shard_map/ppermute | solution.py:388
  193.0 6.8 %collective-permute-start.18 = (bf16[256,384]{1,0:T(8,128)(2,1)S(1)}, bf16[256,384]{1,0:T(8,128)(2,1)S(1)}, u32[]{:S(2)}, u32[]{:S(2)}) collective-permute-start(bf16[256,384]{1,0:T(8,128)(2,1)S(1)} %add_convert_fusion.1), channel_id=1, source_target_pairs={{0,7},{1,0},{2,1},{3,2},{4,3},{5,4},{6,5},{7,6},{8,15},{9,8},{10,9... | collective-permute-start | bytes 589832 | tf_op jit(solution)/shard_map/ppermute | solution.py:388
  (8 other events, 48.1 us)
Sparse Core Ops, SparseCore 0:
  94.0 42.2 all-gather.1

commit v4 on v3

--- a/solution.py
+++ b/solution.py
@@ -11,7 +11,7 @@
 exact = lax.Precision.HIGHEST
 bf16 = jnp.bfloat16
 f32 = jnp.float32
-LIMIT = 60 << 20
+LIMIT = 30 << 20
 
 
 def mm(a, b, contract_a=1, contract_b=0, precision=None):
@@ -73,24 +73,22 @@
         growth[:, lanes] = jnp.broadcast_to(jnp.exp(until[:, h:h + 1]), (positions, size))
 
 
-def project_kernel(queries, inner, growth, state, gate_input, gain, weight, out, normed, *, heads):
+def project_kernel(queries, inner, growth, state, gate_input, gain, weight, out, *, heads):
     size = queries.shape[1] // heads
-
-    @pl.when(pl.program_id(0) == 0)
-    def _():
-        for h in range(heads):
-            lanes = slice(h * size, (h + 1) * size)
-            carried = mm(queries[:, lanes], state[lanes, :])
-            attended = inner[:, lanes] + growth[:, lanes] * carried
-            squares = jnp.mean(attended * attended, axis=1, keepdims=True)
-            gating = jax.nn.sigmoid(gate_input[:, lanes].astype(f32))
-            rows = attended * lax.rsqrt(squares + epsilon) * gain[:, lanes] * gating
-            normed[:, lanes] = rows.astype(bf16)
-
-    product = mm(normed[...], weight[...])
-    for c in range(out.shape[0]):
-        width = out.shape[2]
-        out[c] = product[:, c * width:(c + 1) * width].astype(bf16)
+    normed = []
+    for h in range(heads):
+        lanes = slice(h * size, (h + 1) * size)
+        carried = mm(queries[:, lanes], state[lanes, :])
+        attended = inner[:, lanes] + growth[:, lanes] * carried
+        squares = jnp.mean(attended * attended, axis=1, keepdims=True)
+        gating = jax.nn.sigmoid(gate_input[:, lanes].astype(f32))
+        normed.append((attended * lax.rsqrt(squares + epsilon) * gain[:, lanes] * gating).astype(bf16))
+    normed = jnp.concatenate(normed, axis=1)
+    width = out.shape[2]
+    for c in range(0, out.shape[0], 2):
+        product = mm(normed, weight[:, c * width:(c + 2) * width])
+        out[c] = product[:, :width].astype(bf16)
+        out[c + 1] = product[:, width:].astype(bf16)
 
 
 def slots_of(ids, experts, capacity):
@@ -133,13 +131,27 @@
     return copies
 
 
-def column_pairs(tp, hbm, scratch, distances, peers):
-    share = hbm.shape[1] // peers
+def load_kernel(source, target, sems):
+    parts = sems.shape[0]
+    rows = source.shape[0] // parts
+    pairs = [(source.at[pl.ds(k * rows, rows)], target.at[pl.ds(k * rows, rows)]) for k in range(parts)]
+    for copy in fetch(pairs, sems):
+        copy.wait()
+
+
+def load_experts_kernel(place, gate_hbm, up_hbm, down_hbm, gate_up, down, sems, *, distances, peers):
+    share = down_hbm.shape[1] // peers
+    rows = gate_hbm.shape[0] // 4
     pairs = []
+    for k in range(4):
+        part = pl.ds(k * rows, rows)
+        pairs.append((gate_hbm.at[part], gate_up.at[part, pl.ds(0, share)]))
+        pairs.append((up_hbm.at[part], gate_up.at[part, pl.ds(share, share)]))
     for k, distance in enumerate(distances):
-        start = pl.multiple_of(lax.rem(tp + distance + peers, peers) * share, share)
-        pairs.append((hbm.at[:, pl.ds(start, share)], scratch.at[:, pl.ds(k * share, share)]))
-    return pairs
+        start = pl.multiple_of(lax.rem(place[1] + distance + peers, peers) * share, share)
+        pairs.append((down_hbm.at[:, pl.ds(start, share)], down.at[:, pl.ds(k * share, share)]))
+    for copy in fetch(pairs, sems):
+        copy.wait()
 
 
 def activate(rows, inverse, gate_up, width):
@@ -157,63 +169,42 @@
     return (gated * jax.nn.sigmoid(gated) * total[:, share:]).astype(bf16)
 
 
-def products(activated, down, chunks):
-    share = down.shape[1] // chunks
+def products(activated, down, chunks, share):
     found = []
-    for c in range(0, chunks, 2):
-        both = min(2, chunks - c)
-        product = mm(activated, down[:, c * share:(c + both) * share])
+    chunks = list(chunks)
+    while chunks:
+        both = min(2, len(chunks))
+        product = mm(activated, down[:, chunks[0] * share:(chunks[0] + both) * share])
         found += [product[:, k * share:(k + 1) * share] for k in range(both)]
+        chunks = chunks[both:]
     return found
 
 
-def other_half_kernel(
-    place, rows, inverse, gate_hbm, up_hbm, down_hbm, first, rest, gate_up, down, sems, *, width, distances
-):
+def other_half_kernel(place, rows, inverse, gate_up, down, first, rest, *, width):
+    del place
     chunks, _, share = rows.shape
-    near = len(distances) - rest.shape[0]
-    pairs = [(gate_hbm, gate_up.at[:, pl.ds(0, share)]), (up_hbm, gate_up.at[:, pl.ds(share, share)])]
-    pairs += column_pairs(place[1], down_hbm, down, distances, chunks)
-
-    @pl.when(pl.program_id(0) == 0)
-    def _():
-        copies = fetch(pairs, sems)
-        for copy in copies:
-            copy.wait()
-
-    for k, product in enumerate(products(activate(rows, inverse, gate_up, width), down, chunks)):
-        if k < near:
+    far = chunks - rest.shape[0]
+    activated = activate(rows, inverse, gate_up, width)
+    for k, product in enumerate(products(activated, down, range(chunks), share)):
+        if k < far:
             first[k] = product.astype(bf16)
         else:
-            rest[k - near] = product.astype(bf16)
-
-
-def own_half_kernel(place, rows, inverse, gate_hbm, up_hbm, out, gate_up, sems, *, width):
+            rest[k - far] = product.astype(bf16)
+
+
+def own_half_kernel(place, rows, inverse, gate_up, out, *, width):
     del place
-    share = rows.shape[2]
-
-    @pl.when(pl.program_id(0) == 0)
-    def _():
-        copies = fetch([(gate_hbm, gate_up.at[:, pl.ds(0, share)]), (up_hbm, gate_up.at[:, pl.ds(share, share)])], sems)
-        for copy in copies:
-            copy.wait()
-
     out[...] = activate(rows, inverse, gate_up, width)
 
 
-def own_products_kernel(place, activated, sibling, down_hbm, *rest, distances, peers, split):
-    outs, (down, sems) = rest[:-2], rest[-2:]
-    copies = fetch(column_pairs(place[1], down_hbm, down, distances, peers), sems)
-    for copy in copies:
-        copy.wait()
+def own_products_kernel(activated, sibling, down, *outs, start, split):
+    count, _, share = sibling.shape
     half = activated.shape[0] // 2
     for h in range(2):
         rows = slice(h * half, (h + 1) * half)
-        for k, product in enumerate(products(activated[rows, :], down, len(distances))):
+        for k, product in enumerate(products(activated[rows, :], down, range(start, start + count), share)):
             total = (product + sibling[k, rows, :].astype(f32)).astype(bf16)
-            if split:
-                outs[2 * k + h][...] = total
-            elif k < len(distances) - 1:
+            if split or k < count - 1:
                 outs[2 * k + h][...] = total
             else:
                 outs[-1][rows, :] = total
@@ -239,6 +230,14 @@
         compiler_params=pltpu.CompilerParams(vmem_limit_bytes=LIMIT),
         **kwargs,
     )(*args)
+
+
+def stays(x):
+    return pltpu.with_memory_space_constraint(x, pltpu.HBM)
+
+
+def in_vmem(x):
+    return pltpu.with_memory_space_constraint(x, pltpu.VMEM)
 
 
 def whole(shape):
@@ -263,8 +262,22 @@
     cx = lax.axis_index("chip") * cores + core
     tp = lax.axis_index("tp")
 
+    queries, keys, values, log_decay = stays(queries), stays(keys), stays(values), stays(log_decay)
+    vmem = pl.BlockSpec(memory_space=pltpu.VMEM)
+    hbm = pl.BlockSpec(memory_space=pl.ANY)
+
     rows = heads * size // blocks
     parts = call(block_state_kernel, struct((heads, size // rows, 2 * rows, size), bf16), keys, values, log_decay)
+    parts, out_weight = lax.optimization_barrier((parts, out_weight))
+    out_weight = pl.pallas_call(
+        load_kernel,
+        out_shape=pltpu.VMEM((head_lanes, width), bf16),
+        in_specs=[hbm],
+        out_specs=vmem,
+        scratch_shapes=[pltpu.SemaphoreType.DMA((4,))],
+        compiler_params=pltpu.CompilerParams(vmem_limit_bytes=4 << 20),
+        cost_estimate=pl.CostEstimate(flops=0, bytes_accessed=2 * head_lanes * width, transcendentals=0),
+    )(stays(out_weight))
     received = lax.all_to_all(parts.reshape(blocks, 2 * rows, size), ("chip", "core"), 0, 0, tiled=True)
     inner, growth = call(
         inner_kernel,
@@ -273,23 +286,16 @@
     )
     befores = call(
         state_scan_kernel, struct((blocks, rows, size), bf16),
-        cx.reshape(1), received, prior_state.reshape(heads * size, size),
+        cx.reshape(1), received, stays(prior_state.reshape(heads * size, size)),
         in_specs=[pl.BlockSpec(memory_space=pltpu.SMEM)] + [pl.BlockSpec(memory_space=pltpu.VMEM)] * 2,
     )
     state = lax.all_to_all(befores, ("chip", "core"), 0, 0, tiled=True).reshape(heads * size, size)
 
-    steps = 4
-    each = peers // steps
     partial = call(
         functools.partial(project_kernel, heads=heads),
         struct((peers, positions, share), bf16),
-        queries, inner, growth, state, gate_input, attn_gain.reshape(1, head_lanes), out_weight,
-        grid=(steps,),
-        in_specs=[whole((positions, head_lanes))] * 3
-        + [whole((heads * size, size)), whole((positions, head_lanes)), whole((1, head_lanes))]
-        + [pl.BlockSpec((head_lanes, each * share), lambda i: (0, i))],
-        out_specs=pl.BlockSpec((each, positions, share), lambda i: (i, 0, 0)),
-        scratch_shapes=[pltpu.VMEM((positions, head_lanes), bf16)],
+        queries, inner, growth, state, stays(gate_input), stays(attn_gain.reshape(1, head_lanes)), in_vmem(out_weight),
+        in_specs=[vmem] * 7,
     )
     partial = lax.all_to_all(partial, "tp", 0, 0, tiled=True)
     outgoing, hidden, sums = pl.pallas_call(
@@ -308,47 +314,51 @@
             out_specs=[whole((slots, share)), whole((positions, share)), whole((positions, 128))],
         ),
         compiler_params=pltpu.CompilerParams(vmem_limit_bytes=LIMIT),
-    )(tp.reshape(1), partial, layer_input, moe_gain.reshape(peers, 1, share), router, expert_ids)
+    )(tp.reshape(1), partial, stays(layer_input), stays(moe_gain.reshape(peers, 1, share)), router, expert_ids)
 
     arrived = lax.all_to_all(outgoing.reshape(chips, capacity, share), "chip", 0, 0, tiled=True)
+    arrived, gate, up, down = lax.optimization_barrier((arrived, w_gate[0], w_up[0], w_down[0]))
     gathered = lax.all_gather(arrived.reshape(chips * capacity, share), ("core", "tp"))
+    far, near = (4, 3, -3), (2, -2, 1, -1, 0)
+    place = jnp.stack([core, tp])
+    gate_up, down = pl.pallas_call(
+        functools.partial(load_experts_kernel, distances=far + near, peers=peers),
+        out_shape=(pltpu.VMEM((width, 2 * share), bf16), pltpu.VMEM((share, width), bf16)),
+        in_specs=[pl.BlockSpec(memory_space=pltpu.SMEM), hbm, hbm, hbm],
+        out_specs=(vmem, vmem),
+        scratch_shapes=[pltpu.SemaphoreType.DMA((8 + peers,))],
+        compiler_params=pltpu.CompilerParams(vmem_limit_bytes=4 << 20),
+        cost_estimate=pl.CostEstimate(flops=0, bytes_accessed=6 * width * share, transcendentals=0),
+    )(place, stays(gate), stays(up), stays(down))
+    gate_up, down = in_vmem(gate_up), in_vmem(down)
     for distance in (1, 2, 4):
         sums += lax.ppermute(sums, "tp", [(i, i ^ distance) for i in range(peers)])
     gathered, sums = lax.optimization_barrier((gathered, sums))
-    gathered = gathered.reshape(cores * peers, chips * capacity, share)
+    gathered = stays(gathered.reshape(cores * peers, chips * capacity, share))
     held = chips * capacity
     rows_step = 256
     per_half = held // rows_step
     half = held // 2
-    far, near = (4, 3, -3), (2, -2, 1, -1, 0)
-    place = jnp.stack([core, tp])
     inverse = (1.0 / moe_gain).reshape(1, width)
     params = pltpu.CompilerParams(vmem_limit_bytes=LIMIT)
-    hbm = pl.BlockSpec(memory_space=pl.ANY)
-    gate, up, down = w_gate[0], w_up[0], w_down[0]
     work = 2 * held * width * share
     block = (peers, rows_step, share)
 
     first, rest = pl.pallas_call(
-        functools.partial(other_half_kernel, width=width, distances=far + near),
+        functools.partial(other_half_kernel, width=width),
         out_shape=(struct((len(far), held, share), bf16), struct((len(near), held, share), bf16)),
         grid_spec=pltpu.PrefetchScalarGridSpec(
             num_scalar_prefetch=1,
             grid=(per_half,),
-            in_specs=[pl.BlockSpec(block, lambda i, place: (1 - place[0], i, 0)), whole((1, width)), hbm, hbm, hbm],
+            in_specs=[pl.BlockSpec(block, lambda i, place: (1 - place[0], i, 0)), whole((1, width)), vmem, vmem],
             out_specs=[
                 pl.BlockSpec((len(far), rows_step, share), lambda i, place: (0, i, 0)),
                 pl.BlockSpec((len(near), rows_step, share), lambda i, place: (0, i, 0)),
             ],
-            scratch_shapes=[
-                pltpu.VMEM((width, 2 * share), bf16),
-                pltpu.VMEM((share, width), bf16),
-                pltpu.SemaphoreType.DMA((2 + peers,)),
-            ],
         ),
         compiler_params=params,
-        cost_estimate=pl.CostEstimate(flops=3 * work, bytes_accessed=14 << 20, transcendentals=held * share),
-    )(place, gathered, inverse, gate, up, down)
+        cost_estimate=pl.CostEstimate(flops=3 * work, bytes_accessed=7 << 20, transcendentals=held * share),
+    )(place, gathered, inverse, gate_up, down)
     swap = [(0, 1), (1, 0)]
     first = lax.ppermute(first, "core", swap)
     rest = lax.ppermute(rest, "core", swap)
@@ -358,31 +368,24 @@
         grid_spec=pltpu.PrefetchScalarGridSpec(
             num_scalar_prefetch=1,
             grid=(per_half,),
-            in_specs=[pl.BlockSpec(block, lambda i, place: (place[0], i, 0)), whole((1, width)), hbm, hbm],
+            in_specs=[pl.BlockSpec(block, lambda i, place: (place[0], i, 0)), whole((1, width)), vmem],
             out_specs=pl.BlockSpec((rows_step, share), lambda i, place: (i, 0)),
-            scratch_shapes=[pltpu.VMEM((width, 2 * share), bf16), pltpu.SemaphoreType.DMA((2,))],
         ),
         compiler_params=params,
-        cost_estimate=pl.CostEstimate(flops=2 * work, bytes_accessed=8 << 20, transcendentals=held * share),
-    )(place, gathered, inverse, gate, up)
-
-    def own_products(sibling, distances, split):
-        n = len(distances)
+        cost_estimate=pl.CostEstimate(flops=2 * work, bytes_accessed=4 << 20, transcendentals=held * share),
+    )(place, gathered, inverse, gate_up)
+
+    def own_products(sibling, start, split):
+        n = sibling.shape[0]
         piece = struct((half, share), bf16)
         shapes = (piece,) * (2 * n) if split else (piece,) * (2 * n - 2) + (struct((held, share), bf16),)
         return pl.pallas_call(
-            functools.partial(own_products_kernel, distances=distances, peers=peers, split=split),
+            functools.partial(own_products_kernel, start=start, split=split),
             out_shape=shapes,
-            grid_spec=pltpu.PrefetchScalarGridSpec(
-                num_scalar_prefetch=1,
-                grid=(1,),
-                in_specs=[whole((held, share)), whole((n, held, share)), hbm],
-                out_specs=[whole(s.shape) for s in shapes],
-                scratch_shapes=[pltpu.VMEM((share, n * share), bf16), pltpu.SemaphoreType.DMA((n,))],
-            ),
-            compiler_params=pltpu.CompilerParams(vmem_limit_bytes=24 << 20),
-            cost_estimate=pl.CostEstimate(flops=n * work // peers, bytes_accessed=3 * n * held * share * 2, transcendentals=0),
-        )(place, activated, sibling, down)
+            in_specs=[vmem] * 3,
+            compiler_params=params,
+            cost_estimate=pl.CostEstimate(flops=n * work // peers, bytes_accessed=2 * n * held * share * 2, transcendentals=0),
+        )(activated, sibling, down)
 
     def moved(piece, step):
         return lax.ppermute(piece, "tp", [(i, (i + step) % peers) for i in range(peers)])
@@ -390,10 +393,10 @@
     def plus(*pieces):
         return sum(piece.astype(f32) for piece in pieces).astype(bf16)
 
-    a4, b4, a3, b3, a3m, b3m = own_products(first, far, True)
+    a4, b4, a3, b3, a3m, b3m = own_products(first, 0, True)
     a_up, b_down = moved(a4, 1), moved(b4, -1)
     a_down, b_up = moved(a3m, -1), moved(b3, 1)
-    a2, b2, a2m, b2m, a1, b1, a1m, b1m, mine = own_products(rest, near, False)
+    a2, b2, a2m, b2m, a1, b1, a1m, b1m, mine = own_products(rest, len(far), False)
     a_up, b_down = moved(plus(a_up, a3), 1), moved(plus(b_down, b3m), -1)
     a_down, b_up = moved(plus(a_down, a2m), -1), moved(plus(b_up, b2), 1)
     a_up, b_down = moved(plus(a_up, a2), 1), moved(plus(b_down, b2m), -1)

time: 225 us -> 209 us (0.929)
  Pallas kernels: 43 us -> 31.9 us
  waiting for transfers between devices: 83.3 us -> 78.6 us
  local copies, waits for them, and re-layouts: 5.16 us -> 8.48 us
  other arithmetic: 3.42 us -> 0.82 us
    pallas_call x5, Pallas kernels: 13.9 us -> 8.91 us  [call(): pl.pallas_call(kernel, out_shape=shapes, compiler_params=pltpu.CompilerPa...]
    all_gather x1, waiting for transfers between devices: 19 us -> 14.7 us  [shards(): lax.all_gather(arrived.reshape(chips * capacity, share), ('core', 'tp'))]
    pallas_call x1, Pallas kernels: 8.41 us -> 4.97 us  [shards(): pl.pallas_call(functools.partial(own_half_kernel, width=width), out_shape...]
    unnamed x20 -> x16, local copies, waits for them, and re-layouts: 5.16 us -> 8.48 us
    pallas_call x3 -> x5, Pallas kernels: 18 us -> 16.4 us  [the longest x1 8.68 us: shards(): pl.pallas_call(functools.partial(other_half_kernel, width=width), out_sha...]
  transfers between devices with their start and end apart: 23 -> 23, of which waited for: 14 -> 15; matrix products, arithmetic and copies ran while one was open for 2% -> 1% of each run, Pallas kernels for 7% -> 7%
where the time goes in v4:
time: 209 us; the launch traced here: 208 us
  waiting for transfers between devices  78.6 us (38%)
  starting transfers between devices  46.1 us (22%)
  Pallas kernels  31.9 us (15%)
  blocking collectives  28.9 us (14%)
  between operations  13.7 us (7%)
  local copies, waits for them, and re-layouts  8.48 us (4%)
    ppermute x14, starting transfers between devices, moved(): lax.ppermute(piece, 'tp', [(i, (i + step) % peers) for i in range(peers)])  24.1 us
    all_to_all x1, waiting for transfers between devices, shards(): partial = lax.all_to_all(partial, 'tp', 0, 0, tiled=True)  22 us
    ppermute x3, waiting for transfers between devices, shards(): sums += lax.ppermute(sums, 'tp', [(i, i ^ distance) for i in range(peers)])  21.1 us
    all_to_all x1, blocking collectives, shards(): lax.all_to_all(summed.reshape(chips, capacity, share), 'chip', 0, 0, tile...  14.9 us
    all_gather x1, waiting for transfers between devices, shards(): lax.all_gather(arrived.reshape(chips * capacity, share), ('core', 'tp'))  14.7 us
    all_to_all x1, blocking collectives, shards(): lax.all_to_all(outgoing.reshape(chips, capacity, share), 'chip', 0, 0, ti...  14 us
    ppermute x14, waiting for transfers between devices, moved(): lax.ppermute(piece, 'tp', [(i, (i + step) % peers) for i in range(peers)])  10.8 us
    pallas_call x5, Pallas kernels, call(): pl.pallas_call(kernel, out_shape=shapes, compiler_params=pltpu.CompilerPa...  8.91 us
  transfers between devices with their start and end apart: 23, of which 15 were waited for; matrix products, arithmetic and copies ran while one was open for 1% of the time, Pallas kernels for 7%

profile of v4, /device:TPU:2, one launch (start us, length us, event | category | flops | bytes accessed | tf_op | source)
XLA Modules:
  0.0 208.5 jit_solution(18328008767071167985)
XLA Ops:
  8.8 7.6 %all-to-all-start = ((bf16[32,32,128]{2,1,0:T(8,128)(2,1)}), bf16[32,32,128]{2,1,0:T(8,128)(2,1)S(1)}, u32[]{:S(2)}, u32[]{:S(2)}) async-start(bf16[32,32,128]{2,1,0:T(8,128)(2,1)} %bitcast.3), calls=%async_computation | async-start | bytes 524288 | tf_op jit(solution)/shard_map/all_to_all | solution.py:281
  16.4 7.7 %all-to-all-done.received = bf16[32,32,128]{2,1,0:T(8,128)(2,1)S(1)} async-done(((bf16[32,32,128]{2,1,0:T(8,128)(2,1)}), bf16[32,32,128]{2,1,0:T(8,128)(2,1)S(1)}, u32[]{:S(2)}, u32[]{:S(2)}) %all-to-all-start) | async-done | bytes 262176 | tf_op jit(solution)/shard_map/all_to_all | solution.py:281
  25.8 5.0 %all-to-all-start.1 = ((bf16[32,16,128]{2,1,0:T(8,128)(2,1)}), bf16[32,16,128]{2,1,0:T(8,128)(2,1)S(1)}, u32[]{:S(2)}, u32[]{:S(2)}) async-start(bf16[32,16,128]{2,1,0:T(8,128)(2,1)} %shard_map.147), calls=%async_computation.1 | async-start | bytes 262144 | tf_op jit(solution)/shard_map/all_to_all | solution.py:292
  41.1 8.5 %all-to-all-start.2 = ((bf16[8,128,384]{2,1,0:T(8,128)(2,1)}), bf16[8,128,384]{2,1,0:T(8,128)(2,1)S(1)}, u32[]{:S(2)}, u32[]{:S(2)}) async-start(bf16[8,128,384]{2,1,0:T(8,128)(2,1)} %copy-done.2), calls=%async_computation.2 | async-start | bytes 1572864 | tf_op jit(solution)/shard_map/all_to_all | solution.py:300
  51.0 22.0 %all-to-all-done.2.partial = bf16[8,128,384]{2,1,0:T(8,128)(2,1)S(1)} async-done(((bf16[8,128,384]{2,1,0:T(8,128)(2,1)}), bf16[8,128,384]{2,1,0:T(8,128)(2,1)S(1)}, u32[]{:S(2)}, u32[]{:S(2)}) %all-to-all-start.2) | async-done | bytes 786464 | tf_op jit(solution)/shard_map/all_to_all | solution.py:300
  74.6 14.0 %all_to_all.25 = bf16[16,32,384]{2,1,0:T(8,128)(2,1)} all-to-all(bf16[16,32,384]{2,1,0:T(8,128)(2,1)S(1)} %bitcast.18), channel_id=1, replica_groups=mesh['chip'=16,'core'=2,'tp'=8] {'chip'}, dimensions={0} | all-to-all | bytes 786432 | tf_op jit(solution)/shard_map/all_to_all | solution.py:319
  88.7 4.3 %collective-permute-done = f32[128,128]{1,0:T(8,128)S(1)} collective-permute-done((f32[128,128]{1,0:T(8,128)S(1)}, f32[128,128]{1,0:T(8,128)S(1)}, u32[]{:S(2)}, u32[]{:S(2)}) %collective-permute-start) | collective-permute-done | bytes 65568 | tf_op jit(solution)/shard_map/ppermute | solution.py:335
  93.1 7.3 %collective-permute-done.1 = f32[128,128]{1,0:T(8,128)S(1)} collective-permute-done((f32[128,128]{1,0:T(8,128)S(1)}, f32[128,128]{1,0:T(8,128)S(1)}, u32[]{:S(2)}, u32[]{:S(2)}) %collective-permute-start.1) | collective-permute-done | bytes 65568 | tf_op jit(solution)/shard_map/ppermute | solution.py:335
  100.6 9.5 %collective-permute-done.2 = f32[128,128]{1,0:T(8,128)S(1)} collective-permute-done((f32[128,128]{1,0:T(8,128)S(1)}, f32[128,128]{1,0:T(8,128)S(1)}, u32[]{:S(2)}, u32[]{:S(2)}) %collective-permute-start.2) | collective-permute-done | bytes 65568 | tf_op jit(solution)/shard_map/ppermute | solution.py:335
  110.1 3.8 %shard_map.151 = (bf16[3072,768]{1,0:T(8,128)(2,1)S(1)}, bf16[384,3072]{1,0:T(8,128)(2,1)S(1)}) custom-call(s32[2]{0:T(128)S(1)} %pad_add_fusion.place, bf16[3072,384]{1,0:T(8,128)(2,1)} %bitcast.21, bf16[3072,384]{1,0:T(8,128)(2,1)} %bitcast.22, bf16[384,3072]{1,0:T(8,128)(2,1)} %bitcast.23), custom_call_target="tpu_custom_call" | custom-call | bytes 7077888 | tf_op jit(solution)/shard_map/pallas_call | solution.py:324
  116.2 14.7 %all-gather.2.cloned.1.call-done.rows = bf16[16,512,384]{2,1,0:T(8,128)(2,1)} async-done(((bf16[1,512,384]{2,1,0:T(8,128)(2,1)}), bf16[16,512,384]{2,1,0:T(8,128)(2,1)}) %all-gather.2.cloned.1.call-update) | async-done | bytes 6291472 | tf_op jit(solution)/shard_map/all_gather | solution.py:321
  130.9 2.3 %copy-done.1 = bf16[3072,768]{1,0:T(8,128)(2,1)S(1)} copy-done((bf16[3072,768]{1,0:T(8,128)(2,1)S(1)}, bf16[3072,768]{1,0:T(8,128)(2,1)}, u32[]{:S(2)}) %copy-start.1) | copy-done | bytes 4718616
  133.3 8.7 %shard_map.153 = (bf16[3,512,384]{2,1,0:T(8,128)(2,1)S(1)}, bf16[5,512,384]{2,1,0:T(8,128)(2,1)S(1)}) custom-call(s32[2]{0:T(128)S(1)} %pad_add_fusion.place, bf16[16,512,384]{2,1,0:T(8,128)(2,1)} %all-gather.2.cloned.1.call-done.rows, f32[1,3072]{1,0:T(1,128)S(1)} %bitcast.19, bf16[3072,768]{1,0:T(8,128)(2,1)S(1)} %copy-done.1, ...), custom_call_target="tpu_custom_call" | custom-call | flops 3623878656 | bytes 7340032 | tf_op jit(solution)/shard_map/pallas_call | solution.py:347
  142.5 5.0 %shard_map.152.activated = bf16[512,384]{1,0:T(8,128)(2,1)S(1)} custom-call(s32[2]{0:T(128)S(1)} %pad_add_fusion.place, bf16[16,512,384]{2,1,0:T(8,128)(2,1)} %all-gather.2.cloned.1.call-done.rows, f32[1,3072]{1,0:T(1,128)S(1)} %bitcast.20, bf16[3072,768]{1,0:T(8,128)(2,1)S(1)} %copy-done.1), custom_call_target="tpu_custom_call" | custom-call | flops 2415919104 | bytes 4194304 | tf_op jit(solution)/shard_map/pallas_call | solution.py:365
  152.0 3.2 %collective-permute-start.15 = (bf16[256,384]{1,0:T(8,128)(2,1)S(1)}, bf16[256,384]{1,0:T(8,128)(2,1)S(1)}, u32[]{:S(2)}, u32[]{:S(2)}) collective-permute-start(bf16[256,384]{1,0:T(8,128)(2,1)S(1)} %get-tuple-element.63), channel_id=1, source_target_pairs={{0,7},{1,0},{2,1},{3,2},{4,3},{5,4},{6,5},{7,6},{8,15},{9,8},{10,9... | collective-permute-start | bytes 589832 | tf_op jit(solution)/shard_map/ppermute | solution.py:391
  155.3 2.5 %collective-permute-done.5 = bf16[256,384]{1,0:T(8,128)(2,1)S(1)} collective-permute-done((bf16[256,384]{1,0:T(8,128)(2,1)S(1)}, bf16[256,384]{1,0:T(8,128)(2,1)S(1)}, u32[]{:S(2)}, u32[]{:S(2)}) %collective-permute-start.5) | collective-permute-done | bytes 196640 | tf_op jit(solution)/shard_map/ppermute | solution.py:391
  157.9 3.1 %collective-permute-done.15 = bf16[256,384]{1,0:T(8,128)(2,1)S(1)} collective-permute-done((bf16[256,384]{1,0:T(8,128)(2,1)S(1)}, bf16[256,384]{1,0:T(8,128)(2,1)S(1)}, u32[]{:S(2)}, u32[]{:S(2)}) %collective-permute-start.15) | collective-permute-done | bytes 196640 | tf_op jit(solution)/shard_map/ppermute | solution.py:391
  161.0 3.3 %collective-permute-start.16 = (bf16[256,384]{1,0:T(8,128)(2,1)S(1)}, bf16[256,384]{1,0:T(8,128)(2,1)S(1)}, u32[]{:S(2)}, u32[]{:S(2)}) collective-permute-start(bf16[256,384]{1,0:T(8,128)(2,1)S(1)} %add_convert_fusion.3), channel_id=1, source_target_pairs={{0,7},{1,0},{2,1},{3,2},{4,3},{5,4},{6,5},{7,6},{8,15},{9,8},{10,9... | collective-permute-start | bytes 589832 | tf_op jit(solution)/shard_map/ppermute | solution.py:391
  165.8 3.3 %collective-permute-start.10 = (bf16[256,384]{1,0:T(8,128)(2,1)S(1)}, bf16[256,384]{1,0:T(8,128)(2,1)S(1)}, u32[]{:S(2)}, u32[]{:S(2)}) collective-permute-start(bf16[256,384]{1,0:T(8,128)(2,1)S(1)} %add_convert_fusion.8), channel_id=1, source_target_pairs={{0,7},{1,0},{2,1},{3,2},{4,3},{5,4},{6,5},{7,6},{8,15},{9,8},{10,9... | collective-permute-start | bytes 589832 | tf_op jit(solution)/shard_map/ppermute | solution.py:391
  169.3 3.3 %collective-permute-start.17 = (bf16[256,384]{1,0:T(8,128)(2,1)S(1)}, bf16[256,384]{1,0:T(8,128)(2,1)S(1)}, u32[]{:S(2)}, u32[]{:S(2)}) collective-permute-start(bf16[256,384]{1,0:T(8,128)(2,1)S(1)} %add_convert_fusion.2), channel_id=1, source_target_pairs={{0,7},{1,0},{2,1},{3,2},{4,3},{5,4},{6,5},{7,6},{8,15},{9,8},{10,9... | collective-permute-start | bytes 589832 | tf_op jit(solution)/shard_map/ppermute | solution.py:391
  174.1 3.6 %collective-permute-start.11 = (bf16[256,384]{1,0:T(8,128)(2,1)S(1)}, bf16[256,384]{1,0:T(8,128)(2,1)S(1)}, u32[]{:S(2)}, u32[]{:S(2)}) collective-permute-start(bf16[256,384]{1,0:T(8,128)(2,1)S(1)} %add_convert_fusion.7), channel_id=1, source_target_pairs={{0,7},{1,0},{2,1},{3,2},{4,3},{5,4},{6,5},{7,6},{8,15},{9,8},{10,9... | collective-permute-start | bytes 589832 | tf_op jit(solution)/shard_map/ppermute | solution.py:391
  178.5 3.5 %collective-permute-start.18 = (bf16[256,384]{1,0:T(8,128)(2,1)S(1)}, bf16[256,384]{1,0:T(8,128)(2,1)S(1)}, u32[]{:S(2)}, u32[]{:S(2)}) collective-permute-start(bf16[256,384]{1,0:T(8,128)(2,1)S(1)} %add_convert_fusion.1), channel_id=1, source_target_pairs={{0,7},{1,0},{2,1},{3,2},{4,3},{5,4},{6,5},{7,6},{8,15},{9,8},{10,9... | collective-permute-start | bytes 589832 | tf_op jit(solution)/shard_map/ppermute | solution.py:391
  183.0 2.3 %collective-permute-done.14 = bf16[256,384]{1,0:T(8,128)(2,1)S(1)} collective-permute-done((bf16[256,384]{1,0:T(8,128)(2,1)S(1)}, bf16[256,384]{1,0:T(8,128)(2,1)S(1)}, u32[]{:S(2)}, u32[]{:S(2)}) %collective-permute-start.14) | collective-permute-done | bytes 196640 | tf_op jit(solution)/shard_map/ppermute | solution.py:391
  185.5 14.9 %all_to_all.26 = bf16[16,32,384]{2,1,0:T(8,128)(2,1)S(1)} all-to-all(bf16[16,32,384]{2,1,0:T(8,128)(2,1)S(1)} %bitcast.25), channel_id=1, replica_groups=mesh['chip'=16,'core'=2,'tp'=8] {'chip'}, dimensions={0} | all-to-all | bytes 786432 | tf_op jit(solution)/shard_map/all_to_all | solution.py:406
  (70 shorter events, 31.4 us)
Async XLA Ops:
  8.8 15.3 %all-to-all-start = ((bf16[32,32,128]{2,1,0:T(8,128)(2,1)}), bf16[32,32,128]{2,1,0:T(8,128)(2,1)S(1)}, u32[]{:S(2)}, u32[]{:S(2)}) async-start(bf16[32,32,128]{2,1,0:T(8,128)(2,1)} %bitcast.3), calls=%async_computation | async-start | bytes 524288 | tf_op jit(solution)/shard_map/all_to_all | solution.py:281
  25.8 11.7 %all-to-all-start.1 = ((bf16[32,16,128]{2,1,0:T(8,128)(2,1)}), bf16[32,16,128]{2,1,0:T(8,128)(2,1)S(1)}, u32[]{:S(2)}, u32[]{:S(2)}) async-start(bf16[32,16,128]{2,1,0:T(8,128)(2,1)} %shard_map.147), calls=%async_computation.1 | async-start | bytes 262144 | tf_op jit(solution)/shard_map/all_to_all | solution.py:292
  41.1 31.9 %all-to-all-start.2 = ((bf16[8,128,384]{2,1,0:T(8,128)(2,1)}), bf16[8,128,384]{2,1,0:T(8,128)(2,1)S(1)}, u32[]{:S(2)}, u32[]{:S(2)}) async-start(bf16[8,128,384]{2,1,0:T(8,128)(2,1)} %copy-done.2), calls=%async_computation.2 | async-start | bytes 1572864 | tf_op jit(solution)/shard_map/all_to_all | solution.py:300
  49.6 43.5 %copy-start.5 = (f32[3072]{0:T(1024)S(1)}, f32[3072]{0:T(1024)}, u32[]{:S(2)}) copy-start(f32[3072]{0:T(1024)} %param.24) | copy-start | bytes 36868
  49.6 81.4 %all-gather.2.cloned.1.call-start = ((), (), s32[]{:S(2)}) async-start(), calls=%async_computation.5 | async-start | bytes 6684672 | tf_op jit(solution)/shard_map/all_gather | solution.py:321
  88.6 4.4 %collective-permute-start = (f32[128,128]{1,0:T(8,128)S(1)}, f32[128,128]{1,0:T(8,128)S(1)}, u32[]{:S(2)}, u32[]{:S(2)}) collective-permute-start(f32[128,128]{1,0:T(8,128)S(1)} %get-tuple-element.43), channel_id=1, source_target_pairs={{0,1},{1,0},{2,3},{3,2},{4,5},{5,4},{6,7},{7,6},{8,9},{9,8},{10,11... | collective-permute-start | bytes 196616 | tf_op jit(solution)/shard_map/ppermute | solution.py:335
  93.0 7.4 %collective-permute-start.1 = (f32[128,128]{1,0:T(8,128)S(1)}, f32[128,128]{1,0:T(8,128)S(1)}, u32[]{:S(2)}, u32[]{:S(2)}) collective-permute-start(f32[128,128]{1,0:T(8,128)S(1)} %add.55), channel_id=1, source_target_pairs={{0,2},{1,3},{2,0},{3,1},{4,6},{5,7},{6,4},{7,5},{8,10},{9,11},{10,... | collective-permute-start | bytes 196616 | tf_op jit(solution)/shard_map/ppermute | solution.py:335
  100.4 9.7 %collective-permute-start.2 = (f32[128,128]{1,0:T(8,128)S(1)}, f32[128,128]{1,0:T(8,128)S(1)}, u32[]{:S(2)}, u32[]{:S(2)}) collective-permute-start(f32[128,128]{1,0:T(8,128)S(1)} %add.56), channel_id=1, source_target_pairs={{0,4},{1,5},{2,6},{3,7},{4,0},{5,1},{6,2},{7,3},{8,12},{9,13},{10,... | collective-permute-start | bytes 196616 | tf_op jit(solution)/shard_map/ppermute | solution.py:335
  142.0 22.4 %collective-permute-start.3 = (bf16[5,512,384]{2,1,0:T(8,128)(2,1)S(1)}, bf16[5,512,384]{2,1,0:T(8,128)(2,1)S(1)}, u32[]{:S(2)}, u32[]{:S(2)}) collective-permute-start(bf16[5,512,384]{2,1,0:T(8,128)(2,1)S(1)} %get-tuple-element.50), channel_id=1, source_target_pairs={{0,8},{8,0},{1,9},{9,1},{2,10},{10,2},{3,11},{11,3},{4,12},{12,4},... | collective-permute-start | bytes 5898248 | tf_op jit(solution)/shard_map/ppermute | solution.py:364
  142.3 5.4 %collective-permute-start.4 = (bf16[3,512,384]{2,1,0:T(8,128)(2,1)S(1)}, bf16[3,512,384]{2,1,0:T(8,128)(2,1)S(1)}, u32[]{:S(2)}, u32[]{:S(2)}) collective-permute-start(bf16[3,512,384]{2,1,0:T(8,128)(2,1)S(1)} %get-tuple-element.52), channel_id=1, source_target_pairs={{0,8},{8,0},{1,9},{9,1},{2,10},{10,2},{3,11},{11,3},{4,12},{12,4},... | collective-permute-start | bytes 3538952 | tf_op jit(solution)/shard_map/ppermute | solution.py:363
  148.5 9.2 %collective-permute-start.5 = (bf16[256,384]{1,0:T(8,128)(2,1)S(1)}, bf16[256,384]{1,0:T(8,128)(2,1)S(1)}, u32[]{:S(2)}, u32[]{:S(2)}) collective-permute-start(bf16[256,384]{1,0:T(8,128)(2,1)S(1)} %get-tuple-element.53), channel_id=1, source_target_pairs={{0,1},{1,2},{2,3},{3,4},{4,5},{5,6},{6,7},{7,0},{8,9},{9,10},{10,1... | collective-permute-start | bytes 589832 | tf_op jit(solution)/shard_map/ppermute | solution.py:391
  150.0 15.8 %collective-permute-start.9 = (bf16[256,384]{1,0:T(8,128)(2,1)S(1)}, bf16[256,384]{1,0:T(8,128)(2,1)S(1)}, u32[]{:S(2)}, u32[]{:S(2)}) collective-permute-start(bf16[256,384]{1,0:T(8,128)(2,1)S(1)} %get-tuple-element.57), channel_id=1, source_target_pairs={{0,7},{1,0},{2,1},{3,2},{4,3},{5,4},{6,5},{7,6},{8,15},{9,8},{10,9... | collective-permute-start | bytes 589832 | tf_op jit(solution)/shard_map/ppermute | solution.py:391
  152.0 17.1 %collective-permute-start.12 = (bf16[256,384]{1,0:T(8,128)(2,1)S(1)}, bf16[256,384]{1,0:T(8,128)(2,1)S(1)}, u32[]{:S(2)}, u32[]{:S(2)}) collective-permute-start(bf16[256,384]{1,0:T(8,128)(2,1)S(1)} %get-tuple-element.60), channel_id=1, source_target_pairs={{0,1},{1,2},{2,3},{3,4},{4,5},{5,6},{6,7},{7,0},{8,9},{9,10},{10,1... | collective-permute-start | bytes 589832 | tf_op jit(solution)/shard_map/ppermute | solution.py:391
  152.0 8.9 %collective-permute-start.15 = (bf16[256,384]{1,0:T(8,128)(2,1)S(1)}, bf16[256,384]{1,0:T(8,128)(2,1)S(1)}, u32[]{:S(2)}, u32[]{:S(2)}) collective-permute-start(bf16[256,384]{1,0:T(8,128)(2,1)S(1)} %get-tuple-element.63), channel_id=1, source_target_pairs={{0,7},{1,0},{2,1},{3,2},{4,3},{5,4},{6,5},{7,6},{8,15},{9,8},{10,9... | collective-permute-start | bytes 589832 | tf_op jit(solution)/shard_map/ppermute | solution.py:391
  157.8 7.8 %collective-permute-start.6 = (bf16[256,384]{1,0:T(8,128)(2,1)S(1)}, bf16[256,384]{1,0:T(8,128)(2,1)S(1)}, u32[]{:S(2)}, u32[]{:S(2)}) collective-permute-start(bf16[256,384]{1,0:T(8,128)(2,1)S(1)} %add_convert_fusion.11), channel_id=1, source_target_pairs={{0,1},{1,2},{2,3},{3,4},{4,5},{5,6},{6,7},{7,0},{8,9},{9,10},{10,1... | collective-permute-start | bytes 589832 | tf_op jit(solution)/shard_map/ppermute | solution.py:391
  161.0 8.2 %collective-permute-start.16 = (bf16[256,384]{1,0:T(8,128)(2,1)S(1)}, bf16[256,384]{1,0:T(8,128)(2,1)S(1)}, u32[]{:S(2)}, u32[]{:S(2)}) collective-permute-start(bf16[256,384]{1,0:T(8,128)(2,1)S(1)} %add_convert_fusion.3), channel_id=1, source_target_pairs={{0,7},{1,0},{2,1},{3,2},{4,3},{5,4},{6,5},{7,6},{8,15},{9,8},{10,9... | collective-permute-start | bytes 589832 | tf_op jit(solution)/shard_map/ppermute | solution.py:391
  165.6 8.3 %collective-permute-start.7 = (bf16[256,384]{1,0:T(8,128)(2,1)S(1)}, bf16[256,384]{1,0:T(8,128)(2,1)S(1)}, u32[]{:S(2)}, u32[]{:S(2)}) collective-permute-start(bf16[256,384]{1,0:T(8,128)(2,1)S(1)} %add_convert_fusion.10), channel_id=1, source_target_pairs={{0,1},{1,2},{2,3},{3,4},{4,5},{5,6},{6,7},{7,0},{8,9},{9,10},{10,1... | collective-permute-start | bytes 589832 | tf_op jit(solution)/shard_map/ppermute | solution.py:391
  165.8 8.3 %collective-permute-start.10 = (bf16[256,384]{1,0:T(8,128)(2,1)S(1)}, bf16[256,384]{1,0:T(8,128)(2,1)S(1)}, u32[]{:S(2)}, u32[]{:S(2)}) collective-permute-start(bf16[256,384]{1,0:T(8,128)(2,1)S(1)} %add_convert_fusion.8), channel_id=1, source_target_pairs={{0,7},{1,0},{2,1},{3,2},{4,3},{5,4},{6,5},{7,6},{8,15},{9,8},{10,9... | collective-permute-start | bytes 589832 | tf_op jit(solution)/shard_map/ppermute | solution.py:391
  169.2 9.1 %collective-permute-start.13 = (bf16[256,384]{1,0:T(8,128)(2,1)S(1)}, bf16[256,384]{1,0:T(8,128)(2,1)S(1)}, u32[]{:S(2)}, u32[]{:S(2)}) collective-permute-start(bf16[256,384]{1,0:T(8,128)(2,1)S(1)} %add_convert_fusion.5), channel_id=1, source_target_pairs={{0,1},{1,2},{2,3},{3,4},{4,5},{5,6},{6,7},{7,0},{8,9},{9,10},{10,1... | collective-permute-start | bytes 589832 | tf_op jit(solution)/shard_map/ppermute | solution.py:391
  169.3 9.1 %collective-permute-start.17 = (bf16[256,384]{1,0:T(8,128)(2,1)S(1)}, bf16[256,384]{1,0:T(8,128)(2,1)S(1)}, u32[]{:S(2)}, u32[]{:S(2)}) collective-permute-start(bf16[256,384]{1,0:T(8,128)(2,1)S(1)} %add_convert_fusion.2), channel_id=1, source_target_pairs={{0,7},{1,0},{2,1},{3,2},{4,3},{5,4},{6,5},{7,6},{8,15},{9,8},{10,9... | collective-permute-start | bytes 589832 | tf_op jit(solution)/shard_map/ppermute | solution.py:391
  174.0 8.7 %collective-permute-start.8 = (bf16[256,384]{1,0:T(8,128)(2,1)S(1)}, bf16[256,384]{1,0:T(8,128)(2,1)S(1)}, u32[]{:S(2)}, u32[]{:S(2)}) collective-permute-start(bf16[256,384]{1,0:T(8,128)(2,1)S(1)} %add_convert_fusion.9), channel_id=1, source_target_pairs={{0,1},{1,2},{2,3},{3,4},{4,5},{5,6},{6,7},{7,0},{8,9},{9,10},{10,1... | collective-permute-start | bytes 589832 | tf_op jit(solution)/shard_map/ppermute | solution.py:391
  174.1 8.8 %collective-permute-start.11 = (bf16[256,384]{1,0:T(8,128)(2,1)S(1)}, bf16[256,384]{1,0:T(8,128)(2,1)S(1)}, u32[]{:S(2)}, u32[]{:S(2)}) collective-permute-start(bf16[256,384]{1,0:T(8,128)(2,1)S(1)} %add_convert_fusion.7), channel_id=1, source_target_pairs={{0,7},{1,0},{2,1},{3,2},{4,3},{5,4},{6,5},{7,6},{8,15},{9,8},{10,9... | collective-permute-start | bytes 589832 | tf_op jit(solution)/shard_map/ppermute | solution.py:391
  178.3 7.0 %collective-permute-start.14 = (bf16[256,384]{1,0:T(8,128)(2,1)S(1)}, bf16[256,384]{1,0:T(8,128)(2,1)S(1)}, u32[]{:S(2)}, u32[]{:S(2)}) collective-permute-start(bf16[256,384]{1,0:T(8,128)(2,1)S(1)} %add_convert_fusion.4), channel_id=1, source_target_pairs={{0,1},{1,2},{2,3},{3,4},{4,5},{5,6},{6,7},{7,0},{8,9},{9,10},{10,1... | collective-permute-start | bytes 589832 | tf_op jit(solution)/shard_map/ppermute | solution.py:391
  178.5 6.8 %collective-permute-start.18 = (bf16[256,384]{1,0:T(8,128)(2,1)S(1)}, bf16[256,384]{1,0:T(8,128)(2,1)S(1)}, u32[]{:S(2)}, u32[]{:S(2)}) collective-permute-start(bf16[256,384]{1,0:T(8,128)(2,1)S(1)} %add_convert_fusion.1), channel_id=1, source_target_pairs={{0,7},{1,0},{2,1},{3,2},{4,3},{5,4},{6,5},{7,6},{8,15},{9,8},{10,9... | collective-permute-start | bytes 589832 | tf_op jit(solution)/shard_map/ppermute | solution.py:391
  (6 other events, 18.3 us)
Sparse Core Ops, SparseCore 0:
  88.7 42.1 all-gather.1

commit v5 on v1

v5 whole, which is shorter than its diff:
```python
import functools

import jax
import jax.numpy as jnp
from jax import lax
from jax.experimental import pallas as pl
from jax.experimental.pallas import tpu as pltpu
from jax.sharding import Mesh, PartitionSpec as P

epsilon = 1e-06
exact = lax.Precision.HIGHEST
bf16 = jnp.bfloat16
f32 = jnp.float32
LIMIT = 30 << 20


def mm(a, b, contract_a=1, contract_b=0, precision=None):
    return lax.dot_general(
        a, b, (((contract_a,), (contract_b,)), ((), ())),
        precision=precision, preferred_element_type=f32,
    )


def lower_triangle(n, strict=False):
    rows = lax.broadcasted_iota(jnp.int32, (n, n), 0)
    cols = lax.broadcasted_iota(jnp.int32, (n, n), 1)
    return (rows > cols) if strict else (rows >= cols)


def block_state_kernel(keys, values, log_decay, ids, out, *, experts, capacity):
    heads, positions = log_decay.shape
    size = keys.shape[1] // heads
    per_head = out.shape[1]
    rows = size // per_head
    until = mm(lower_triangle(positions).astype(f32), log_decay[...], 1, 1, exact)
    first, second = slots_of(ids[...], experts, capacity)
    chosen = [jnp.broadcast_to(ids[k:k + 1, :].astype(f32), (8, positions)).astype(bf16) for k in range(2)]
    others = mm(chosen[1], first.astype(bf16), 1, 1) + mm(chosen[0], second.astype(bf16), 1, 1)
    for h in range(heads):
        lanes = slice(h * size, (h + 1) * size)
        total = until[positions - 1:positions, h:h + 1]
        trailing = jnp.exp(total - until[:, h:h + 1])
        weighted = (keys[:, lanes].astype(f32) * trailing).astype(bf16)
        state = mm(weighted, values[:, lanes], 0, 0)
        out[h, :, :rows, :] = state.astype(bf16).reshape(per_head, rows, size)
        high = total.astype(bf16).astype(f32)
        middle = (total - high).astype(bf16).astype(f32)
        low = total - high - middle
        row = lax.broadcasted_iota(jnp.int32, (rows, size), 0)
        terms = jnp.where(row == 0, high, jnp.where(row == 1, middle, jnp.where(row == 2, low, 0.0)))
        terms = jnp.where(row == 3, others[0:1, lanes], terms)
        out[h, :, rows:, :] = jnp.broadcast_to(terms.astype(bf16), (per_head, rows, size))


def state_scan_kernel(part, received, prior, out, others):
    blocks, rows, _ = out.shape
    state = prior[pl.ds(pl.multiple_of(part[0] * rows, rows), rows), :]
    for k in range(blocks):
        out[k] = state.astype(bf16)
        terms = received[k, rows:, :].astype(f32)
        total = terms[0:1] + terms[1:2] + terms[2:3]
        state = jnp.exp(total) * state + received[k, :rows, :].astype(f32)
        others[k:k + 1, :] = terms[3:4]


def inner_kernel(queries, keys, values, log_decay, out, growth):
    heads, positions = log_decay.shape
    size = queries.shape[1] // heads
    causal = lower_triangle(positions)
    until = mm(causal.astype(f32), log_decay[...], 1, 1, exact)
    until_row = mm(log_decay[...], causal.astype(f32), 1, 1, exact)
    for h in range(heads):
        lanes = slice(h * size, (h + 1) * size)
        spread = until[:, h:h + 1] - until_row[h:h + 1, :]
        weights = jnp.where(causal, jnp.exp(jnp.where(causal, spread, 0.0)), 0.0)
        scores = mm(queries[:, lanes], keys[:, lanes], 1, 1) * weights
        out[:, lanes] = mm(scores.astype(bf16), values[:, lanes])
    growth[...] = jnp.exp(until)


def project_kernel(queries, inner, growth, state, gate_input, gain, weight, out, normed, *, heads):
    size = queries.shape[1] // heads
    step = pl.program_id(0)

    @pl.when(step == 0)
    def _():
        for h in range(heads):
            lanes = slice(h * size, (h + 1) * size)
            carried = mm(queries[:, lanes], state[lanes, :])
            attended = inner[:, lanes] + growth[:, h:h + 1] * carried
            squares = jnp.mean(attended * attended, axis=1, keepdims=True)
            gating = jax.nn.sigmoid(gate_input[:, lanes].astype(f32))
            normed[:, lanes] = (attended * lax.rsqrt(squares + epsilon) * gain[:, lanes] * gating).astype(bf16)

    each, _, width = out.shape
    product = mm(normed[...], weight[:, pl.ds(pl.multiple_of(step * each * width, each * width), each * width)])
    for c in range(each):
        out[c] = product[:, c * width:(c + 1) * width].astype(bf16)


def slots_of(ids, experts, capacity):
    positions = ids.shape[1]
    expert = lax.broadcasted_iota(jnp.int32, (experts, positions), 0)
    choices = [(ids[k:k + 1, :] == expert).astype(f32) for k in range(2)]
    earlier = mm((choices[0] + choices[1]).astype(bf16), lower_triangle(positions, True).astype(bf16), 1, 1)
    slot = lax.broadcasted_iota(jnp.int32, (experts * capacity, positions), 0)
    found = []
    for k, choice in enumerate(choices):
        position = jnp.sum(choice * earlier, axis=0, keepdims=True).astype(jnp.int32)
        found.append((slot == ids[k:k + 1, :] * capacity + position).astype(f32))
    return found


def dispatch_kernel(index, partial, layer_input, gain, ids, outgoing, hidden, *, experts, capacity):
    del index
    total = layer_input[...].astype(f32)
    for k in range(partial.shape[0]):
        total += partial[k].astype(f32)
    hidden[...] = total
    first, second = slots_of(ids[...], experts, capacity)
    outgoing[...] = mm((first + second).astype(bf16), (total * gain[0]).astype(bf16)).astype(bf16)


def fetch(pairs, sems):
    copies = [pltpu.make_async_copy(source, target, sems.at[k]) for k, (source, target) in enumerate(pairs)]
    for copy in copies:
        copy.start()
    return copies


def load_kernel(source, target, sems):
    parts = sems.shape[0]
    rows = source.shape[0] // parts
    pairs = [(source.at[pl.ds(k * rows, rows)], target.at[pl.ds(k * rows, rows)]) for k in range(parts)]
    for copy in fetch(pairs, sems):
        copy.wait()


def load_experts_kernel(place, *refs, order, distances, peers):
    weights, (gate_up, down, sems) = refs[:6], refs[6:]
    depth, share = weights[0].shape
    rows = depth // peers
    pairs = []
    for c, distance in enumerate(order):
        start = pl.multiple_of(lax.rem(place[0] + distance + peers, peers) * rows, rows)
        for k, weight in enumerate(weights[:4]):
            pairs.append((weight.at[pl.ds(start, rows)], gate_up.at[pl.ds(c * rows, rows), pl.ds(k * share, share)]))
    for c, distance in enumerate(distances):
        start = pl.multiple_of(lax.rem(place[0] + distance + peers, peers) * rows, rows)
        for k, weight in enumerate(weights[4:]):
            pairs.append((weight.at[:, pl.ds(start, rows)], down.at[pl.ds(k * share, share), pl.ds(c * rows, rows)]))
    for copy in fetch(pairs, sems):
        copy.wait()


def gate_up_sums(place, chunks, gain, router, gate_up, order, first, h):
    peers, _, width = gain.shape
    experts = router.shape[0]
    total, squares, logits = 0.0, 0.0, 0.0
    for c in range(0, len(chunks), 2):
        pair = [chunk[h][...] for chunk in chunks[c:c + 2]]
        for k, piece in enumerate(pair):
            group = lax.rem(place[0] + order[first + c + k] + peers, peers)
            wide = piece.astype(f32) / gain[group]
            squares += jnp.sum(wide * wide, axis=1, keepdims=True)
            logits += mm(piece, router[:, pl.ds(pl.multiple_of(group * width, width), width)], 1, 1)
        lanes = slice((first + c) * width, (first + c + 2) * width)
        total += mm(jnp.concatenate(pair, axis=1), gate_up[lanes, :])
    beside = jnp.concatenate([logits, jnp.broadcast_to(squares, (logits.shape[0], 128 - experts))], axis=1)
    return total, beside


def near_chunks_kernel(place, gain, router, gate_up, *refs, order, count):
    chunks, (total, beside) = refs[:2 * count], refs[2 * count:]
    chunks = [chunks[2 * k:2 * k + 2] for k in range(count)]
    half = chunks[0][0].shape[0]
    for h in range(2):
        rows = slice(h * half, (h + 1) * half)
        total[rows, :], beside[rows, :] = gate_up_sums(place, chunks, gain, router, gate_up, order, 0, h)


def mixing_of(place, others, logits, h, capacity):
    rows, experts = logits.shape
    blocks, lanes = others.shape
    row = lax.broadcasted_iota(jnp.int32, (rows, blocks), 0)
    block = lax.broadcasted_iota(jnp.int32, (rows, blocks), 1)
    sender = 2 * (lax.div(row, capacity) + h * (rows // capacity)) + place[1]
    from_sender = mm((sender == block).astype(bf16), others[...].astype(bf16))
    row = lax.broadcasted_iota(jnp.int32, (rows, lanes), 0)
    lane = lax.broadcasted_iota(jnp.int32, (rows, lanes), 1)
    own_lane = lax.rem(place[2], lanes // capacity) * capacity + lax.rem(row, capacity)
    other = jnp.sum(jnp.where(lane == own_lane, from_sender, 0.0), axis=1, keepdims=True).astype(jnp.int32)
    expert = lax.broadcasted_iota(jnp.int32, (rows, experts), 1)
    sign = (expert == place[2]).astype(f32) - (expert == other).astype(f32)
    return jax.nn.sigmoid(jnp.sum(sign * logits, axis=1, keepdims=True))


def products(activated, down, start, count, share):
    found = []
    for c in range(start, start + count, 2):
        both = min(2, start + count - c)
        product = mm(activated, down[:, c * share:(c + both) * share])
        found += [product[:, k * share:(k + 1) * share].astype(bf16) for k in range(both)]
    return found


def far_chunks_kernel(
    place, gain, router, gate_up, down, others, total, beside, *refs, order, count, far, width, capacity
):
    chunks, outs, activated = refs[:2 * count], refs[2 * count:-1], refs[-1]
    chunks = [chunks[2 * k:2 * k + 2] for k in range(count)]
    half = chunks[0][0].shape[0]
    units = activated.shape[1]
    for h in range(2):
        rows = slice(h * half, (h + 1) * half)
        product, sums = gate_up_sums(place, chunks, gain, router, gate_up, order, len(order) - count, h)
        sums += beside[rows, :]
        experts = router.shape[0]
        scale = lax.rsqrt(sums[:, experts:experts + 1] / width + epsilon)
        mixing = mixing_of(place, others, sums[:, :experts] * scale, h, capacity)
        both = (total[rows, :] + product) * scale
        gated = both[:, :units]
        active = (gated * jax.nn.sigmoid(gated) * both[:, units:] * mixing).astype(bf16)
        activated[rows, :] = active
        for k, piece in enumerate(products(active, down, 0, far, outs[0].shape[1])):
            outs[2 * k + h][...] = piece


def near_products_kernel(activated, down, *outs, far, near):
    half = activated.shape[0] // 2
    for h in range(2):
        rows = slice(h * half, (h + 1) * half)
        for k, piece in enumerate(products(activated[rows, :], down, far, near, outs[0].shape[1])):
            outs[2 * k + h][...] = piece


def combine_kernel(returned, hidden, ids, out, *, experts, capacity):
    first, second = slots_of(ids[...], experts, capacity)
    out[...] = (hidden[...] + mm((first + second).astype(bf16), returned[...], 0, 0)).astype(out.dtype)


def call(kernel, shapes, *args, **kwargs):
    return pl.pallas_call(
        kernel,
        out_shape=shapes,
        compiler_params=pltpu.CompilerParams(vmem_limit_bytes=LIMIT),
        **kwargs,
    )(*args)


def stays(x):
    return pltpu.with_memory_space_constraint(x, pltpu.HBM)


def in_vmem(x):
    return pltpu.with_memory_space_constraint(x, pltpu.VMEM)


def whole(shape):
    return pl.BlockSpec(shape, lambda *_: (0,) * len(shape))


def shards(
    layer_input, queries, keys, values, gate_input, log_decay, prior_state, attn_gain,
    out_weight, moe_gain, router, expert_ids, w_gate, w_up, w_down,
):
    struct = jax.ShapeDtypeStruct
    positions, head_lanes = queries.shape
    heads, size, _ = prior_state.shape
    chips, cores, peers = lax.axis_size("chip"), lax.axis_size("core"), lax.axis_size("tp")
    blocks = chips * cores
    width = out_weight.shape[1]
    share = layer_input.shape[1]
    experts = router.shape[1]
    capacity = 8 * positions // blocks
    slots = experts * capacity
    core = lax.axis_index("core")
    cx = lax.axis_index("chip") * cores + core
    tp = lax.axis_index("tp")

    ids = stays(expert_ids.T)
    queries, keys, values, log_decay = stays(queries), stays(keys), stays(values), stays(log_decay)
    vmem = pl.BlockSpec(memory_space=pltpu.VMEM)
    hbm = pl.BlockSpec(memory_space=pl.ANY)

    swap = [(0, 1), (1, 0)]
    weights = []
    for weight in (w_gate[0], w_up[0], w_down[0]):
        weights += [weight, lax.ppermute(weight, "core", swap)]

    rows = heads * size // blocks
    parts = call(
        functools.partial(block_state_kernel, experts=experts, capacity=capacity),
        struct((heads, size // rows, 2 * rows, size), bf16), keys, values, log_decay, ids,
    )
    parts, out_weight = lax.optimization_barrier((parts, out_weight))
    out_weight = pl.pallas_call(
        load_kernel,
        out_shape=pltpu.VMEM((head_lanes, width), bf16),
        in_specs=[hbm],
        out_specs=vmem,
        scratch_shapes=[pltpu.SemaphoreType.DMA((4,))],
        compiler_params=pltpu.CompilerParams(vmem_limit_bytes=4 << 20),
        cost_estimate=pl.CostEstimate(flops=0, bytes_accessed=2 * head_lanes * width, transcendentals=0),
    )(stays(out_weight))
    received = lax.all_to_all(parts.reshape(blocks, 2 * rows, size), ("chip", "core"), 0, 0, tiled=True)
    inner, growth = call(
        inner_kernel,
        (struct((positions, head_lanes), f32), struct((positions, heads), f32)),
        queries, keys, values, log_decay,
    )
    befores, others = call(
        state_scan_kernel, (struct((blocks, rows, size), bf16), struct((blocks, size), f32)),
        cx.reshape(1), received, stays(prior_state.reshape(heads * size, size)),
        in_specs=[pl.BlockSpec(memory_space=pltpu.SMEM)] + [pl.BlockSpec(memory_space=pltpu.VMEM)] * 2,
    )
    state = lax.all_to_all(befores, ("chip", "core"), 0, 0, tiled=True).reshape(heads * size, size)

    each = 2
    partial = call(
        functools.partial(project_kernel, heads=heads),
        struct((peers, positions, share), bf16),
        queries, stays(inner), stays(growth), state, stays(gate_input), stays(attn_gain.reshape(1, head_lanes)),
        in_vmem(out_weight),
        grid=(peers // each,),
        in_specs=[whole((positions, head_lanes))] * 2 + [whole((positions, heads)), whole((heads * size, size))]
        + [whole((positions, head_lanes)), whole((1, head_lanes)), vmem],
        out_specs=pl.BlockSpec((each, positions, share), lambda i: (i, 0, 0)),
        scratch_shapes=[pltpu.VMEM((positions, head_lanes), bf16)],
    )
    partial = lax.all_to_all(partial, "tp", 0, 0, tiled=True)
    outgoing, hidden = pl.pallas_call(
        functools.partial(dispatch_kernel, experts=experts, capacity=capacity),
        out_shape=(struct((slots, share), bf16), struct((positions, share), f32)),
        grid_spec=pltpu.PrefetchScalarGridSpec(
            num_scalar_prefetch=1,
            grid=(1,),
            in_specs=[
                whole((peers, positions, share)),
                whole((positions, share)),
                pl.BlockSpec((1, 1, share), lambda i, index: (index[0], 0, 0)),
                whole(ids.shape),
            ],
            out_specs=[whole((slots, share)), whole((positions, share))],
        ),
        compiler_params=pltpu.CompilerParams(vmem_limit_bytes=LIMIT),
    )(tp.reshape(1), partial, stays(layer_input), stays(moe_gain.reshape(peers, 1, share)), ids)

    arrived = lax.all_to_all(outgoing.reshape(chips, capacity, share), "chip", 0, 0, tiled=True)
    held = chips * capacity
    half = held // 2
    arrived = arrived.reshape(held, share)
    here = (arrived[:half], arrived[half:])
    here, weights = lax.optimization_barrier((here, weights))

    def moved(piece, step):
        return lax.ppermute(piece, "tp", [(i, (i + step) % peers) for i in range(peers)])

    order = (0, 1, -1, 2, -2, 3, -3, 4)
    far, near = (4, 3, -3), (2, -2, 1, -1, 0)
    units = cores * share
    work = 2 * held * width * units
    place = jnp.stack([tp, core, lax.axis_index("chip")])
    params = pltpu.CompilerParams(vmem_limit_bytes=LIMIT)
    smem = pl.BlockSpec(memory_space=pltpu.SMEM)
    gate_up, down = pl.pallas_call(
        functools.partial(load_experts_kernel, order=order, distances=far + near, peers=peers),
        out_shape=(pltpu.VMEM((width, 2 * units), bf16), pltpu.VMEM((units, width), bf16)),
        in_specs=[smem] + [hbm] * 6,
        out_specs=(vmem, vmem),
        scratch_shapes=[pltpu.SemaphoreType.DMA((6 * peers,))],
        compiler_params=pltpu.CompilerParams(vmem_limit_bytes=4 << 20),
        cost_estimate=pl.CostEstimate(flops=0, bytes_accessed=6 * width * units, transcendentals=0),
    )(place, *[stays(weight) for weight in weights])
    gain, router = stays(moe_gain.reshape(peers, 1, share)), stays(router.T)
    others = stays(others)
    chunks = {0: here}
    up, down_way = here, here
    for distance in (1, 2, 3):
        up = (moved(up[0], 1), moved(up[1], 1))
        down_way = (moved(down_way[0], -1), moved(down_way[1], -1))
        if distance == 1:
            up, down_way, gate_up, down = lax.optimization_barrier((up, down_way, gate_up, down))
        chunks[-distance], chunks[distance] = up, down_way
    chunks[4] = (moved(up[0], 1), moved(down_way[1], -1))
    gate_up, down = in_vmem(gate_up), in_vmem(down)
    last = 2
    first_chunks = [piece for distance in order[:-last] for piece in chunks[distance]]
    total, beside = pl.pallas_call(
        functools.partial(near_chunks_kernel, order=order, count=len(order) - last),
        out_shape=(struct((held, 2 * units), f32), struct((held, 128), f32)),
        in_specs=[smem] + [vmem] * (3 + len(first_chunks)),
        compiler_params=params,
        cost_estimate=pl.CostEstimate(
            flops=2 * work * (peers - last) // peers, bytes_accessed=4 << 20, transcendentals=0),
    )(place, gain, router, gate_up, *first_chunks)
    last_chunks = [piece for distance in order[-last:] for piece in chunks[distance]]
    piece = struct((half, share), bf16)
    *ready, activated = pl.pallas_call(
        functools.partial(far_chunks_kernel, order=order, count=last, far=len(far), width=width, capacity=capacity),
        out_shape=(piece,) * (2 * len(far)) + (struct((held, units), bf16),),
        in_specs=[smem] + [vmem] * (7 + len(last_chunks)),
        compiler_params=params,
        cost_estimate=pl.CostEstimate(
            flops=2 * work * last // peers + work * len(far) // peers, bytes_accessed=4 << 20,
            transcendentals=held * units),
    )(place, gain, router, gate_up, down, others, total, beside, *last_chunks)
    a4, b4, a3, b3, a3m, b3m = ready

    def plus(*pieces):
        return sum(piece.astype(f32) for piece in pieces).astype(bf16)

    a_up, b_down = moved(a4, 1), moved(b4, -1)
    a_down, b_up = moved(a3m, -1), moved(b3, 1)
    a2, b2, a2m, b2m, a1, b1, a1m, b1m, a0, b0 = pl.pallas_call(
        functools.partial(near_products_kernel, far=len(far), near=len(near)),
        out_shape=(piece,) * (2 * len(near)),
        in_specs=[vmem] * 2,
        compiler_params=params,
        cost_estimate=pl.CostEstimate(flops=work * len(near) // peers, bytes_accessed=4 << 20, transcendentals=0),
    )(activated, down)
    a_up, b_down = moved(plus(a_up, a3), 1), moved(plus(b_down, b3m), -1)
    a_down, b_up = moved(plus(a_down, a2m), -1), moved(plus(b_up, b2), 1)
    a_up, b_down = moved(plus(a_up, a2), 1), moved(plus(b_down, b2m), -1)
    a_down, b_up = moved(plus(a_down, a1m), -1), moved(plus(b_up, b1), 1)
    a_up, b_down = moved(plus(a_up, a1), 1), moved(plus(b_down, b1m), -1)
    summed = jnp.concatenate([plus(a0, a_up, a_down), plus(b0, b_up, b_down)])
    returned = lax.all_to_all(summed.reshape(chips, capacity, share), "chip", 0, 0, tiled=True)
    return call(
        functools.partial(combine_kernel, experts=experts, capacity=capacity),
        struct((positions, share), bf16),
        returned.reshape(slots, share), hidden, ids,
    )


def solution(mesh):
    cx, tp = mesh.devices.shape
    fine = Mesh(mesh.devices.reshape(cx // 2, 2, tp), ("chip", "core", "tp"))
    both = ("chip", "core")
    placed = (
        P(both, "tp"), P(both, "tp"), P(both, "tp"), P(both, "tp"), P(both, "tp"),
        P("tp", both), P("tp", None, None), P("tp"), P("tp", None), P(), P(),
        P(both, None), P(both, None, "tp"), P(both, None, "tp"), P(both, "tp", None),
    )
    return jax.shard_map(shards, mesh=fine, in_specs=placed, out_specs=P(both, "tp"), check_vma=False)
```

time: 303 us -> 177 us (0.58)
  waiting for transfers between devices: 197 us -> 47.7 us
  starting transfers between devices: 28.9 us -> 66.5 us
  local copies, waits for them, and re-layouts: 18.1 us -> 2.92 us
  blocking collectives: 13.7 us -> 26.7 us
  between operations: 13.2 us -> 0.37 us
  Pallas kernels: 25.7 us -> 31.1 us
  other arithmetic: 5.34 us -> 0.78 us
    psum x1 -> x0, waiting for transfers between devices: 72.9 us -> none  [shards(): sums = lax.psum(sums, 'tp')]
    reduce_scatter x1 -> x0, waiting for transfers between devices: 45.6 us -> none  [shards(): lax.psum_scatter(both.reshape(peers * held, share), 'tp', scatter_dimensi...]
    ppermute x1 -> x31, starting transfers between devices: 0.34 us -> 45.5 us  [the longest x28 44.7 us: moved(): lax.ppermute(piece, 'tp', [(i, (i + step) % peers) for i in range(peers)])]
    all_gather x1 -> x0, waiting for transfers between devices: 39.4 us -> none  [shards(): lax.all_gather(arrived.reshape(chips * capacity, share), ('core', 'tp'))]
    pallas_call x0 -> x5, Pallas kernels: none -> 19.5 us  [the longest x1 6.03 us: shards(): pl.pallas_call(functools.partial(load_experts_kernel, order=order, distan...]
    pallas_call x6 -> x5, Pallas kernels: 24.6 us -> 10.3 us  [call(): pl.pallas_call(kernel, out_shape=shapes, compiler_params=pltpu.CompilerPa...]
    unnamed x40 -> x8, local copies, waits for them, and re-layouts: 15.9 us -> 2.88 us
    all_to_all x0 -> x1, blocking collectives: none -> 12.2 us  [shards(): lax.all_to_all(summed.reshape(chips, capacity, share), 'chip', 0, 0, tile...]
  transfers between devices with their start and end apart: 8 -> 34, of which waited for: 7 -> 11; matrix products, arithmetic and copies ran while one was open for 0% -> 0% of each run, Pallas kernels for 0% -> 13%
where the time goes in v5:
time: 177 us; the launch traced here: 176 us
  starting transfers between devices  66.5 us (38%)
  waiting for transfers between devices  47.7 us (27%)
  Pallas kernels  31.1 us (18%)
  blocking collectives  26.7 us (15%)
  local copies, waits for them, and re-layouts  2.92 us (2%)
    ppermute x28, starting transfers between devices, moved(): lax.ppermute(piece, 'tp', [(i, (i + step) % peers) for i in range(peers)])  44.7 us
    all_to_all x1, waiting for transfers between devices, shards(): partial = lax.all_to_all(partial, 'tp', 0, 0, tiled=True)  23.4 us
    ppermute x28, waiting for transfers between devices, moved(): lax.ppermute(piece, 'tp', [(i, (i + step) % peers) for i in range(peers)])  15.8 us
    all_to_all x1, blocking collectives, shards(): lax.all_to_all(outgoing.reshape(chips, capacity, share), 'chip', 0, 0, ti...  14.5 us
    all_to_all x1, blocking collectives, shards(): lax.all_to_all(summed.reshape(chips, capacity, share), 'chip', 0, 0, tile...  12.2 us
    pallas_call x5, Pallas kernels, call(): pl.pallas_call(kernel, out_shape=shapes, compiler_params=pltpu.CompilerPa...  10.3 us
    all_to_all x1, starting transfers between devices, shards(): partial = lax.all_to_all(partial, 'tp', 0, 0, tiled=True)  8.46 us
    all_to_all x1, starting transfers between devices, shards(): lax.all_to_all(parts.reshape(blocks, 2 * rows, size), ('chip', 'core'), 0...  7.62 us
  transfers between devices with their start and end apart: 34, of which 11 were waited for; matrix products, arithmetic and copies ran while one was open for 0% of the time, Pallas kernels for 13%

profile of v5, /device:TPU:2, one launch (start us, length us, event | category | flops | bytes accessed | tf_op | source)
XLA Modules:
  0.0 176.1 jit_solution(10916306248813771819)
XLA Ops:
  2.2 7.6 %all-to-all-start = ((bf16[32,32,128]{2,1,0:T(8,128)(2,1)}), bf16[32,32,128]{2,1,0:T(8,128)(2,1)S(1)}, u32[]{:S(2)}, u32[]{:S(2)}) async-start(bf16[32,32,128]{2,1,0:T(8,128)(2,1)} %bitcast.7), calls=%async_computation | async-start | bytes 524288 | tf_op jit(solution)/shard_map/all_to_all | solution.py:306
  10.6 6.9 %all-to-all-done.received = bf16[32,32,128]{2,1,0:T(8,128)(2,1)S(1)} async-done(((bf16[32,32,128]{2,1,0:T(8,128)(2,1)}), bf16[32,32,128]{2,1,0:T(8,128)(2,1)S(1)}, u32[]{:S(2)}, u32[]{:S(2)}) %all-to-all-start) | async-done | bytes 262176 | tf_op jit(solution)/shard_map/all_to_all | solution.py:306
  19.8 5.0 %all-to-all-start.1 = ((bf16[32,16,128]{2,1,0:T(8,128)(2,1)}), bf16[32,16,128]{2,1,0:T(8,128)(2,1)S(1)}, u32[]{:S(2)}, u32[]{:S(2)}) async-start(bf16[32,16,128]{2,1,0:T(8,128)(2,1)} %get-tuple-element.51), calls=%async_computation.1 | async-start | bytes 262144 | tf_op jit(solution)/shard_map/all_to_all | solution.py:317
  35.1 8.5 %all-to-all-start.2 = ((bf16[8,128,384]{2,1,0:T(8,128)(2,1)}), bf16[8,128,384]{2,1,0:T(8,128)(2,1)S(1)}, u32[]{:S(2)}, u32[]{:S(2)}) async-start(bf16[8,128,384]{2,1,0:T(8,128)(2,1)} %copy-done), calls=%async_computation.2 | async-start | bytes 1572864 | tf_op jit(solution)/shard_map/all_to_all | solution.py:331
  43.6 23.4 %all-to-all-done.2.partial = bf16[8,128,384]{2,1,0:T(8,128)(2,1)S(1)} async-done(((bf16[8,128,384]{2,1,0:T(8,128)(2,1)}), bf16[8,128,384]{2,1,0:T(8,128)(2,1)S(1)}, u32[]{:S(2)}, u32[]{:S(2)}) %all-to-all-start.2) | async-done | bytes 786464 | tf_op jit(solution)/shard_map/all_to_all | solution.py:331
  68.4 14.5 %all_to_all.25 = bf16[16,32,384]{2,1,0:T(8,128)(2,1)S(1)} all-to-all(bf16[16,32,384]{2,1,0:T(8,128)(2,1)S(1)} %bitcast.21), channel_id=1, replica_groups=mesh['chip'=16,'core'=2,'tp'=8] {'chip'}, dimensions={0} | all-to-all | bytes 786432 | tf_op jit(solution)/shard_map/all_to_all | solution.py:349
  83.2 3.2 %collective-permute-start.5 = (bf16[256,384]{1,0:T(8,128)(2,1)S(1)}, bf16[256,384]{1,0:T(8,128)(2,1)S(1)}, u32[]{:S(2)}, u32[]{:S(2)}) collective-permute-start(bf16[256,384]{1,0:T(8,128)(2,1)S(1)} %bitcast.26), channel_id=1, source_target_pairs={{0,7},{1,0},{2,1},{3,2},{4,3},{5,4},{6,5},{7,6},{8,15},{9,8},{10,9... | collective-permute-start | bytes 589832 | tf_op jit(solution)/shard_map/ppermute | solution.py:357
  88.4 6.0 %shard_map.151 = (bf16[3072,1536]{1,0:T(8,128)(2,1)S(1)}, bf16[768,3072]{1,0:T(8,128)(2,1)S(1)}) custom-call(s32[3]{0:T(128)S(1)} %pad_add_fusion.place, bf16[3072,384]{1,0:T(8,128)(2,1)} %bitcast.29, bf16[3072,384]{1,0:T(8,128)(2,1)} %collective-permute-done.refs_1_, bf16[3072,384]{1,0:T(8,128)(2,1)} %bitcast.31, ...), custom_call_target="tpu_custom_call" | custom-call | bytes 14155776 | tf_op jit(solution)/shard_map/pallas_call | solution.py:366
  94.6 3.1 %collective-permute-start.8 = (bf16[256,384]{1,0:T(8,128)(2,1)S(1)}, bf16[256,384]{1,0:T(8,128)(2,1)S(1)}, u32[]{:S(2)}, u32[]{:S(2)}) collective-permute-start(bf16[256,384]{1,0:T(8,128)(2,1)S(1)} %collective-permute-done.6.refs_3_), channel_id=1, source_target_pairs={{0,7},{1,0},{2,1},{3,2},{4,3},{5,4},{6,5},{7,6},{8,15},{9,8},{10,9... | collective-permute-start | bytes 589832 | tf_op jit(solution)/shard_map/ppermute | solution.py:357
  99.8 3.5 %collective-permute-done.9.refs_8_ = bf16[256,384]{1,0:T(8,128)(2,1)S(1)} collective-permute-done((bf16[256,384]{1,0:T(8,128)(2,1)S(1)}, bf16[256,384]{1,0:T(8,128)(2,1)S(1)}, u32[]{:S(2)}, u32[]{:S(2)}) %collective-permute-start.9) | collective-permute-done | bytes 196640 | tf_op jit(solution)/shard_map/ppermute | solution.py:357
  103.4 3.2 %collective-permute-start.12 = (bf16[256,384]{1,0:T(8,128)(2,1)S(1)}, bf16[256,384]{1,0:T(8,128)(2,1)S(1)}, u32[]{:S(2)}, u32[]{:S(2)}) collective-permute-start(bf16[256,384]{1,0:T(8,128)(2,1)S(1)} %collective-permute-done.8.refs_7_), channel_id=1, source_target_pairs={{0,7},{1,0},{2,1},{3,2},{4,3},{5,4},{6,5},{7,6},{8,15},{9,8},{10,9... | collective-permute-start | bytes 589832 | tf_op jit(solution)/shard_map/ppermute | solution.py:357
  106.6 3.3 %collective-permute-start.11 = (bf16[256,384]{1,0:T(8,128)(2,1)S(1)}, bf16[256,384]{1,0:T(8,128)(2,1)S(1)}, u32[]{:S(2)}, u32[]{:S(2)}) collective-permute-start(bf16[256,384]{1,0:T(8,128)(2,1)S(1)} %collective-permute-done.7.refs_6_), channel_id=1, source_target_pairs={{0,7},{1,0},{2,1},{3,2},{4,3},{5,4},{6,5},{7,6},{8,15},{9,8},{10,9... | collective-permute-start | bytes 589832 | tf_op jit(solution)/shard_map/ppermute | solution.py:357
  112.4 3.2 %collective-permute-start.16 = (bf16[256,384]{1,0:T(8,128)(2,1)S(1)}, bf16[256,384]{1,0:T(8,128)(2,1)S(1)}, u32[]{:S(2)}, u32[]{:S(2)}) collective-permute-start(bf16[256,384]{1,0:T(8,128)(2,1)S(1)} %collective-permute-done.12.refs_11_), channel_id=1, source_target_pairs={{0,7},{1,0},{2,1},{3,2},{4,3},{5,4},{6,5},{7,6},{8,15},{9,8},{10,9... | collective-permute-start | bytes 589832 | tf_op jit(solution)/shard_map/ppermute | solution.py:357
  115.7 5.4 %shard_map.152 = (f32[512,1536]{1,0:T(8,128)S(1)}, f32[512,128]{1,0:T(8,128)S(1)}) custom-call(s32[3]{0:T(128)S(1)} %pad_add_fusion.place, f32[8,1,384]{2,1,0:T(1,128)} %bitcast.39, bf16[16,3072]{1,0:T(8,128)(2,1)} %bitcast.36, bf16[3072,1536]{1,0:T(8,128)(2,1)S(1)} %get-tuple-element.64.gate_up, bf16[256,384]{1,0:T(8,128)(2,1)S(1)} %bitcast.27, ...), custom_call_target="tpu_custom_call" | custom-call | flops 3623878656 | bytes 4194304 | tf_op jit(solution)/shard_map/pallas_call | solution.py:389
  121.1 4.4 %shard_map.153 = (bf16[256,384]{1,0:T(8,128)(2,1)S(1)}, bf16[256,384]{1,0:T(8,128)(2,1)S(1)}, bf16[256,384]{1,0:T(8,128)(2,1)S(1)}, bf16[256,384]{1,0:T(8,128)(2...) custom-call(s32[3]{0:T(128)S(1)} %pad_add_fusion.place, ...), custom_call_target="tpu_custom_call" | custom-call | flops 2113929216 | bytes 4194304 | tf_op jit(solution)/shard_map/pallas_call | solution.py:399
  125.6 3.2 %collective-permute-start.21 = (bf16[256,384]{1,0:T(8,128)(2,1)S(1)}, bf16[256,384]{1,0:T(8,128)(2,1)S(1)}, u32[]{:S(2)}, u32[]{:S(2)}) collective-permute-start(bf16[256,384]{1,0:T(8,128)(2,1)S(1)} %get-tuple-element.79), channel_id=1, source_target_pairs={{0,7},{1,0},{2,1},{3,2},{4,3},{5,4},{6,5},{7,6},{8,15},{9,8},{10,9... | collective-permute-start | bytes 589832 | tf_op jit(solution)/shard_map/ppermute | solution.py:357
  128.8 3.2 %collective-permute-start.27 = (bf16[256,384]{1,0:T(8,128)(2,1)S(1)}, bf16[256,384]{1,0:T(8,128)(2,1)S(1)}, u32[]{:S(2)}, u32[]{:S(2)}) collective-permute-start(bf16[256,384]{1,0:T(8,128)(2,1)S(1)} %get-tuple-element.86), channel_id=1, source_target_pairs={{0,7},{1,0},{2,1},{3,2},{4,3},{5,4},{6,5},{7,6},{8,15},{9,8},{10,9... | collective-permute-start | bytes 589832 | tf_op jit(solution)/shard_map/ppermute | solution.py:357
  134.1 3.3 %collective-permute-start.22 = (bf16[256,384]{1,0:T(8,128)(2,1)S(1)}, bf16[256,384]{1,0:T(8,128)(2,1)S(1)}, u32[]{:S(2)}, u32[]{:S(2)}) collective-permute-start(bf16[256,384]{1,0:T(8,128)(2,1)S(1)} %add_convert_fusion.8), channel_id=1, source_target_pairs={{0,7},{1,0},{2,1},{3,2},{4,3},{5,4},{6,5},{7,6},{8,15},{9,8},{10,9... | collective-permute-start | bytes 589832 | tf_op jit(solution)/shard_map/ppermute | solution.py:357
  138.1 3.3 %collective-permute-start.28 = (bf16[256,384]{1,0:T(8,128)(2,1)S(1)}, bf16[256,384]{1,0:T(8,128)(2,1)S(1)}, u32[]{:S(2)}, u32[]{:S(2)}) collective-permute-start(bf16[256,384]{1,0:T(8,128)(2,1)S(1)} %add_convert_fusion.3), channel_id=1, source_target_pairs={{0,7},{1,0},{2,1},{3,2},{4,3},{5,4},{6,5},{7,6},{8,15},{9,8},{10,9... | collective-permute-start | bytes 589832 | tf_op jit(solution)/shard_map/ppermute | solution.py:357
  142.5 3.6 %collective-permute-start.23 = (bf16[256,384]{1,0:T(8,128)(2,1)S(1)}, bf16[256,384]{1,0:T(8,128)(2,1)S(1)}, u32[]{:S(2)}, u32[]{:S(2)}) collective-permute-start(bf16[256,384]{1,0:T(8,128)(2,1)S(1)} %add_convert_fusion.7), channel_id=1, source_target_pairs={{0,7},{1,0},{2,1},{3,2},{4,3},{5,4},{6,5},{7,6},{8,15},{9,8},{10,9... | collective-permute-start | bytes 589832 | tf_op jit(solution)/shard_map/ppermute | solution.py:357
  147.3 3.3 %collective-permute-start.29 = (bf16[256,384]{1,0:T(8,128)(2,1)S(1)}, bf16[256,384]{1,0:T(8,128)(2,1)S(1)}, u32[]{:S(2)}, u32[]{:S(2)}) collective-permute-start(bf16[256,384]{1,0:T(8,128)(2,1)S(1)} %add_convert_fusion.2), channel_id=1, source_target_pairs={{0,7},{1,0},{2,1},{3,2},{4,3},{5,4},{6,5},{7,6},{8,15},{9,8},{10,9... | collective-permute-start | bytes 589832 | tf_op jit(solution)/shard_map/ppermute | solution.py:357
  151.5 3.5 %collective-permute-done.29 = bf16[256,384]{1,0:T(8,128)(2,1)S(1)} collective-permute-done((bf16[256,384]{1,0:T(8,128)(2,1)S(1)}, bf16[256,384]{1,0:T(8,128)(2,1)S(1)}, u32[]{:S(2)}, u32[]{:S(2)}) %collective-permute-start.29) | collective-permute-done | bytes 196640 | tf_op jit(solution)/shard_map/ppermute | solution.py:357
  155.1 3.8 %collective-permute-start.30 = (bf16[256,384]{1,0:T(8,128)(2,1)S(1)}, bf16[256,384]{1,0:T(8,128)(2,1)S(1)}, u32[]{:S(2)}, u32[]{:S(2)}) collective-permute-start(bf16[256,384]{1,0:T(8,128)(2,1)S(1)} %add_convert_fusion.1), channel_id=1, source_target_pairs={{0,7},{1,0},{2,1},{3,2},{4,3},{5,4},{6,5},{7,6},{8,15},{9,8},{10,9... | collective-permute-start | bytes 589832 | tf_op jit(solution)/shard_map/ppermute | solution.py:357
  162.2 12.2 %all_to_all.26 = bf16[16,32,384]{2,1,0:T(8,128)(2,1)S(1)} all-to-all(bf16[16,32,384]{2,1,0:T(8,128)(2,1)S(1)} %bitcast.34), channel_id=1, replica_groups=mesh['chip'=16,'core'=2,'tp'=8] {'chip'}, dimensions={0} | all-to-all | bytes 786432 | tf_op jit(solution)/shard_map/all_to_all | solution.py:428
  (80 shorter events, 34.9 us)
Async XLA Ops:
  2.2 15.3 %all-to-all-start = ((bf16[32,32,128]{2,1,0:T(8,128)(2,1)}), bf16[32,32,128]{2,1,0:T(8,128)(2,1)S(1)}, u32[]{:S(2)}, u32[]{:S(2)}) async-start(bf16[32,32,128]{2,1,0:T(8,128)(2,1)} %bitcast.7), calls=%async_computation | async-start | bytes 524288 | tf_op jit(solution)/shard_map/all_to_all | solution.py:306
  9.9 73.1 %collective-permute-start = (bf16[3072,384]{1,0:T(8,128)(2,1)}, bf16[3072,384]{1,0:T(8,128)(2,1)}, u32[]{:S(2)}, u32[]{:S(2)}) collective-permute-start(bf16[3072,384]{1,0:T(8,128)(2,1)} %bitcast.28), channel_id=1, source_target_pairs={{0,8},{8,0},{1,9},{9,1},{2,10},{10,2},{3,11},{11,3},{4,12},{12,4},... | collective-permute-start | bytes 7077896 | tf_op jit(solution)/shard_map/ppermute | solution.py:289
  10.1 72.8 %collective-permute-start.1 = (bf16[3072,384]{1,0:T(8,128)(2,1)}, bf16[3072,384]{1,0:T(8,128)(2,1)}, u32[]{:S(2)}, u32[]{:S(2)}) collective-permute-start(bf16[3072,384]{1,0:T(8,128)(2,1)} %bitcast.30), channel_id=1, source_target_pairs={{0,8},{8,0},{1,9},{9,1},{2,10},{10,2},{3,11},{11,3},{4,12},{12,4},... | collective-permute-start | bytes 7077896 | tf_op jit(solution)/shard_map/ppermute | solution.py:289
  10.5 72.5 %collective-permute-start.2 = (bf16[384,3072]{1,0:T(8,128)(2,1)}, bf16[384,3072]{1,0:T(8,128)(2,1)}, u32[]{:S(2)}, u32[]{:S(2)}) collective-permute-start(bf16[384,3072]{1,0:T(8,128)(2,1)} %bitcast.32), channel_id=1, source_target_pairs={{0,8},{8,0},{1,9},{9,1},{2,10},{10,2},{3,11},{11,3},{4,12},{12,4},... | collective-permute-start | bytes 7077896 | tf_op jit(solution)/shard_map/ppermute | solution.py:289
  19.8 11.7 %all-to-all-start.1 = ((bf16[32,16,128]{2,1,0:T(8,128)(2,1)}), bf16[32,16,128]{2,1,0:T(8,128)(2,1)S(1)}, u32[]{:S(2)}, u32[]{:S(2)}) async-start(bf16[32,16,128]{2,1,0:T(8,128)(2,1)} %get-tuple-element.51), calls=%async_computation.1 | async-start | bytes 262144 | tf_op jit(solution)/shard_map/all_to_all | solution.py:317
  35.1 31.9 %all-to-all-start.2 = ((bf16[8,128,384]{2,1,0:T(8,128)(2,1)}), bf16[8,128,384]{2,1,0:T(8,128)(2,1)S(1)}, u32[]{:S(2)}, u32[]{:S(2)}) async-start(bf16[8,128,384]{2,1,0:T(8,128)(2,1)} %copy-done), calls=%async_computation.2 | async-start | bytes 1572864 | tf_op jit(solution)/shard_map/all_to_all | solution.py:331
  83.0 11.5 %collective-permute-start.3 = (bf16[256,384]{1,0:T(8,128)(2,1)S(1)}, bf16[256,384]{1,0:T(8,128)(2,1)S(1)}, u32[]{:S(2)}, u32[]{:S(2)}) collective-permute-start(bf16[256,384]{1,0:T(8,128)(2,1)S(1)} %bitcast.25), channel_id=1, source_target_pairs={{0,1},{1,2},{2,3},{3,4},{4,5},{5,6},{6,7},{7,0},{8,9},{9,10},{10,1... | collective-permute-start | bytes 589832 | tf_op jit(solution)/shard_map/ppermute | solution.py:357
  83.1 11.4 %collective-permute-start.4 = (bf16[256,384]{1,0:T(8,128)(2,1)S(1)}, bf16[256,384]{1,0:T(8,128)(2,1)S(1)}, u32[]{:S(2)}, u32[]{:S(2)}) collective-permute-start(bf16[256,384]{1,0:T(8,128)(2,1)S(1)} %bitcast.22), channel_id=1, source_target_pairs={{0,1},{1,2},{2,3},{3,4},{4,5},{5,6},{6,7},{7,0},{8,9},{9,10},{10,1... | collective-permute-start | bytes 589832 | tf_op jit(solution)/shard_map/ppermute | solution.py:357
  83.2 11.2 %collective-permute-start.5 = (bf16[256,384]{1,0:T(8,128)(2,1)S(1)}, bf16[256,384]{1,0:T(8,128)(2,1)S(1)}, u32[]{:S(2)}, u32[]{:S(2)}) collective-permute-start(bf16[256,384]{1,0:T(8,128)(2,1)S(1)} %bitcast.26), channel_id=1, source_target_pairs={{0,7},{1,0},{2,1},{3,2},{4,3},{5,4},{6,5},{7,6},{8,15},{9,8},{10,9... | collective-permute-start | bytes 589832 | tf_op jit(solution)/shard_map/ppermute | solution.py:357
  94.5 8.9 %collective-permute-start.9 = (bf16[256,384]{1,0:T(8,128)(2,1)S(1)}, bf16[256,384]{1,0:T(8,128)(2,1)S(1)}, u32[]{:S(2)}, u32[]{:S(2)}) collective-permute-start(bf16[256,384]{1,0:T(8,128)(2,1)S(1)} %collective-permute-done.3.refs_4_), channel_id=1, source_target_pairs={{0,1},{1,2},{2,3},{3,4},{4,5},{5,6},{6,7},{7,0},{8,9},{9,10},{10,1... | collective-permute-start | bytes 589832 | tf_op jit(solution)/shard_map/ppermute | solution.py:357
  94.6 8.7 %collective-permute-start.8 = (bf16[256,384]{1,0:T(8,128)(2,1)S(1)}, bf16[256,384]{1,0:T(8,128)(2,1)S(1)}, u32[]{:S(2)}, u32[]{:S(2)}) collective-permute-start(bf16[256,384]{1,0:T(8,128)(2,1)S(1)} %collective-permute-done.6.refs_3_), channel_id=1, source_target_pairs={{0,7},{1,0},{2,1},{3,2},{4,3},{5,4},{6,5},{7,6},{8,15},{9,8},{10,9... | collective-permute-start | bytes 589832 | tf_op jit(solution)/shard_map/ppermute | solution.py:357
  97.8 8.8 %collective-permute-start.7 = (bf16[256,384]{1,0:T(8,128)(2,1)S(1)}, bf16[256,384]{1,0:T(8,128)(2,1)S(1)}, u32[]{:S(2)}, u32[]{:S(2)}) collective-permute-start(bf16[256,384]{1,0:T(8,128)(2,1)S(1)} %collective-permute-done.5.refs_2_), channel_id=1, source_target_pairs={{0,7},{1,0},{2,1},{3,2},{4,3},{5,4},{6,5},{7,6},{8,15},{9,8},{10,9... | collective-permute-start | bytes 589832 | tf_op jit(solution)/shard_map/ppermute | solution.py:357
  99.1 10.9 %collective-permute-start.10 = (bf16[256,384]{1,0:T(8,128)(2,1)S(1)}, bf16[256,384]{1,0:T(8,128)(2,1)S(1)}, u32[]{:S(2)}, u32[]{:S(2)}) collective-permute-start(bf16[256,384]{1,0:T(8,128)(2,1)S(1)} %collective-permute-done.4.refs_5_), channel_id=1, source_target_pairs={{0,1},{1,2},{2,3},{3,4},{4,5},{5,6},{6,7},{7,0},{8,9},{9,10},{10,1... | collective-permute-start | bytes 589832 | tf_op jit(solution)/shard_map/ppermute | solution.py:357
  103.4 9.1 %collective-permute-start.13 = (bf16[256,384]{1,0:T(8,128)(2,1)S(1)}, bf16[256,384]{1,0:T(8,128)(2,1)S(1)}, u32[]{:S(2)}, u32[]{:S(2)}) collective-permute-start(bf16[256,384]{1,0:T(8,128)(2,1)S(1)} %collective-permute-done.9.refs_8_), channel_id=1, source_target_pairs={{0,1},{1,2},{2,3},{3,4},{4,5},{5,6},{6,7},{7,0},{8,9},{9,10},{10,1... | collective-permute-start | bytes 589832 | tf_op jit(solution)/shard_map/ppermute | solution.py:357
  103.4 9.1 %collective-permute-start.12 = (bf16[256,384]{1,0:T(8,128)(2,1)S(1)}, bf16[256,384]{1,0:T(8,128)(2,1)S(1)}, u32[]{:S(2)}, u32[]{:S(2)}) collective-permute-start(bf16[256,384]{1,0:T(8,128)(2,1)S(1)} %collective-permute-done.8.refs_7_), channel_id=1, source_target_pairs={{0,7},{1,0},{2,1},{3,2},{4,3},{5,4},{6,5},{7,6},{8,15},{9,8},{10,9... | collective-permute-start | bytes 589832 | tf_op jit(solution)/shard_map/ppermute | solution.py:357
  106.6 9.0 %collective-permute-start.11 = (bf16[256,384]{1,0:T(8,128)(2,1)S(1)}, bf16[256,384]{1,0:T(8,128)(2,1)S(1)}, u32[]{:S(2)}, u32[]{:S(2)}) collective-permute-start(bf16[256,384]{1,0:T(8,128)(2,1)S(1)} %collective-permute-done.7.refs_6_), channel_id=1, source_target_pairs={{0,7},{1,0},{2,1},{3,2},{4,3},{5,4},{6,5},{7,6},{8,15},{9,8},{10,9... | collective-permute-start | bytes 589832 | tf_op jit(solution)/shard_map/ppermute | solution.py:357
  109.9 11.1 %collective-permute-start.14 = (bf16[256,384]{1,0:T(8,128)(2,1)S(1)}, bf16[256,384]{1,0:T(8,128)(2,1)S(1)}, u32[]{:S(2)}, u32[]{:S(2)}) collective-permute-start(bf16[256,384]{1,0:T(8,128)(2,1)S(1)} %collective-permute-done.10.refs_9_), channel_id=1, source_target_pairs={{0,1},{1,2},{2,3},{3,4},{4,5},{5,6},{6,7},{7,0},{8,9},{9,10},{10,1... | collective-permute-start | bytes 589832 | tf_op jit(solution)/shard_map/ppermute | solution.py:357
  128.8 9.1 %collective-permute-start.24 = (bf16[256,384]{1,0:T(8,128)(2,1)S(1)}, bf16[256,384]{1,0:T(8,128)(2,1)S(1)}, u32[]{:S(2)}, u32[]{:S(2)}) collective-permute-start(bf16[256,384]{1,0:T(8,128)(2,1)S(1)} %get-tuple-element.83), channel_id=1, source_target_pairs={{0,1},{1,2},{2,3},{3,4},{4,5},{5,6},{6,7},{7,0},{8,9},{9,10},{10,1... | collective-permute-start | bytes 589832 | tf_op jit(solution)/shard_map/ppermute | solution.py:357
  128.8 9.2 %collective-permute-start.27 = (bf16[256,384]{1,0:T(8,128)(2,1)S(1)}, bf16[256,384]{1,0:T(8,128)(2,1)S(1)}, u32[]{:S(2)}, u32[]{:S(2)}) collective-permute-start(bf16[256,384]{1,0:T(8,128)(2,1)S(1)} %get-tuple-element.86), channel_id=1, source_target_pairs={{0,7},{1,0},{2,1},{3,2},{4,3},{5,4},{6,5},{7,6},{8,15},{9,8},{10,9... | collective-permute-start | bytes 589832 | tf_op jit(solution)/shard_map/ppermute | solution.py:357
  137.9 9.1 %collective-permute-start.25 = (bf16[256,384]{1,0:T(8,128)(2,1)S(1)}, bf16[256,384]{1,0:T(8,128)(2,1)S(1)}, u32[]{:S(2)}, u32[]{:S(2)}) collective-permute-start(bf16[256,384]{1,0:T(8,128)(2,1)S(1)} %add_convert_fusion.5), channel_id=1, source_target_pairs={{0,1},{1,2},{2,3},{3,4},{4,5},{5,6},{6,7},{7,0},{8,9},{9,10},{10,1... | collective-permute-start | bytes 589832 | tf_op jit(solution)/shard_map/ppermute | solution.py:357
  138.1 9.1 %collective-permute-start.28 = (bf16[256,384]{1,0:T(8,128)(2,1)S(1)}, bf16[256,384]{1,0:T(8,128)(2,1)S(1)}, u32[]{:S(2)}, u32[]{:S(2)}) collective-permute-start(bf16[256,384]{1,0:T(8,128)(2,1)S(1)} %add_convert_fusion.3), channel_id=1, source_target_pairs={{0,7},{1,0},{2,1},{3,2},{4,3},{5,4},{6,5},{7,6},{8,15},{9,8},{10,9... | collective-permute-start | bytes 589832 | tf_op jit(solution)/shard_map/ppermute | solution.py:357
  142.3 9.1 %collective-permute-start.19 = (bf16[256,384]{1,0:T(8,128)(2,1)S(1)}, bf16[256,384]{1,0:T(8,128)(2,1)S(1)}, u32[]{:S(2)}, u32[]{:S(2)}) collective-permute-start(bf16[256,384]{1,0:T(8,128)(2,1)S(1)} %add_convert_fusion.10), channel_id=1, source_target_pairs={{0,1},{1,2},{2,3},{3,4},{4,5},{5,6},{6,7},{7,0},{8,9},{9,10},{10,1... | collective-permute-start | bytes 589832 | tf_op jit(solution)/shard_map/ppermute | solution.py:357
  142.5 16.3 %collective-permute-start.23 = (bf16[256,384]{1,0:T(8,128)(2,1)S(1)}, bf16[256,384]{1,0:T(8,128)(2,1)S(1)}, u32[]{:S(2)}, u32[]{:S(2)}) collective-permute-start(bf16[256,384]{1,0:T(8,128)(2,1)S(1)} %add_convert_fusion.7), channel_id=1, source_target_pairs={{0,7},{1,0},{2,1},{3,2},{4,3},{5,4},{6,5},{7,6},{8,15},{9,8},{10,9... | collective-permute-start | bytes 589832 | tf_op jit(solution)/shard_map/ppermute | solution.py:357
  147.1 11.8 %collective-permute-start.26 = (bf16[256,384]{1,0:T(8,128)(2,1)S(1)}, bf16[256,384]{1,0:T(8,128)(2,1)S(1)}, u32[]{:S(2)}, u32[]{:S(2)}) collective-permute-start(bf16[256,384]{1,0:T(8,128)(2,1)S(1)} %add_convert_fusion.4), channel_id=1, source_target_pairs={{0,1},{1,2},{2,3},{3,4},{4,5},{5,6},{6,7},{7,0},{8,9},{9,10},{10,1... | collective-permute-start | bytes 589832 | tf_op jit(solution)/shard_map/ppermute | solution.py:357
  (14 other events, 83.9 us)
